TPU v7x, 256 devices: a whole 4x4x8 slice. The times are simulated.
256 devices in a mesh: grp: 8 (over z), dom: 32 (over x, y, core).
Axes of the slice: x: 4, y: 4, z: 8, core: 2. Of those that a mesh axis runs over, the one named last changes fastest.
Arguments:
- features: bfloat16 [262144, 512], P(('grp', 'dom')), parts along dimension 0, may hold values from -6 to 6
- send_rows: int32 [512, 128], P(('grp', 'dom')), parts along dimension 0, may hold values from 0 to 1023, as said below
- neighbors: int32 [262144, 4], P(('grp', 'dom')), parts along dimension 0, may hold values from 0 to 1279, as said below
- membership: int32 [262144], P(('grp', 'dom')), parts along dimension 0, may hold values from 0 to 2047, as said below
- coarse_links: int32 [16384, 8], P(('grp', 'dom')), parts along dimension 0, may hold values from 0 to 2047, as said below
- edge_first: bfloat16 [1024, 512], replicated, may hold values from -0.1875 to 0.1875
- edge_second: bfloat16 [512, 512], replicated, may hold values from -0.25 to 0.25
- node_first: bfloat16 [1024, 512], replicated, may hold values from -0.1875 to 0.1875
- node_second: bfloat16 [512, 512], replicated, may hold values from -0.25 to 0.25
- coarse_edge_first: bfloat16 [1024, 512], replicated, may hold values from -0.1875 to 0.1875
- coarse_edge_second: bfloat16 [512, 512], replicated, may hold values from -0.25 to 0.25
- coarse_node_first: bfloat16 [1024, 512], replicated, may hold values from -0.1875 to 0.1875
- coarse_node_second: bfloat16 [512, 512], replicated, may hold values from -0.25 to 0.25
Outputs:
- output_cells: bfloat16 [262144, 512], P(('grp', 'dom')), parts along dimension 0
There are 8 independent parts, one for each index of `grp`. A program takes and returns all parts, laid end to end along the dimension named above; an argument that names none is the same for every part. Nothing has to cross between parts.
Inputs may be any that keep to these rules, and one draw needn't show every extreme that they name: `send_rows`: each row holds 128 distinct local row numbers; row 2d lists what block d sends to block d+1, row 2d+1 what it sends to block d-1. `neighbors`: values below 1024 name a row of the cell's own block; 1024 + j names slot j of the rows from the block below, 1152 + j slot j of the rows from the block above; the first and last blocks never name the missing side. `membership`: cluster c is owned by block c // 64, which lies at most 2 blocks from the cell's block; every cluster has at least one member. `coarse_links`: every source cluster is owned by a block at most 2 blocks from the owner of the target cluster.
All inputs are finite; a program needn't handle non-finite values.
Results may differ from a plain program's by a relative error of at most 0.011.
Values may be sent and summed in bfloat16 or wider, within the bound.
No kernel may reach another device: no remote copies, remote signals or barrier semaphores. Data moves between devices by JAX's collectives and lax.ppermute only.
A program may use at most 128 MiB of HBM per device.

v0:
```python
import jax
import jax.numpy as jnp
from jax import lax
from jax.sharding import PartitionSpec as P

REACH = 2


def shifted(value, axis, steps):
    count = lax.axis_size(axis)
    leading, last = (max(0, -steps), min(count, count - steps))
    return lax.ppermute(value, axis, [(source, source + steps) for source in range(leading, last)])


def shortened(x):
    return jax.tree.map(lambda a: a.astype(jnp.bfloat16) if a.dtype == jnp.float32 else a, x)


def layer_norm(values):
    average = jnp.mean(values, axis=-1, keepdims=True)
    centred = values - average
    variance = jnp.mean(centred * centred, axis=-1, keepdims=True)
    return centred * lax.rsqrt(variance + 1e-05)


def message_pass(node_rows, other_part, edge_first, edge_second, node_first, node_second):
    channels = node_rows.shape[1]
    self_part = jnp.dot(node_rows, edge_first[:channels], preferred_element_type=jnp.float32)
    preact = self_part[:, None, :] + other_part
    hidden = jax.nn.silu(preact).astype(jnp.bfloat16)
    messages = jnp.dot(
        hidden.reshape(-1, channels), edge_second, preferred_element_type=jnp.float32
    )
    aggregate = jnp.sum(messages.reshape(other_part.shape), axis=1).astype(jnp.bfloat16)
    node_pre = jnp.dot(node_rows, node_first[:channels], preferred_element_type=jnp.float32)
    node_pre = node_pre + jnp.dot(
        aggregate, node_first[channels:], preferred_element_type=jnp.float32
    )
    node_hidden = jax.nn.silu(node_pre).astype(jnp.bfloat16)
    update = jnp.dot(node_hidden, node_second, preferred_element_type=jnp.float32)
    return (node_rows.astype(jnp.float32) + layer_norm(update)).astype(jnp.bfloat16)


def shards(
    features,
    send_rows,
    neighbors,
    membership,
    coarse_links,
    edge_first,
    edge_second,
    node_first,
    node_second,
    coarse_edge_first,
    coarse_edge_second,
    coarse_node_first,
    coarse_node_second,
):
    channels = features.shape[1]
    clusters_dev = coarse_links.shape[0]
    device = lax.axis_index("dom")
    first_id = (device - REACH) * clusters_dev
    received = []
    for offset, column in ((1, 0), (-1, 1)):
        received.append(shifted(features[send_rows[column]], "dom", offset))
    extended = jnp.concatenate([features] + received, axis=0)
    projected = jnp.dot(extended, edge_first[channels:], preferred_element_type=jnp.float32)
    updated = message_pass(
        features, projected[neighbors], edge_first, edge_second, node_first, node_second
    )
    span = (2 * REACH + 1) * clusters_dev
    targets = first_id + jnp.arange(span, dtype=jnp.int32)
    onehot = (membership[None, :] == targets[:, None]).astype(jnp.bfloat16)
    partial_sums = jnp.dot(onehot, updated, preferred_element_type=jnp.float32)
    partial_counts = jnp.sum(onehot, axis=1, dtype=jnp.float32)

    def block_of(offset):
        start = (offset + REACH) * clusters_dev
        return (
            partial_sums[start : start + clusters_dev],
            partial_counts[start : start + clusters_dev],
        )

    totals, counts = block_of(0)
    for offset in range(-REACH, REACH + 1):
        if offset != 0:
            moved_sums, moved_counts = shifted(shortened(block_of(offset)), "dom", offset)
            totals = totals + moved_sums
            counts = counts + moved_counts
    coarse = (totals / counts[:, None]).astype(jnp.bfloat16)
    positions = (coarse_links - first_id).reshape(-1)
    pieces = []
    for offset in range(-REACH, REACH + 1):
        if offset == 0:
            pieces.append(coarse)
        else:
            pieces.append(shifted(coarse, "dom", -offset))
    lookup = jnp.concatenate(pieces, axis=0)
    other_part = jnp.dot(
        lookup[positions], coarse_edge_first[channels:], preferred_element_type=jnp.float32
    )
    other_part = other_part.reshape(clusters_dev, coarse_links.shape[1], channels)
    coarse_new = message_pass(
        coarse,
        other_part,
        coarse_edge_first,
        coarse_edge_second,
        coarse_node_first,
        coarse_node_second,
    )
    pieces = []
    for offset in range(-REACH, REACH + 1):
        if offset == 0:
            pieces.append(coarse_new)
        else:
            pieces.append(shifted(coarse_new, "dom", -offset))
    unpooled = jnp.concatenate(pieces, axis=0)
    member_pos = membership - first_id
    result = updated.astype(jnp.float32) + unpooled[member_pos].astype(jnp.float32)
    return result.astype(jnp.bfloat16)


def solution(mesh):
    placed = (
        P(("grp", "dom"), None),
        P(("grp", "dom"), None),
        P(("grp", "dom"), None),
        P(("grp", "dom")),
        P(("grp", "dom"), None),
        P(),
        P(),
        P(),
        P(),
        P(),
        P(),
        P(),
        P(),
    )
    return jax.shard_map(
        shards, mesh=mesh, in_specs=placed, out_specs=P(("grp", "dom"), None), check_vma=False
    )
```

profile of v0, /device:TPU:56, one launch (start us, length us, event | category | flops | bytes accessed | tf_op | source)
XLA Modules:
  0.0 140.4 jit_solution(2984275162645214089)
XLA Ops:
  0.0 1.1 convert_reduce_fusion
  1.2 2.6 %collective-permute-start.6 = (bf16[64]{0:T(256)(128)(2,1)S(1)}, bf16[64]{0:T(256)(128)(2,1)S(1)}, u32[]{:S(2)}, u32[]{:S(2)}) collective-permute-start(bf16[64]{0:T(256)(128)(2,1)S(1)} %get-tuple-element.9), channel_id=1, source_target_pairs={{2,0},{3,1},{4,2},{5,3},{6,4},{7,5},{8,6},{9,7},{10,8},{11,9},{12,... | collective-permute-start | bytes 392 | tf_op jit(solution)/shard_map/ppermute | solution.py:12
  3.9 1.9 %collective-permute-start.7 = (bf16[64]{0:T(256)(128)(2,1)S(1)}, bf16[64]{0:T(256)(128)(2,1)S(1)}, u32[]{:S(2)}, u32[]{:S(2)}) collective-permute-start(bf16[64]{0:T(256)(128)(2,1)S(1)} %get-tuple-element.12), channel_id=1, source_target_pairs={{1,0},{2,1},{3,2},{4,3},{5,4},{6,5},{7,6},{8,7},{9,8},{10,9},{11,1... | collective-permute-start | bytes 392 | tf_op jit(solution)/shard_map/ppermute | solution.py:12
  5.8 2.4 %collective-permute-start.8 = (bf16[64]{0:T(256)(128)(2,1)S(1)}, bf16[64]{0:T(256)(128)(2,1)S(1)}, u32[]{:S(2)}, u32[]{:S(2)}) collective-permute-start(bf16[64]{0:T(256)(128)(2,1)S(1)} %get-tuple-element.11), channel_id=1, source_target_pairs={{0,1},{1,2},{2,3},{3,4},{4,5},{5,6},{6,7},{7,8},{8,9},{9,10},{10,1... | collective-permute-start | bytes 392 | tf_op jit(solution)/shard_map/ppermute | solution.py:12
  8.2 0.8 fusion.48
  9.0 2.2 %gather_fusion = bf16[128,512]{1,0:T(8,128)(2,1)S(1)} fusion(bf16[1024,512]{1,0:T(8,128)(2,1)} %param.13, s32[1024]{0:T(1024)S(1)} %pad_clamp_fusion.2), kind=kCustom, calls=%fused_computation | custom fusion | bytes 262656 | tf_op jit(solution)/shard_map/gather | solution.py:65
  11.3 4.9 %collective-permute-start = (bf16[128,512]{1,0:T(8,128)(2,1)S(1)}, bf16[128,512]{1,0:T(8,128)(2,1)}, u32[]{:S(2)}, u32[]{:S(2)}) collective-permute-start(bf16[128,512]{1,0:T(8,128)(2,1)S(1)} %gather_fusion), channel_id=1, source_target_pairs={{0,1},{1,2},{2,3},{3,4},{4,5},{5,6},{6,7},{7,8},{8,9},{9,10},{10,1... | collective-permute-start | bytes 393224 | tf_op jit(solution)/shard_map/ppermute | solution.py:12
  16.2 2.2 %gather_fusion.1 = bf16[128,512]{1,0:T(8,128)(2,1)S(1)} fusion(bf16[1024,512]{1,0:T(8,128)(2,1)} %param.13, s32[1024]{0:T(1024)S(1)} %pad_clamp_fusion.1), kind=kCustom, calls=%fused_computation.1 | custom fusion | bytes 262656 | tf_op jit(solution)/shard_map/gather | solution.py:65
  18.4 1.9 %collective-permute-start.1 = (bf16[128,512]{1,0:T(8,128)(2,1)S(1)}, bf16[128,512]{1,0:T(8,128)(2,1)}, u32[]{:S(2)}, u32[]{:S(2)}) collective-permute-start(bf16[128,512]{1,0:T(8,128)(2,1)S(1)} %gather_fusion.1), channel_id=1, source_target_pairs={{1,0},{2,1},{3,2},{4,3},{5,4},{6,5},{7,6},{8,7},{9,8},{10,9},{11,1... | collective-permute-start | bytes 393224 | tf_op jit(solution)/shard_map/ppermute | solution.py:12
  20.4 0.2 copy.23
  20.6 0.3 reshape.148
  20.9 2.0 %fusion.31 = f32[1024,512]{1,0:T(8,128)} fusion(bf16[1024,512]{1,0:T(8,128)(2,1)S(1)} %copy-done.1, bf16[1024,512]{1,0:T(8,128)(2,1)S(1)} %copy-done.5), kind=kOutput, calls=%fused_computation.45 | convolution fusion | flops 536870912 | bytes 3670016 | tf_op jit(solution)/shard_map/dot_general | solution.py:28
  23.0 2.0 %fusion.33 = f32[1024,512]{1,0:T(8,128)} fusion(bf16[1024,512]{1,0:T(8,128)(2,1)S(1)} %copy-done.1, bf16[1024,512]{1,0:T(8,128)(2,1)S(1)} %copy-done.6), kind=kOutput, calls=%fused_computation.47 | convolution fusion | flops 536870912 | bytes 3670016 | tf_op jit(solution)/shard_map/dot_general | solution.py:35
  25.2 1.3 copy.22
  26.5 6.1 %collective-permute-start.9 = (bf16[64]{0:T(256)(128)(2,1)S(1)}, bf16[64]{0:T(256)(128)(2,1)S(1)}, u32[]{:S(2)}, u32[]{:S(2)}) collective-permute-start(bf16[64]{0:T(256)(128)(2,1)S(1)} %get-tuple-element.10), channel_id=1, source_target_pairs={{0,2},{1,3},{2,4},{3,5},{4,6},{5,7},{6,8},{7,9},{8,10},{9,11},{10,... | collective-permute-start | bytes 392 | tf_op jit(solution)/shard_map/ppermute | solution.py:12
  32.7 2.3 %fusion.5 = f32[1280,512]{1,0:T(8,128)S(1)} fusion(bf16[128,512]{1,0:T(8,128)(2,1)} %collective-permute-done.1, bf16[128,512]{1,0:T(8,128)(2,1)} %collective-permute-done, bf16[1024,512]{1,0:T(8,128)(2,1)} %param.13, bf16[1024,512]{1,0:T(8,128)(2,1)} %param.18), kind=kOutput, calls=%fused_computation.18 | convolution fusion | flops 675020800 | bytes 4456448 | tf_op jit(solution)/shard_map/dot_general | solution.py:67
  35.0 16.8 %gather_fusion.2 = f32[4096,512]{1,0:T(8,128)} fusion(f32[1280,512]{1,0:T(8,128)S(1)} %fusion.5, s32[4096]{0:T(1024)S(1)} %broadcast_clamp_fusion), kind=kCustom, calls=%fused_computation.2 | custom fusion | bytes 16793600 | tf_op jit(solution)/shard_map/gather | solution.py:69
  51.9 10.0 %reshape.147 = f32[1024,4,512]{2,1,0:T(4,128)} reshape(f32[4096,512]{1,0:T(8,128)} %gather_fusion.2) | data formatting | bytes 16777216 | tf_op jit(solution)/shard_map/gather | solution.py:69
  61.9 8.3 %fusion.1 = bf16[1024,512]{1,0:T(8,128)(2,1)} fusion(f32[1024,4,512]{2,1,0:T(4,128)} %reshape.147, f32[1024,512]{1,0:T(8,128)S(1)} %copy-done.4, bf16[512,512]{1,0:T(8,128)(2,1)S(1)} %copy-done.12), kind=kOutput, calls=%fused_computation.8 | convolution fusion | flops 2161639424 | bytes 12058624 | tf_op jit(solution)/shard_map/dot_general | solution.py:31
  70.1 3.6 %fusion.57 = (f32[1024]{0:T(1024)S(1)}, f32[1024,512]{0,1:T(8,128)S(1)}) fusion(bf16[512,512]{1,0:T(8,128)(2,1)S(1)} %copy-done, f32[1024,512]{1,0:T(8,128)} %fusion.33, bf16[1024,512]{1,0:T(8,128)(2,1)} %fusion.1, bf16[1024,512]{1,0:T(8,128)(2,1)} %param.20), kind=kOutput, calls=%fused_computation.97 | convolution fusion | flops 1077410816 | bytes 6295552 | tf_op jit(solution)/shard_map/dot_general | solution.py:40
  73.7 0.3 multiply_reduce_fusion
  74.0 0.9 copy-done.3
  75.0 0.4 add_convert_fusion.1
  75.4 0.3 copy-done.10
  75.6 0.5 fusion.60
  76.2 2.1 %collective-permute-start.2 = (bf16[64,512]{1,0:T(8,128)(2,1)S(1)}, bf16[64,512]{1,0:T(8,128)(2,1)S(1)}, u32[]{:S(2)}, u32[]{:S(2)}) collective-permute-start(bf16[64,512]{1,0:T(8,128)(2,1)S(1)} %get-tuple-element.5), channel_id=1, source_target_pairs={{2,0},{3,1},{4,2},{5,3},{6,4},{7,5},{8,6},{9,7},{10,8},{11,9},{12,... | collective-permute-start | bytes 196616 | tf_op jit(solution)/shard_map/ppermute | solution.py:12
  78.3 1.9 %collective-permute-start.3 = (bf16[64,512]{1,0:T(8,128)(2,1)S(1)}, bf16[64,512]{1,0:T(8,128)(2,1)S(1)}, u32[]{:S(2)}, u32[]{:S(2)}) collective-permute-start(bf16[64,512]{1,0:T(8,128)(2,1)S(1)} %get-tuple-element.8), channel_id=1, source_target_pairs={{1,0},{2,1},{3,2},{4,3},{5,4},{6,5},{7,6},{8,7},{9,8},{10,9},{11,1... | collective-permute-start | bytes 196616 | tf_op jit(solution)/shard_map/ppermute | solution.py:12
  80.2 2.4 %collective-permute-start.4 = (bf16[64,512]{1,0:T(8,128)(2,1)S(1)}, bf16[64,512]{1,0:T(8,128)(2,1)S(1)}, u32[]{:S(2)}, u32[]{:S(2)}) collective-permute-start(bf16[64,512]{1,0:T(8,128)(2,1)S(1)} %get-tuple-element.7), channel_id=1, source_target_pairs={{0,1},{1,2},{2,3},{3,4},{4,5},{5,6},{6,7},{7,8},{8,9},{9,10},{10,1... | collective-permute-start | bytes 196616 | tf_op jit(solution)/shard_map/ppermute | solution.py:12
  82.7 6.0 %collective-permute-start.5 = (bf16[64,512]{1,0:T(8,128)(2,1)S(1)}, bf16[64,512]{1,0:T(8,128)(2,1)S(1)}, u32[]{:S(2)}, u32[]{:S(2)}) collective-permute-start(bf16[64,512]{1,0:T(8,128)(2,1)S(1)} %get-tuple-element.6), channel_id=1, source_target_pairs={{0,2},{1,3},{2,4},{3,5},{4,6},{5,7},{6,8},{7,9},{8,10},{9,11},{10,... | collective-permute-start | bytes 196616 | tf_op jit(solution)/shard_map/ppermute | solution.py:12
  88.8 1.8 %collective-permute-done.5 = bf16[64,512]{1,0:T(8,128)(2,1)S(1)} collective-permute-done((bf16[64,512]{1,0:T(8,128)(2,1)S(1)}, bf16[64,512]{1,0:T(8,128)(2,1)S(1)}, u32[]{:S(2)}, u32[]{:S(2)}) %collective-permute-start.5) | collective-permute-done | bytes 65568 | tf_op jit(solution)/shard_map/ppermute | solution.py:12
  90.7 6.4 %collective-permute-start.10 = (bf16[64,512]{1,0:T(8,128)(2,1)S(1)}, bf16[64,512]{1,0:T(8,128)(2,1)S(1)}, u32[]{:S(2)}, u32[]{:S(2)}) collective-permute-start(bf16[64,512]{1,0:T(8,128)(2,1)S(1)} %fusion.44), channel_id=1, source_target_pairs={{0,2},{1,3},{2,4},{3,5},{4,6},{5,7},{6,8},{7,9},{8,10},{9,11},{10,... | collective-permute-start | bytes 196616 | tf_op jit(solution)/shard_map/ppermute | solution.py:12
  97.1 1.9 %collective-permute-start.11 = (bf16[64,512]{1,0:T(8,128)(2,1)S(1)}, bf16[64,512]{1,0:T(8,128)(2,1)S(1)}, u32[]{:S(2)}, u32[]{:S(2)}) collective-permute-start(bf16[64,512]{1,0:T(8,128)(2,1)S(1)} %fusion.44), channel_id=1, source_target_pairs={{0,1},{1,2},{2,3},{3,4},{4,5},{5,6},{6,7},{7,8},{8,9},{9,10},{10,1... | collective-permute-start | bytes 196616 | tf_op jit(solution)/shard_map/ppermute | solution.py:12
  99.0 3.6 %collective-permute-start.12 = (bf16[64,512]{1,0:T(8,128)(2,1)S(1)}, bf16[64,512]{1,0:T(8,128)(2,1)S(1)}, u32[]{:S(2)}, u32[]{:S(2)}) collective-permute-start(bf16[64,512]{1,0:T(8,128)(2,1)S(1)} %fusion.44), channel_id=1, source_target_pairs={{1,0},{2,1},{3,2},{4,3},{5,4},{6,5},{7,6},{8,7},{9,8},{10,9},{11,1... | collective-permute-start | bytes 196616 | tf_op jit(solution)/shard_map/ppermute | solution.py:12
  102.6 2.1 %collective-permute-start.13 = (bf16[64,512]{1,0:T(8,128)(2,1)S(1)}, bf16[64,512]{1,0:T(8,128)(2,1)S(1)}, u32[]{:S(2)}, u32[]{:S(2)}) collective-permute-start(bf16[64,512]{1,0:T(8,128)(2,1)S(1)} %fusion.44), channel_id=1, source_target_pairs={{2,0},{3,1},{4,2},{5,3},{6,4},{7,5},{8,6},{9,7},{10,8},{11,9},{12,... | collective-permute-start | bytes 196616 | tf_op jit(solution)/shard_map/ppermute | solution.py:12
  104.8 0.9 fusion.25
  105.7 5.2 %collective-permute-done.13 = bf16[64,512]{1,0:T(8,128)(2,1)S(1)} collective-permute-done((bf16[64,512]{1,0:T(8,128)(2,1)S(1)}, bf16[64,512]{1,0:T(8,128)(2,1)S(1)}, u32[]{:S(2)}, u32[]{:S(2)}) %collective-permute-start.13) | collective-permute-done | bytes 65568 | tf_op jit(solution)/shard_map/ppermute | solution.py:12
  110.9 2.0 %gather_fusion.3 = bf16[512,512]{1,0:T(8,128)(2,1)S(1)} fusion(bf16[320,512]{1,0:T(8,128)(2,1)S(1)} %constant_dynamic-update-slice_fusion, s32[1024]{0:T(1024)S(1)} %pad_clamp_fusion), kind=kCustom, calls=%fused_computation.3 | custom fusion | bytes 1050624 | tf_op jit(solution)/shard_map/gather | solution.py:100
  112.9 2.1 %convolution_reduce_fusion = bf16[64,512]{1,0:T(8,128)(2,1)S(1)} fusion(bf16[512,512]{1,0:T(8,128)(2,1)S(1)} %gather_fusion.3, bf16[512,512]{1,0:T(8,128)(2,1)} %param.23, bf16[1024,512]{1,0:T(8,128)(2,1)S(1)} %copy-done.7, f32[64,512]{1,0:T(8,128)} %fusion.25), kind=kOutput, calls=%fused_computation.25 | convolution fusion | flops 538673152 | bytes 1769472 | tf_op jit(solution)/shard_map/dot_general | solution.py:31
  115.2 1.5 %fusion.61 = (f32[64]{0:T(128)S(1)}, f32[64,512]{1,0:T(8,128)S(1)}) fusion(bf16[512,512]{1,0:T(8,128)(2,1)} %param.25, f32[64,512]{1,0:T(8,128)S(1)} %fusion.19, bf16[64,512]{1,0:T(8,128)(2,1)S(1)} %fusion.44, bf16[1024,512]{1,0:T(8,128)(2,1)S(1)} %copy-done.8), kind=kOutput, calls=%fused_computation.99 | convolution fusion | flops 67338176 | bytes 1376512 | tf_op jit(solution)/shard_map/dot_general | solution.py:40
  117.1 1.9 %collective-permute-start.14 = (bf16[64,512]{1,0:T(8,128)(2,1)S(1)}, bf16[64,512]{1,0:T(8,128)(2,1)S(1)}, u32[]{:S(2)}, u32[]{:S(2)}) collective-permute-start(bf16[64,512]{1,0:T(8,128)(2,1)S(1)} %add_convert_fusion.2), channel_id=1, source_target_pairs={{0,2},{1,3},{2,4},{3,5},{4,6},{5,7},{6,8},{7,9},{8,10},{9,11},{10,... | collective-permute-start | bytes 196616 | tf_op jit(solution)/shard_map/ppermute | solution.py:12
  119.1 1.9 %collective-permute-start.15 = (bf16[64,512]{1,0:T(8,128)(2,1)S(1)}, bf16[64,512]{1,0:T(8,128)(2,1)S(1)}, u32[]{:S(2)}, u32[]{:S(2)}) collective-permute-start(bf16[64,512]{1,0:T(8,128)(2,1)S(1)} %add_convert_fusion.2), channel_id=1, source_target_pairs={{0,1},{1,2},{2,3},{3,4},{4,5},{5,6},{6,7},{7,8},{8,9},{9,10},{10,1... | collective-permute-start | bytes 196616 | tf_op jit(solution)/shard_map/ppermute | solution.py:12
  121.0 3.6 %collective-permute-start.16 = (bf16[64,512]{1,0:T(8,128)(2,1)S(1)}, bf16[64,512]{1,0:T(8,128)(2,1)S(1)}, u32[]{:S(2)}, u32[]{:S(2)}) collective-permute-start(bf16[64,512]{1,0:T(8,128)(2,1)S(1)} %add_convert_fusion.2), channel_id=1, source_target_pairs={{1,0},{2,1},{3,2},{4,3},{5,4},{6,5},{7,6},{8,7},{9,8},{10,9},{11,1... | collective-permute-start | bytes 196616 | tf_op jit(solution)/shard_map/ppermute | solution.py:12
  124.6 3.9 %collective-permute-start.17 = (bf16[64,512]{1,0:T(8,128)(2,1)S(1)}, bf16[64,512]{1,0:T(8,128)(2,1)S(1)}, u32[]{:S(2)}, u32[]{:S(2)}) collective-permute-start(bf16[64,512]{1,0:T(8,128)(2,1)S(1)} %add_convert_fusion.2), channel_id=1, source_target_pairs={{2,0},{3,1},{4,2},{5,3},{6,4},{7,5},{8,6},{9,7},{10,8},{11,9},{12,... | collective-permute-start | bytes 196616 | tf_op jit(solution)/shard_map/ppermute | solution.py:12
  128.7 4.2 %collective-permute-done.17 = bf16[64,512]{1,0:T(8,128)(2,1)S(1)} collective-permute-done((bf16[64,512]{1,0:T(8,128)(2,1)S(1)}, bf16[64,512]{1,0:T(8,128)(2,1)S(1)}, u32[]{:S(2)}, u32[]{:S(2)}) %collective-permute-start.17) | collective-permute-done | bytes 65568 | tf_op jit(solution)/shard_map/ppermute | solution.py:12
  132.9 4.0 %gather_fusion.4 = bf16[1024,512]{1,0:T(8,128)(2,1)S(1)} fusion(bf16[320,512]{1,0:T(8,128)(2,1)S(1)} %constant_dynamic-update-slice_fusion.5, s32[1024]{0:T(1024)S(1)} %fusion.47), kind=kCustom, calls=%fused_computation.4 | custom fusion | bytes 2101248 | tf_op jit(solution)/shard_map/gather | solution.py:119
  136.9 0.5 copy.26
  137.4 1.6 %add_convert_fusion = bf16[1024,512]{0,1:T(8,128)(2,1)S(1)} fusion(bf16[1024,512]{0,1:T(8,128)(2,1)S(1)} %copy.26, bf16[1024,512]{0,1:T(8,128)(2,1)} %copy-done.2), kind=kLoop, calls=%fused_computation.9 | loop fusion | flops 2097152 | bytes 3145728 | tf_op jit(solution)/shard_map/convert_element_type | solution.py:120
  139.0 1.3 copy.27
  (72 shorter events, 1.1 us)
Async XLA Ops:
  0.0 70.1 %copy-start = (bf16[512,512]{1,0:T(8,128)(2,1)S(1)}, bf16[512,512]{1,0:T(8,128)(2,1)}, u32[]{:S(2)}) copy-start(bf16[512,512]{1,0:T(8,128)(2,1)} %param.21) | copy-start | bytes 1572868
  0.0 20.9 %copy-start.1 = (bf16[1024,512]{1,0:T(8,128)(2,1)S(1)}, bf16[1024,512]{1,0:T(8,128)(2,1)}, u32[]{:S(2)}) copy-start(bf16[1024,512]{1,0:T(8,128)(2,1)} %param.13) | copy-start | bytes 3145732
  0.0 20.4 %copy-start.9 = (s32[1024,4]{0,1:T(4,128)S(1)}, s32[1024,4]{0,1:T(4,128)}, u32[]{:S(2)}) copy-start(s32[1024,4]{0,1:T(4,128)} %param.15) | copy-start | bytes 49156
  0.0 20.9 %copy-start.5 = (bf16[1024,512]{1,0:T(8,128)(2,1)S(1)}, bf16[1024,512]{1,0:T(8,128)(2,1)}, u32[]{:S(2)}) copy-start(bf16[1024,512]{1,0:T(8,128)(2,1)} %param.18) | copy-start | bytes 3145732
  1.2 77.0 %collective-permute-start.6 = (bf16[64]{0:T(256)(128)(2,1)S(1)}, bf16[64]{0:T(256)(128)(2,1)S(1)}, u32[]{:S(2)}, u32[]{:S(2)}) collective-permute-start(bf16[64]{0:T(256)(128)(2,1)S(1)} %get-tuple-element.9), channel_id=1, source_target_pairs={{2,0},{3,1},{4,2},{5,3},{6,4},{7,5},{8,6},{9,7},{10,8},{11,9},{12,... | collective-permute-start | bytes 392 | tf_op jit(solution)/shard_map/ppermute | solution.py:12
  3.9 76.3 %collective-permute-start.7 = (bf16[64]{0:T(256)(128)(2,1)S(1)}, bf16[64]{0:T(256)(128)(2,1)S(1)}, u32[]{:S(2)}, u32[]{:S(2)}) collective-permute-start(bf16[64]{0:T(256)(128)(2,1)S(1)} %get-tuple-element.12), channel_id=1, source_target_pairs={{1,0},{2,1},{3,2},{4,3},{5,4},{6,5},{7,6},{8,7},{9,8},{10,9},{11,1... | collective-permute-start | bytes 392 | tf_op jit(solution)/shard_map/ppermute | solution.py:12
  5.8 76.8 %collective-permute-start.8 = (bf16[64]{0:T(256)(128)(2,1)S(1)}, bf16[64]{0:T(256)(128)(2,1)S(1)}, u32[]{:S(2)}, u32[]{:S(2)}) collective-permute-start(bf16[64]{0:T(256)(128)(2,1)S(1)} %get-tuple-element.11), channel_id=1, source_target_pairs={{0,1},{1,2},{2,3},{3,4},{4,5},{5,6},{6,7},{7,8},{8,9},{9,10},{10,1... | collective-permute-start | bytes 392 | tf_op jit(solution)/shard_map/ppermute | solution.py:12
  11.3 15.3 %collective-permute-start = (bf16[128,512]{1,0:T(8,128)(2,1)S(1)}, bf16[128,512]{1,0:T(8,128)(2,1)}, u32[]{:S(2)}, u32[]{:S(2)}) collective-permute-start(bf16[128,512]{1,0:T(8,128)(2,1)S(1)} %gather_fusion), channel_id=1, source_target_pairs={{0,1},{1,2},{2,3},{3,4},{4,5},{5,6},{6,7},{7,8},{8,9},{9,10},{10,1... | collective-permute-start | bytes 393224 | tf_op jit(solution)/shard_map/ppermute | solution.py:12
  18.4 14.2 %collective-permute-start.1 = (bf16[128,512]{1,0:T(8,128)(2,1)S(1)}, bf16[128,512]{1,0:T(8,128)(2,1)}, u32[]{:S(2)}, u32[]{:S(2)}) collective-permute-start(bf16[128,512]{1,0:T(8,128)(2,1)S(1)} %gather_fusion.1), channel_id=1, source_target_pairs={{1,0},{2,1},{3,2},{4,3},{5,4},{6,5},{7,6},{8,7},{9,8},{10,9},{11,1... | collective-permute-start | bytes 393224 | tf_op jit(solution)/shard_map/ppermute | solution.py:12
  20.9 2.1 %copy-start.6 = (bf16[1024,512]{1,0:T(8,128)(2,1)S(1)}, bf16[1024,512]{1,0:T(8,128)(2,1)}, u32[]{:S(2)}) copy-start(bf16[1024,512]{1,0:T(8,128)(2,1)} %param.20) | copy-start | bytes 3145732
  23.0 2.0 %copy-start.11 = (s32[64,8]{0,1:T(8,128)S(1)}, s32[64,8]{0,1:T(8,128)}, u32[]{:S(2)}) copy-start(s32[64,8]{0,1:T(8,128)} %param.17) | copy-start | bytes 6148
  26.5 62.2 %collective-permute-start.9 = (bf16[64]{0:T(256)(128)(2,1)S(1)}, bf16[64]{0:T(256)(128)(2,1)S(1)}, u32[]{:S(2)}, u32[]{:S(2)}) collective-permute-start(bf16[64]{0:T(256)(128)(2,1)S(1)} %get-tuple-element.10), channel_id=1, source_target_pairs={{0,2},{1,3},{2,4},{3,5},{4,6},{5,7},{6,8},{7,9},{8,10},{9,11},{10,... | collective-permute-start | bytes 392 | tf_op jit(solution)/shard_map/ppermute | solution.py:12
  51.9 10.0 %copy-start.4 = (f32[1024,512]{1,0:T(8,128)S(1)}, f32[1024,512]{1,0:T(8,128)}, u32[]{:S(2)}) copy-start(f32[1024,512]{1,0:T(8,128)} %fusion.31) | copy-start | bytes 6291460
  51.9 10.0 %copy-start.12 = (bf16[512,512]{1,0:T(8,128)(2,1)S(1)}, bf16[512,512]{1,0:T(8,128)(2,1)}, u32[]{:S(2)}) copy-start(bf16[512,512]{1,0:T(8,128)(2,1)} %param.19) | copy-start | bytes 1572868
  73.7 1.2 copy-start.3
  74.9 0.7 copy-start.10
  75.6 30.1 %copy-start.2 = (bf16[1024,512]{0,1:T(8,128)(2,1)}, bf16[1024,512]{0,1:T(8,128)(2,1)S(1)}, u32[]{:S(2)}) copy-start(bf16[1024,512]{0,1:T(8,128)(2,1)S(1)} %add_convert_fusion.1) | copy-start | bytes 3145732
  75.6 29.1 %copy-start.7 = (bf16[1024,512]{1,0:T(8,128)(2,1)S(1)}, bf16[1024,512]{1,0:T(8,128)(2,1)}, u32[]{:S(2)}) copy-start(bf16[1024,512]{1,0:T(8,128)(2,1)} %param.22) | copy-start | bytes 3145732
  76.2 12.5 %collective-permute-start.2 = (bf16[64,512]{1,0:T(8,128)(2,1)S(1)}, bf16[64,512]{1,0:T(8,128)(2,1)S(1)}, u32[]{:S(2)}, u32[]{:S(2)}) collective-permute-start(bf16[64,512]{1,0:T(8,128)(2,1)S(1)} %get-tuple-element.5), channel_id=1, source_target_pairs={{2,0},{3,1},{4,2},{5,3},{6,4},{7,5},{8,6},{9,7},{10,8},{11,9},{12,... | collective-permute-start | bytes 196616 | tf_op jit(solution)/shard_map/ppermute | solution.py:12
  78.3 10.4 %collective-permute-start.3 = (bf16[64,512]{1,0:T(8,128)(2,1)S(1)}, bf16[64,512]{1,0:T(8,128)(2,1)S(1)}, u32[]{:S(2)}, u32[]{:S(2)}) collective-permute-start(bf16[64,512]{1,0:T(8,128)(2,1)S(1)} %get-tuple-element.8), channel_id=1, source_target_pairs={{1,0},{2,1},{3,2},{4,3},{5,4},{6,5},{7,6},{8,7},{9,8},{10,9},{11,1... | collective-permute-start | bytes 196616 | tf_op jit(solution)/shard_map/ppermute | solution.py:12
  80.2 8.5 %collective-permute-start.4 = (bf16[64,512]{1,0:T(8,128)(2,1)S(1)}, bf16[64,512]{1,0:T(8,128)(2,1)S(1)}, u32[]{:S(2)}, u32[]{:S(2)}) collective-permute-start(bf16[64,512]{1,0:T(8,128)(2,1)S(1)} %get-tuple-element.7), channel_id=1, source_target_pairs={{0,1},{1,2},{2,3},{3,4},{4,5},{5,6},{6,7},{7,8},{8,9},{9,10},{10,1... | collective-permute-start | bytes 196616 | tf_op jit(solution)/shard_map/ppermute | solution.py:12
  82.7 7.9 %collective-permute-start.5 = (bf16[64,512]{1,0:T(8,128)(2,1)S(1)}, bf16[64,512]{1,0:T(8,128)(2,1)S(1)}, u32[]{:S(2)}, u32[]{:S(2)}) collective-permute-start(bf16[64,512]{1,0:T(8,128)(2,1)S(1)} %get-tuple-element.6), channel_id=1, source_target_pairs={{0,2},{1,3},{2,4},{3,5},{4,6},{5,7},{6,8},{7,9},{8,10},{9,11},{10,... | collective-permute-start | bytes 196616 | tf_op jit(solution)/shard_map/ppermute | solution.py:12
  90.7 15.0 %collective-permute-start.10 = (bf16[64,512]{1,0:T(8,128)(2,1)S(1)}, bf16[64,512]{1,0:T(8,128)(2,1)S(1)}, u32[]{:S(2)}, u32[]{:S(2)}) collective-permute-start(bf16[64,512]{1,0:T(8,128)(2,1)S(1)} %fusion.44), channel_id=1, source_target_pairs={{0,2},{1,3},{2,4},{3,5},{4,6},{5,7},{6,8},{7,9},{8,10},{9,11},{10,... | collective-permute-start | bytes 196616 | tf_op jit(solution)/shard_map/ppermute | solution.py:12
  97.1 8.6 %collective-permute-start.11 = (bf16[64,512]{1,0:T(8,128)(2,1)S(1)}, bf16[64,512]{1,0:T(8,128)(2,1)S(1)}, u32[]{:S(2)}, u32[]{:S(2)}) collective-permute-start(bf16[64,512]{1,0:T(8,128)(2,1)S(1)} %fusion.44), channel_id=1, source_target_pairs={{0,1},{1,2},{2,3},{3,4},{4,5},{5,6},{6,7},{7,8},{8,9},{9,10},{10,1... | collective-permute-start | bytes 196616 | tf_op jit(solution)/shard_map/ppermute | solution.py:12
  99.0 6.7 %collective-permute-start.12 = (bf16[64,512]{1,0:T(8,128)(2,1)S(1)}, bf16[64,512]{1,0:T(8,128)(2,1)S(1)}, u32[]{:S(2)}, u32[]{:S(2)}) collective-permute-start(bf16[64,512]{1,0:T(8,128)(2,1)S(1)} %fusion.44), channel_id=1, source_target_pairs={{1,0},{2,1},{3,2},{4,3},{5,4},{6,5},{7,6},{8,7},{9,8},{10,9},{11,1... | collective-permute-start | bytes 196616 | tf_op jit(solution)/shard_map/ppermute | solution.py:12
  102.6 8.3 %collective-permute-start.13 = (bf16[64,512]{1,0:T(8,128)(2,1)S(1)}, bf16[64,512]{1,0:T(8,128)(2,1)S(1)}, u32[]{:S(2)}, u32[]{:S(2)}) collective-permute-start(bf16[64,512]{1,0:T(8,128)(2,1)S(1)} %fusion.44), channel_id=1, source_target_pairs={{2,0},{3,1},{4,2},{5,3},{6,4},{7,5},{8,6},{9,7},{10,8},{11,9},{12,... | collective-permute-start | bytes 196616 | tf_op jit(solution)/shard_map/ppermute | solution.py:12
  112.9 2.1 %copy-start.8 = (bf16[1024,512]{1,0:T(8,128)(2,1)S(1)}, bf16[1024,512]{1,0:T(8,128)(2,1)}, u32[]{:S(2)}) copy-start(bf16[1024,512]{1,0:T(8,128)(2,1)} %param.24) | copy-start | bytes 3145732
  117.1 11.5 %collective-permute-start.14 = (bf16[64,512]{1,0:T(8,128)(2,1)S(1)}, bf16[64,512]{1,0:T(8,128)(2,1)S(1)}, u32[]{:S(2)}, u32[]{:S(2)}) collective-permute-start(bf16[64,512]{1,0:T(8,128)(2,1)S(1)} %add_convert_fusion.2), channel_id=1, source_target_pairs={{0,2},{1,3},{2,4},{3,5},{4,6},{5,7},{6,8},{7,9},{8,10},{9,11},{10,... | collective-permute-start | bytes 196616 | tf_op jit(solution)/shard_map/ppermute | solution.py:12
  119.1 9.5 %collective-permute-start.15 = (bf16[64,512]{1,0:T(8,128)(2,1)S(1)}, bf16[64,512]{1,0:T(8,128)(2,1)S(1)}, u32[]{:S(2)}, u32[]{:S(2)}) collective-permute-start(bf16[64,512]{1,0:T(8,128)(2,1)S(1)} %add_convert_fusion.2), channel_id=1, source_target_pairs={{0,1},{1,2},{2,3},{3,4},{4,5},{5,6},{6,7},{7,8},{8,9},{9,10},{10,1... | collective-permute-start | bytes 196616 | tf_op jit(solution)/shard_map/ppermute | solution.py:12
  121.0 7.6 %collective-permute-start.16 = (bf16[64,512]{1,0:T(8,128)(2,1)S(1)}, bf16[64,512]{1,0:T(8,128)(2,1)S(1)}, u32[]{:S(2)}, u32[]{:S(2)}) collective-permute-start(bf16[64,512]{1,0:T(8,128)(2,1)S(1)} %add_convert_fusion.2), channel_id=1, source_target_pairs={{1,0},{2,1},{3,2},{4,3},{5,4},{6,5},{7,6},{8,7},{9,8},{10,9},{11,1... | collective-permute-start | bytes 196616 | tf_op jit(solution)/shard_map/ppermute | solution.py:12
  124.6 8.3 %collective-permute-start.17 = (bf16[64,512]{1,0:T(8,128)(2,1)S(1)}, bf16[64,512]{1,0:T(8,128)(2,1)S(1)}, u32[]{:S(2)}, u32[]{:S(2)}) collective-permute-start(bf16[64,512]{1,0:T(8,128)(2,1)S(1)} %add_convert_fusion.2), channel_id=1, source_target_pairs={{2,0},{3,1},{4,2},{5,3},{6,4},{7,5},{8,6},{9,7},{10,8},{11,9},{12,... | collective-permute-start | bytes 196616 | tf_op jit(solution)/shard_map/ppermute | solution.py:12
where the time goes:
time: 141 us; the launch traced here: 140 us
  starting transfers between devices  57.8 us (41%)
  local copies, waits for them, and re-layouts  42.4 us (30%)
  matrix products  23.5 us (17%)
  waiting for transfers between devices  11.3 us (8%)
  other arithmetic  4.69 us (3%)
    ppermute x18, starting transfers between devices, shifted(): lax.ppermute(value, axis, [(source, source + steps) for source in range(l...  57.8 us
    gather x2, local copies, waits for them, and re-layouts, shards(): projected[neighbors]  26.8 us
    ppermute x18, waiting for transfers between devices, shifted(): lax.ppermute(value, axis, [(source, source + steps) for source in range(l...  11.3 us
    dot_general x2, matrix products, message_pass(): jnp.dot(hidden.reshape(-1, channels), edge_second, preferred_element_type...  10.4 us
    dot_general x2, matrix products, message_pass(): jnp.dot(node_hidden, node_second, preferred_element_type=jnp.float32)  5.14 us
    gather x2, local copies, waits for them, and re-layouts, shards(): unpooled[member_pos].astype(jnp.float32)  4.49 us
    gather x2, local copies, waits for them, and re-layouts, shards(): received.append(shifted(features[send_rows[column]], 'dom', offset))  4.47 us
    dot_general x2, matrix products, message_pass(): jnp.dot(node_rows, edge_first[:channels], preferred_element_type=jnp.floa...  2.9 us
  transfers between devices with their start and end apart: 18, of which 3 were waited for; matrix products, arithmetic and copies ran while one was open for 39% of the time, Pallas kernels for 0%

commit v1 on v0

v1 whole, which is shorter than its diff:
```python
import jax
import jax.numpy as jnp
from jax import lax
from jax.experimental import pallas as pl
from jax.experimental.pallas import tpu as pltpu
from jax.sharding import PartitionSpec as P

H = 512
ROWS = 1024
HALO = 128
OWNED = 64
CHIP = 128
TILE = 256
WIDE = H + 128
DOM = 32
F32 = jnp.float32
BF16 = jnp.bfloat16

SIBLING = [(i, i ^ 1) for i in range(DOM)]
ACROSS = [(i, (i + 1) % DOM if i % 2 else (i - 1) % DOM) for i in range(DOM)]


def sibling(value):
    return lax.ppermute(value, "dom", SIBLING)


def across(value):
    return lax.ppermute(value, "dom", ACROSS)


def dot(a, b):
    return jnp.dot(a, b, preferred_element_type=F32)


def gated(half):
    return half + half * jnp.tanh(half)


def columns(ids, span):
    spread = jnp.transpose(jnp.broadcast_to(ids, (128, 128)))
    lane = lax.broadcasted_iota(jnp.int32, (128, 128), 1)
    return jnp.concatenate(
        [(spread == lane + 128 * j).astype(F32).astype(BF16) for j in range(span // 128)], axis=1
    )


def layer_norm(values):
    average = jnp.mean(values, axis=-1, keepdims=True)
    centred = values - average
    variance = jnp.mean(centred * centred, axis=-1, keepdims=True)
    return centred * lax.rsqrt(variance + 1e-05)


def node_update(rows, total, edge_second, node_first, node_second):
    aggregate = dot(total.astype(BF16), edge_second).astype(BF16)
    pre = dot(rows, node_first[:H, :]) + dot(aggregate, node_first[H:, :])
    hidden = gated(0.5 * pre).astype(BF16)
    return (rows.astype(F32) + layer_norm(dot(hidden, node_second))).astype(BF16)


def halo_body(features, send_rows, near, far):
    core = lax.rem(lax.axis_index("dom"), 2)
    up, down = send_rows[0:1, :], send_rows[1:2, :]
    to_sibling = jnp.where(core == 0, up, down)
    to_across = jnp.where(core == 0, down, up)
    near[...] = dot(columns(to_sibling, ROWS), features[...]).astype(BF16)
    far[...] = dot(columns(to_across, ROWS), features[...]).astype(BF16)


def fine_body(
    features, near, far, neighbors, membership, edge_first, edge_second, node_first, node_second,
    updated, first, base, own, projected, pooled,
):
    device = lax.axis_index("dom")
    core = lax.rem(device, 2)
    other = edge_first[H:, :]
    projected[0:ROWS, :] = (0.5 * dot(features[...], other)).astype(BF16)
    below = jnp.where(core == 0, far[...], near[...])
    above = jnp.where(core == 0, near[...], far[...])
    halo = jnp.concatenate([below, above], axis=0)
    projected[ROWS:, :] = (0.5 * dot(halo, other)).astype(BF16)

    for tile in range(ROWS // TILE):
        here = slice(tile * TILE, (tile + 1) * TILE)
        rows = features[here, :]
        self_part = 0.5 * dot(rows, edge_first[:H, :])
        total = jnp.zeros((TILE, H), F32)
        for k in range(4):
            chosen = jnp.concatenate(
                [
                    columns(neighbors[k : k + 1, tile * TILE + s : tile * TILE + s + 128], ROWS + 2 * HALO)
                    for s in range(0, TILE, 128)
                ],
                axis=0,
            )
            total = total + gated(self_part + dot(chosen, projected[...]))
        updated[here, :] = node_update(rows, total, edge_second[...], node_first, node_second[...])

    target = (device - 2) * OWNED + lax.broadcasted_iota(jnp.int32, (5 * OWNED, 128), 0)
    belongs = jnp.concatenate(
        [(membership[j : j + 1, :] == target).astype(F32).astype(BF16) for j in range(ROWS // 128)], axis=1
    )
    pooled[:, :H] = dot(belongs, updated[...])
    count = dot(belongs, jnp.ones((ROWS, 128), BF16))
    high = jnp.floor(count * (1.0 / 64.0))
    lane = lax.broadcasted_iota(jnp.int32, (5 * OWNED, 128), 1)
    pooled[:, H:] = jnp.where(lane < 64, high, count - 64.0 * high)
    first[...] = pooled[pl.ds(pl.multiple_of((1 - core) * 256, 64), OWNED), :].astype(BF16)
    base[...] = pooled[pl.ds(pl.multiple_of(core * 192, 64), CHIP), :].astype(BF16)
    own[...] = pooled[pl.ds(pl.multiple_of(128 - 64 * core, 64), CHIP), :].astype(BF16)


def coarse_body(
    coarse, near, far, links, edge_first, edge_second, node_first, node_second, updated, projected
):
    device = lax.axis_index("dom")
    core = lax.rem(device, 2)
    start = (lax.div(device, 2) - 1) * CHIP
    below = jnp.where(core == 0, far[...], near[...])
    above = jnp.where(core == 0, near[...], far[...])
    rows = coarse[...]
    lookup = jnp.concatenate([below, rows, above], axis=0)
    projected[...] = (0.5 * dot(lookup, edge_first[H:, :])).astype(BF16)
    self_part = 0.5 * dot(rows, edge_first[:H, :])
    total = jnp.zeros((CHIP, H), F32)
    for k in range(8):
        chosen = columns(links[k : k + 1, :] - start, 3 * CHIP)
        total = total + gated(self_part + dot(chosen, projected[...]))
    updated[...] = node_update(rows, total, edge_second[...], node_first, node_second[...])


def unpool_body(fine, coarse, near, far, membership, result):
    device = lax.axis_index("dom")
    core = lax.rem(device, 2)
    start = (lax.div(device, 2) - 1) * CHIP
    below = jnp.where(core == 0, far[...], near[...])
    above = jnp.where(core == 0, near[...], far[...])
    lookup = jnp.concatenate([below, coarse[...], above], axis=0)
    for j in range(ROWS // 128):
        here = slice(j * 128, (j + 1) * 128)
        chosen = columns(membership[j : j + 1, :] - start, 3 * CHIP)
        result[here, :] = (fine[here, :].astype(F32) + dot(chosen, lookup)).astype(BF16)


def call(body, outs, scratch, flops, *args):
    return pl.pallas_call(
        body,
        out_shape=[jax.ShapeDtypeStruct(shape, BF16) for shape in outs],
        in_specs=[pl.BlockSpec(memory_space=pltpu.VMEM)] * len(args),
        out_specs=[pl.BlockSpec(memory_space=pltpu.VMEM)] * len(outs),
        scratch_shapes=scratch,
        compiler_params=pltpu.CompilerParams(vmem_limit_bytes=40 * 1024 * 1024),
        cost_estimate=pl.CostEstimate(flops=flops, bytes_accessed=4 * 1024 * 1024, transcendentals=0),
    )(*args)


def shards(
    features,
    send_rows,
    neighbors,
    membership,
    coarse_links,
    edge_first,
    edge_second,
    node_first,
    node_second,
    coarse_edge_first,
    coarse_edge_second,
    coarse_node_first,
    coarse_node_second,
):
    core = lax.rem(lax.axis_index("dom"), 2)
    members = membership.reshape(ROWS // 128, 128)
    near, far = call(halo_body, [(HALO, H)] * 2, [], 300000000, features, send_rows)
    near, far = sibling(near), across(far)
    my_links = coarse_links.T
    their_links = sibling(my_links)
    links = jnp.where(
        core == 0,
        jnp.concatenate([my_links, their_links], axis=1),
        jnp.concatenate([their_links, my_links], axis=1),
    )
    updated, first, base, own = call(
        fine_body,
        [(ROWS, H), (OWNED, WIDE), (CHIP, WIDE), (CHIP, WIDE)],
        [pltpu.VMEM((ROWS + 2 * HALO, H), BF16), pltpu.VMEM((5 * OWNED, WIDE), F32)],
        9000000000,
        features, near, far, neighbors.T, members, edge_first, edge_second, node_first, node_second,
    )
    first = sibling(first).astype(F32)
    nothing = jnp.zeros_like(first)
    extra = jnp.where(
        core == 0, jnp.concatenate([nothing, first], axis=0), jnp.concatenate([first, nothing], axis=0)
    )
    arrived = across((base.astype(F32) + extra).astype(BF16))
    mine = (own.astype(F32) + arrived.astype(F32)).astype(BF16)
    theirs = sibling(mine)
    sums = mine.astype(F32) + theirs.astype(F32)
    counts = 64.0 * sums[:, H : H + 1] + sums[:, H + 64 : H + 65]
    coarse = (sums[:, :H] / counts).astype(BF16)

    far = across(coarse)
    near = sibling(far)
    (coarse_new,) = call(
        coarse_body,
        [(CHIP, H)],
        [pltpu.VMEM((3 * CHIP, H), BF16)],
        1000000000,
        coarse, near, far, links, coarse_edge_first, coarse_edge_second, coarse_node_first, coarse_node_second,
    )
    far = across(coarse_new)
    near = sibling(far)
    (result,) = call(unpool_body, [(ROWS, H)], [], 400000000, updated, coarse_new, near, far, members)
    return result


def solution(mesh):
    placed = (
        P(("grp", "dom"), None),
        P(("grp", "dom"), None),
        P(("grp", "dom"), None),
        P(("grp", "dom")),
        P(("grp", "dom"), None),
        P(),
        P(),
        P(),
        P(),
        P(),
        P(),
        P(),
        P(),
    )
    return jax.shard_map(
        shards, mesh=mesh, in_specs=placed, out_specs=P(("grp", "dom"), None), check_vma=False
    )
```

time: 141 us -> 62.4 us (0.44)
  the two profiles are of different devices: /device:TPU:56 before, /device:TPU:1 now
where the time goes in v1:
time: 62.4 us; the launch traced here: 62.1 us
  waiting for transfers between devices  22 us (35%)
  starting transfers between devices  18.2 us (29%)
  Pallas kernels  16 us (26%)
  local copies, waits for them, and re-layouts  5.24 us (8%)
    ppermute x6, starting transfers between devices, sibling(): return lax.ppermute(value, 'dom', SIBLING)  18 us
    ppermute x4, waiting for transfers between devices, across(): return lax.ppermute(value, 'dom', ACROSS)  16.9 us
    pallas_call x4, Pallas kernels, call(): pl.pallas_call(body, out_shape=[jax.ShapeDtypeStruct(shape, BF16) for sha...  16 us
    unnamed x26, local copies, waits for them, and re-layouts  5.24 us
    ppermute x6, waiting for transfers between devices, sibling(): return lax.ppermute(value, 'dom', SIBLING)  5.09 us
  transfers between devices with their start and end apart: 10, of which 9 were waited for; matrix products, arithmetic and copies ran while one was open for 0% of the time, Pallas kernels for 0%

profile of v1, /device:TPU:1, one launch (start us, length us, event | category | flops | bytes accessed | tf_op | source)
XLA Modules:
  0.0 62.1 jit_solution(13716238731701276768)
XLA Ops:
  0.0 0.0 copy-start.1
  0.0 1.2 %copy-done.1 = bf16[1024,512]{1,0:T(8,128)(2,1)S(1)} copy-done((bf16[1024,512]{1,0:T(8,128)(2,1)S(1)}, bf16[1024,512]{1,0:T(8,128)(2,1)}, u32[]{:S(2)}) %copy-start.1) | copy-done | bytes 1048600
  1.2 0.0 copy-start.11
  1.2 0.7 %copy-done.11 = s32[2,128]{1,0:T(2,128)S(1)} copy-done((s32[2,128]{1,0:T(2,128)S(1)}, s32[2,128]{1,0:T(2,128)}, u32[]{:S(2)}) %copy-start.11) | copy-done | bytes 1048
  1.9 0.0 copy-start.2
  1.9 0.5 shard_map.127
  2.4 0.0 copy-start
  2.4 3.3 %collective-permute-start = (bf16[128,512]{1,0:T(8,128)(2,1)S(1)}, bf16[128,512]{1,0:T(8,128)(2,1)S(1)}, u32[]{:S(2)}, u32[]{:S(2)}) collective-permute-start(bf16[128,512]{1,0:T(8,128)(2,1)S(1)} %get-tuple-element.11), channel_id=1, source_target_pairs={{0,1},{1,0},{2,3},{3,2},{4,5},{5,4},{6,7},{7,6},{8,9},{9,8},{10,11... | collective-permute-start | bytes 393224 | tf_op jit(solution)/shard_map/ppermute | solution.py:24
  5.8 0.0 collective-permute-start.1
  5.8 1.0 %collective-permute-done.near = bf16[128,512]{1,0:T(8,128)(2,1)S(1)} collective-permute-done((bf16[128,512]{1,0:T(8,128)(2,1)S(1)}, bf16[128,512]{1,0:T(8,128)(2,1)S(1)}, u32[]{:S(2)}, u32[]{:S(2)}) %collective-permute-start) | collective-permute-done | bytes 131104 | tf_op jit(solution)/shard_map/ppermute | solution.py:24
  6.8 3.4 %collective-permute-done.1.far = bf16[128,512]{1,0:T(8,128)(2,1)S(1)} collective-permute-done((bf16[128,512]{1,0:T(8,128)(2,1)S(1)}, bf16[128,512]{1,0:T(8,128)(2,1)S(1)}, u32[]{:S(2)}, u32[]{:S(2)}) %collective-permute-start.1) | collective-permute-done | bytes 131104 | tf_op jit(solution)/shard_map/ppermute | solution.py:28
  10.2 0.0 copy-done.2
  10.2 0.0 copy-done.10
  10.2 0.0 copy-done
  10.2 0.0 copy-start.3
  10.2 1.2 %copy-done.3 = bf16[1024,512]{1,0:T(8,128)(2,1)S(1)} copy-done((bf16[1024,512]{1,0:T(8,128)(2,1)S(1)}, bf16[1024,512]{1,0:T(8,128)(2,1)}, u32[]{:S(2)}) %copy-start.3) | copy-done | bytes 1048600
  11.4 1.0 %copy-done.6 = bf16[512,512]{1,0:T(8,128)(2,1)S(1)} copy-done((bf16[512,512]{1,0:T(8,128)(2,1)S(1)}, bf16[512,512]{1,0:T(8,128)(2,1)}, u32[]{:S(2)}) %copy-start.6) | copy-done | bytes 524312
  12.4 1.0 %copy-done.7 = bf16[512,512]{1,0:T(8,128)(2,1)S(1)} copy-done((bf16[512,512]{1,0:T(8,128)(2,1)S(1)}, bf16[512,512]{1,0:T(8,128)(2,1)}, u32[]{:S(2)}) %copy-start.7) | copy-done | bytes 524312
  13.5 11.8 %shard_map.128 = (bf16[1024,512]{1,0:T(8,128)(2,1)S(1)}, bf16[64,640]{1,0:T(8,128)(2,1)S(1)}, bf16[128,640]{1,0:T(8,128)(2,1)S(1)}, bf16[128,640]{1,0:T(8,128)(2,1)S(1)}) custom-call(bf16[1024,512]{1,0:T(8,128)(2,1)S(1)} %copy-done.1, bf16[128,512]{1,0:T(8,128)(2,1)S(1)} %collective-permute-done.near, bf16[128,512]{1,0:T(8,128)(2,1)S(1)} %collective-permute-done.1.far, ...), custom_call_target="tpu_custom_call" | custom-call | flops 8999999488 | bytes 4194304 | tf_op jit(solution)/shard_map/pallas_call | solution.py:146
  25.3 3.7 %collective-permute-start.2 = (bf16[64,640]{1,0:T(8,128)(2,1)S(1)}, bf16[64,640]{1,0:T(8,128)(2,1)S(1)}, u32[]{:S(2)}, u32[]{:S(2)}) collective-permute-start(bf16[64,640]{1,0:T(8,128)(2,1)S(1)} %get-tuple-element.16), channel_id=1, source_target_pairs={{0,1},{1,0},{2,3},{3,2},{4,5},{5,4},{6,7},{7,6},{8,9},{9,8},{10,11... | collective-permute-start | bytes 245768 | tf_op jit(solution)/shard_map/ppermute | solution.py:24
  29.0 0.9 %collective-permute-done.2 = bf16[64,640]{1,0:T(8,128)(2,1)S(1)} collective-permute-done((bf16[64,640]{1,0:T(8,128)(2,1)S(1)}, bf16[64,640]{1,0:T(8,128)(2,1)S(1)}, u32[]{:S(2)}, u32[]{:S(2)}) %collective-permute-start.2) | collective-permute-done | bytes 81952 | tf_op jit(solution)/shard_map/ppermute | solution.py:24
  29.9 0.0 copy-start.4
  29.9 0.0 copy-start.5
  30.0 0.1 collective-permute-start.3
  30.1 4.7 %collective-permute-done.3 = bf16[128,640]{1,0:T(8,128)(2,1)S(1)} collective-permute-done((bf16[128,640]{1,0:T(8,128)(2,1)S(1)}, bf16[128,640]{1,0:T(8,128)(2,1)S(1)}, u32[]{:S(2)}, u32[]{:S(2)}) %collective-permute-start.3) | collective-permute-done | bytes 163872 | tf_op jit(solution)/shard_map/ppermute | solution.py:28
  34.8 3.8 %collective-permute-start.4 = (bf16[128,640]{1,0:T(8,128)(2,1)S(1)}, bf16[128,640]{1,0:T(8,128)(2,1)S(1)}, u32[]{:S(2)}, u32[]{:S(2)}) collective-permute-start(bf16[128,640]{1,0:T(8,128)(2,1)S(1)} %add_convert_fusion), channel_id=1, source_target_pairs={{0,1},{1,0},{2,3},{3,2},{4,5},{5,4},{6,7},{7,6},{8,9},{9,8},{10,11... | collective-permute-start | bytes 491528 | tf_op jit(solution)/shard_map/ppermute | solution.py:24
  38.6 1.0 %collective-permute-done.4 = bf16[128,640]{1,0:T(8,128)(2,1)S(1)} collective-permute-done((bf16[128,640]{1,0:T(8,128)(2,1)S(1)}, bf16[128,640]{1,0:T(8,128)(2,1)S(1)}, u32[]{:S(2)}, u32[]{:S(2)}) %collective-permute-start.4) | collective-permute-done | bytes 163872 | tf_op jit(solution)/shard_map/ppermute | solution.py:24
  39.7 0.2 fusion.1
  39.9 0.0 copy-start.12
  39.9 0.1 fusion.coarse
  40.0 0.1 collective-permute-start.5
  40.1 4.4 %collective-permute-done.5.far = bf16[128,512]{1,0:T(8,128)(2,1)S(1)} collective-permute-done((bf16[128,512]{1,0:T(8,128)(2,1)S(1)}, bf16[128,512]{1,0:T(8,128)(2,1)S(1)}, u32[]{:S(2)}, u32[]{:S(2)}) %collective-permute-start.5) | collective-permute-done | bytes 131104 | tf_op jit(solution)/shard_map/ppermute | solution.py:28
  44.4 3.7 %collective-permute-start.6 = (bf16[128,512]{1,0:T(8,128)(2,1)S(1)}, bf16[128,512]{1,0:T(8,128)(2,1)S(1)}, u32[]{:S(2)}, u32[]{:S(2)}) collective-permute-start(bf16[128,512]{1,0:T(8,128)(2,1)S(1)} %collective-permute-done.5.far), channel_id=1, source_target_pairs={{0,1},{1,0},{2,3},{3,2},{4,5},{5,4},{6,7},{7,6},{8,9},{9,8},{10,11... | collective-permute-start | bytes 393224 | tf_op jit(solution)/shard_map/ppermute | solution.py:24
  48.1 0.0 copy-done.12
  48.1 0.0 collective-permute-start.7
  48.1 1.2 %collective-permute-done.7 = s32[8,64]{1,0:T(8,128)S(1)} collective-permute-done((s32[8,64]{1,0:T(8,128)S(1)}, s32[8,64]{1,0:T(8,128)S(1)}, u32[]{:S(2)}, u32[]{:S(2)}) %collective-permute-start.7) | collective-permute-done | bytes 2080 | tf_op jit(solution)/shard_map/ppermute | solution.py:24
  49.3 0.1 add_select_fusion.links
  49.4 0.0 collective-permute-done.6.near
  49.4 0.0 copy-done.8
  49.4 0.0 copy-done.9
  49.4 0.0 copy-done.4
  49.4 0.0 copy-done.5
  49.4 2.0 %shard_map.129.coarse = bf16[128,512]{1,0:T(8,128)(2,1)S(1)} custom-call(bf16[128,512]{1,0:T(8,128)(2,1)S(1)} %fusion.coarse, bf16[128,512]{1,0:T(8,128)(2,1)S(1)} %collective-permute-done.6.near, bf16[128,512]{1,0:T(8,128)(2,1)S(1)} %collective-permute-done.5.far, s32[8,128]{1,0:T(8,128)S(1)} %add_select_fusion.links, bf16[1024,512]{1,0:T(8,128)(2,1)S(1)} %copy-done.4, ...), custom_call_target="tpu_custom_call" | custom-call | flops 1000000000 | bytes 4194304 | tf_op jit(solution)/shard_map/pallas_call | solution.py:146
  51.4 0.1 collective-permute-start.8
  51.5 4.4 %collective-permute-done.8.far = bf16[128,512]{1,0:T(8,128)(2,1)S(1)} collective-permute-done((bf16[128,512]{1,0:T(8,128)(2,1)S(1)}, bf16[128,512]{1,0:T(8,128)(2,1)S(1)}, u32[]{:S(2)}, u32[]{:S(2)}) %collective-permute-start.8) | collective-permute-done | bytes 131104 | tf_op jit(solution)/shard_map/ppermute | solution.py:28
  55.9 3.5 %collective-permute-start.9 = (bf16[128,512]{1,0:T(8,128)(2,1)S(1)}, bf16[128,512]{1,0:T(8,128)(2,1)S(1)}, u32[]{:S(2)}, u32[]{:S(2)}) collective-permute-start(bf16[128,512]{1,0:T(8,128)(2,1)S(1)} %collective-permute-done.8.far), channel_id=1, source_target_pairs={{0,1},{1,0},{2,3},{3,2},{4,5},{5,4},{6,7},{7,6},{8,9},{9,8},{10,11... | collective-permute-start | bytes 393224 | tf_op jit(solution)/shard_map/ppermute | solution.py:24
  59.4 1.0 %collective-permute-done.9.near = bf16[128,512]{1,0:T(8,128)(2,1)S(1)} collective-permute-done((bf16[128,512]{1,0:T(8,128)(2,1)S(1)}, bf16[128,512]{1,0:T(8,128)(2,1)S(1)}, u32[]{:S(2)}, u32[]{:S(2)}) %collective-permute-start.9) | collective-permute-done | bytes 131104 | tf_op jit(solution)/shard_map/ppermute | solution.py:24
  60.3 1.8 %shard_map.130 = bf16[1024,512]{1,0:T(8,128)(2,1)} custom-call(bf16[1024,512]{1,0:T(8,128)(2,1)S(1)} %get-tuple-element.13.fine, bf16[128,512]{1,0:T(8,128)(2,1)S(1)} %shard_map.129.coarse, bf16[128,512]{1,0:T(8,128)(2,1)S(1)} %collective-permute-done.9.near, bf16[128,512]{1,0:T(8,128)(2,1)S(1)} %collective-permute-done.8.far, s32[8,128]{1,0:T(8,128)S(1)} %bitcast.4), custom_call_target="tpu_custom_call" | custom-call | flops 400000000 | bytes 4194304 | tf_op jit(solution)/shard_map/pallas_call | solution.py:146
  (9 shorter events, 0.1 us)
Async XLA Ops:
  0.0 1.2 %copy-start.1 = (bf16[1024,512]{1,0:T(8,128)(2,1)S(1)}, bf16[1024,512]{1,0:T(8,128)(2,1)}, u32[]{:S(2)}) copy-start(bf16[1024,512]{1,0:T(8,128)(2,1)} %features.3) | copy-start | bytes 3145732
  1.2 0.7 %copy-start.11 = (s32[2,128]{1,0:T(2,128)S(1)}, s32[2,128]{1,0:T(2,128)}, u32[]{:S(2)}) copy-start(s32[2,128]{1,0:T(2,128)} %send_rows.1) | copy-start | bytes 3076
  1.9 8.3 %copy-start.2 = (bf16[1024,512]{1,0:T(8,128)(2,1)S(1)}, bf16[1024,512]{1,0:T(8,128)(2,1)}, u32[]{:S(2)}) copy-start(bf16[1024,512]{1,0:T(8,128)(2,1)} %edge_first.2) | copy-start | bytes 3145732
  1.9 8.3 %copy-start.10 = (s32[1024,4]{0,1:T(4,128)S(1)}, s32[1024,4]{0,1:T(4,128)}, u32[]{:S(2)}) copy-start(s32[1024,4]{0,1:T(4,128)} %param.15) | copy-start | bytes 49156
  2.4 7.7 %copy-start = (s32[1024]{0:T(1024)S(1)}, s32[1024]{0:T(1024)}, u32[]{:S(2)}) copy-start(s32[1024]{0:T(1024)} %param.16) | copy-start | bytes 12292
  2.4 4.3 %collective-permute-start = (bf16[128,512]{1,0:T(8,128)(2,1)S(1)}, bf16[128,512]{1,0:T(8,128)(2,1)S(1)}, u32[]{:S(2)}, u32[]{:S(2)}) collective-permute-start(bf16[128,512]{1,0:T(8,128)(2,1)S(1)} %get-tuple-element.11), channel_id=1, source_target_pairs={{0,1},{1,0},{2,3},{3,2},{4,5},{5,4},{6,7},{7,6},{8,9},{9,8},{10,11... | collective-permute-start | bytes 393224 | tf_op jit(solution)/shard_map/ppermute | solution.py:24
  5.8 4.4 %collective-permute-start.1 = (bf16[128,512]{1,0:T(8,128)(2,1)S(1)}, bf16[128,512]{1,0:T(8,128)(2,1)S(1)}, u32[]{:S(2)}, u32[]{:S(2)}) collective-permute-start(bf16[128,512]{1,0:T(8,128)(2,1)S(1)} %get-tuple-element.12), channel_id=1, source_target_pairs={{0,31},{1,2},{2,1},{3,4},{4,3},{5,6},{6,5},{7,8},{8,7},{9,10},{10,... | collective-permute-start | bytes 393224 | tf_op jit(solution)/shard_map/ppermute | solution.py:28
  10.2 1.2 %copy-start.3 = (bf16[1024,512]{1,0:T(8,128)(2,1)S(1)}, bf16[1024,512]{1,0:T(8,128)(2,1)}, u32[]{:S(2)}) copy-start(bf16[1024,512]{1,0:T(8,128)(2,1)} %node_first.2) | copy-start | bytes 3145732
  11.4 1.0 %copy-start.6 = (bf16[512,512]{1,0:T(8,128)(2,1)S(1)}, bf16[512,512]{1,0:T(8,128)(2,1)}, u32[]{:S(2)}) copy-start(bf16[512,512]{1,0:T(8,128)(2,1)} %edge_second.2) | copy-start | bytes 1572868
  12.4 1.0 %copy-start.7 = (bf16[512,512]{1,0:T(8,128)(2,1)S(1)}, bf16[512,512]{1,0:T(8,128)(2,1)}, u32[]{:S(2)}) copy-start(bf16[512,512]{1,0:T(8,128)(2,1)} %node_second.2) | copy-start | bytes 1572868
  13.5 35.9 %copy-start.8 = (bf16[512,512]{1,0:T(8,128)(2,1)S(1)}, bf16[512,512]{1,0:T(8,128)(2,1)}, u32[]{:S(2)}) copy-start(bf16[512,512]{1,0:T(8,128)(2,1)} %edge_second.3) | copy-start | bytes 1572868
  13.5 35.9 %copy-start.9 = (bf16[512,512]{1,0:T(8,128)(2,1)S(1)}, bf16[512,512]{1,0:T(8,128)(2,1)}, u32[]{:S(2)}) copy-start(bf16[512,512]{1,0:T(8,128)(2,1)} %node_second.3) | copy-start | bytes 1572868
  25.3 4.6 %collective-permute-start.2 = (bf16[64,640]{1,0:T(8,128)(2,1)S(1)}, bf16[64,640]{1,0:T(8,128)(2,1)S(1)}, u32[]{:S(2)}, u32[]{:S(2)}) collective-permute-start(bf16[64,640]{1,0:T(8,128)(2,1)S(1)} %get-tuple-element.16), channel_id=1, source_target_pairs={{0,1},{1,0},{2,3},{3,2},{4,5},{5,4},{6,7},{7,6},{8,9},{9,8},{10,11... | collective-permute-start | bytes 245768 | tf_op jit(solution)/shard_map/ppermute | solution.py:24
  29.9 19.5 %copy-start.4 = (bf16[1024,512]{1,0:T(8,128)(2,1)S(1)}, bf16[1024,512]{1,0:T(8,128)(2,1)}, u32[]{:S(2)}) copy-start(bf16[1024,512]{1,0:T(8,128)(2,1)} %edge_first.3) | copy-start | bytes 3145732
  29.9 19.5 %copy-start.5 = (bf16[1024,512]{1,0:T(8,128)(2,1)S(1)}, bf16[1024,512]{1,0:T(8,128)(2,1)}, u32[]{:S(2)}) copy-start(bf16[1024,512]{1,0:T(8,128)(2,1)} %node_first.3) | copy-start | bytes 3145732
  30.0 4.8 %collective-permute-start.3 = (bf16[128,640]{1,0:T(8,128)(2,1)S(1)}, bf16[128,640]{1,0:T(8,128)(2,1)S(1)}, u32[]{:S(2)}, u32[]{:S(2)}) collective-permute-start(bf16[128,640]{1,0:T(8,128)(2,1)S(1)} %add_convert_fusion.1), channel_id=1, source_target_pairs={{0,31},{1,2},{2,1},{3,4},{4,3},{5,6},{6,5},{7,8},{8,7},{9,10},{10,... | collective-permute-start | bytes 491528 | tf_op jit(solution)/shard_map/ppermute | solution.py:28
  34.8 4.8 %collective-permute-start.4 = (bf16[128,640]{1,0:T(8,128)(2,1)S(1)}, bf16[128,640]{1,0:T(8,128)(2,1)S(1)}, u32[]{:S(2)}, u32[]{:S(2)}) collective-permute-start(bf16[128,640]{1,0:T(8,128)(2,1)S(1)} %add_convert_fusion), channel_id=1, source_target_pairs={{0,1},{1,0},{2,3},{3,2},{4,5},{5,4},{6,7},{7,6},{8,9},{9,8},{10,11... | collective-permute-start | bytes 491528 | tf_op jit(solution)/shard_map/ppermute | solution.py:24
  39.9 8.3 %copy-start.12 = (s32[64,8]{0,1:T(8,128)S(1)}, s32[64,8]{0,1:T(8,128)}, u32[]{:S(2)}) copy-start(s32[64,8]{0,1:T(8,128)} %param.17) | copy-start | bytes 6148
  40.0 4.5 %collective-permute-start.5 = (bf16[128,512]{1,0:T(8,128)(2,1)S(1)}, bf16[128,512]{1,0:T(8,128)(2,1)S(1)}, u32[]{:S(2)}, u32[]{:S(2)}) collective-permute-start(bf16[128,512]{1,0:T(8,128)(2,1)S(1)} %fusion.coarse), channel_id=1, source_target_pairs={{0,31},{1,2},{2,1},{3,4},{4,3},{5,6},{6,5},{7,8},{8,7},{9,10},{10,... | collective-permute-start | bytes 393224 | tf_op jit(solution)/shard_map/ppermute | solution.py:28
  44.4 4.9 %collective-permute-start.6 = (bf16[128,512]{1,0:T(8,128)(2,1)S(1)}, bf16[128,512]{1,0:T(8,128)(2,1)S(1)}, u32[]{:S(2)}, u32[]{:S(2)}) collective-permute-start(bf16[128,512]{1,0:T(8,128)(2,1)S(1)} %collective-permute-done.5.far), channel_id=1, source_target_pairs={{0,1},{1,0},{2,3},{3,2},{4,5},{5,4},{6,7},{7,6},{8,9},{9,8},{10,11... | collective-permute-start | bytes 393224 | tf_op jit(solution)/shard_map/ppermute | solution.py:24
  48.1 1.2 %collective-permute-start.7 = (s32[8,64]{1,0:T(8,128)S(1)}, s32[8,64]{1,0:T(8,128)S(1)}, u32[]{:S(2)}, u32[]{:S(2)}) collective-permute-start(s32[8,64]{1,0:T(8,128)S(1)} %bitcast.6), channel_id=1, source_target_pairs={{0,1},{1,0},{2,3},{3,2},{4,5},{5,4},{6,7},{7,6},{8,9},{9,8},{10,11... | collective-permute-start | bytes 6152 | tf_op jit(solution)/shard_map/ppermute | solution.py:24
  51.4 4.5 %collective-permute-start.8 = (bf16[128,512]{1,0:T(8,128)(2,1)S(1)}, bf16[128,512]{1,0:T(8,128)(2,1)S(1)}, u32[]{:S(2)}, u32[]{:S(2)}) collective-permute-start(bf16[128,512]{1,0:T(8,128)(2,1)S(1)} %shard_map.129.coarse), channel_id=1, source_target_pairs={{0,31},{1,2},{2,1},{3,4},{4,3},{5,6},{6,5},{7,8},{8,7},{9,10},{10,... | collective-permute-start | bytes 393224 | tf_op jit(solution)/shard_map/ppermute | solution.py:28
  55.9 4.5 %collective-permute-start.9 = (bf16[128,512]{1,0:T(8,128)(2,1)S(1)}, bf16[128,512]{1,0:T(8,128)(2,1)S(1)}, u32[]{:S(2)}, u32[]{:S(2)}) collective-permute-start(bf16[128,512]{1,0:T(8,128)(2,1)S(1)} %collective-permute-done.8.far), channel_id=1, source_target_pairs={{0,1},{1,0},{2,3},{3,2},{4,5},{5,4},{6,7},{7,6},{8,9},{9,8},{10,11... | collective-permute-start | bytes 393224 | tf_op jit(solution)/shard_map/ppermute | solution.py:24

commit v2 on v1

v2 whole, which is shorter than its diff:
```python
import jax
import jax.numpy as jnp
from jax import lax
from jax.experimental import pallas as pl
from jax.experimental.pallas import tpu as pltpu
from jax.sharding import PartitionSpec as P

H = 512
ROWS = 1024
HALO = 128
OWNED = 64
CHIP = 128
TILE = 512
WIDE = H + 128
DOM = 32
F32 = jnp.float32
BF16 = jnp.bfloat16

SIBLING = [(i, i ^ 1) for i in range(DOM)]


def facing(parts):
    pairs = []
    for part in range(parts):
        other = part ^ 1 if (part ^ 1) < parts else part
        for i in range(DOM):
            j = i + 1 if i % 2 else i - 1
            pairs.append((part * DOM + i, part * DOM + j if 0 <= j < DOM else other * DOM + i))
    return pairs


def sibling(value):
    return lax.ppermute(value, "dom", SIBLING)


def across(value):
    return lax.ppermute(value, ("grp", "dom"), facing(lax.axis_size("grp")))


def dot(a, b):
    return jnp.dot(a, b, preferred_element_type=F32)


def gated(half):
    return half + half * jnp.tanh(half)


def columns(ids, span):
    spread = jnp.transpose(jnp.broadcast_to(ids, (128, 128))).astype(jnp.int16)
    lane = lax.broadcasted_iota(jnp.int32, (128, 128), 1).astype(jnp.int16)
    one, zero = jnp.ones((), BF16), jnp.zeros((), BF16)
    return jnp.concatenate(
        [jnp.where(spread == lane + jnp.int16(128 * j), one, zero) for j in range(span // 128)], axis=1
    )


def layer_norm(values):
    average = jnp.mean(values, axis=-1, keepdims=True)
    centred = values - average
    variance = jnp.mean(centred * centred, axis=-1, keepdims=True)
    return centred * lax.rsqrt(variance + 1e-05)


def node_update(rows, node_part, total, edge_second, node_other, node_second):
    aggregate = dot(total.astype(BF16), edge_second).astype(BF16)
    hidden = gated(node_part + 0.5 * dot(aggregate, node_other)).astype(BF16)
    return (rows.astype(F32) + layer_norm(dot(hidden, node_second))).astype(BF16)


def pieces(source, target, arrived, count):
    step = source.shape[0] // count
    return [
        pltpu.make_async_copy(source.at[pl.ds(j * step, step), :], target.at[pl.ds(j * step, step), :], arrived.at[j])
        for j in range(count)
    ]


def halo_body(features, send_rows, edge_first, held, edge_held, near, far, ids, ids_arrived, arrived, edge_arrived):
    core = lax.rem(lax.axis_index("dom"), 2)
    ids_copy = pltpu.make_async_copy(send_rows, ids, ids_arrived)
    ids_copy.start()
    copies = pieces(features, held, arrived, 4)
    edge_copies = pieces(edge_first, edge_held, edge_arrived, 4)
    for copy in copies + edge_copies:
        copy.start()
    ids_copy.wait()
    up, down = ids[0:1, :], ids[1:2, :]
    chosen = jnp.concatenate(
        [columns(jnp.where(core == 0, up, down), ROWS), columns(jnp.where(core == 0, down, up), ROWS)], axis=0
    )
    for copy in copies:
        copy.wait()
    rows = dot(chosen, held[...]).astype(BF16)
    near[...] = rows[:HALO, :]
    far[...] = rows[HALO:, :]
    for copy in edge_copies:
        copy.wait()


def local_body(features, neighbors, edge_first, node_first, projected, self_part, early, node_part, node_self, arrived):
    copy = pltpu.make_async_copy(node_first.at[pl.ds(0, H), :], node_self, arrived)
    copy.start()
    projected[...] = (0.5 * dot(features[...], edge_first[H:, :])).astype(BF16)
    self_part[...] = 0.5 * dot(features[...], edge_first[:H, :])
    chosen = jnp.concatenate([columns(neighbors[0:1, s : s + 128], ROWS) for s in range(0, ROWS, 128)], axis=0)
    early[...] = self_part[...] + dot(chosen, projected[...])
    copy.wait()
    node_part[...] = 0.5 * dot(features[...], node_self[...])


def pool(target, membership, updated):
    belongs = jnp.concatenate(
        [
            jnp.where(membership[j : j + 1, :] == target, jnp.ones((), F32), jnp.zeros((), F32)).astype(BF16)
            for j in range(ROWS // 128)
        ],
        axis=1,
    )
    count = dot(belongs, jnp.ones((ROWS, 128), BF16))
    high = jnp.floor(count * (1.0 / 64.0))
    lane = lax.broadcasted_iota(jnp.int32, count.shape, 1)
    return dot(belongs, updated).astype(BF16), jnp.where(lane < 64, high, count - 64.0 * high).astype(BF16)


def fine_body(
    features, local, self_part, early, node_part, near, far, neighbors, membership,
    edge_first, edge_second, node_first, node_second,
    updated, first,
    projected, second, node_other, last, arrived,
):
    copies = [
        pltpu.make_async_copy(edge_second, second, arrived.at[0]),
        pltpu.make_async_copy(node_first.at[pl.ds(H, H), :], node_other, arrived.at[1]),
        pltpu.make_async_copy(node_second, last, arrived.at[2]),
    ]
    for copy in copies:
        copy.start()
    device = lax.axis_index("dom")
    core = lax.rem(device, 2)
    projected[0:ROWS, :] = local[...]
    below = jnp.where(core == 0, far[...], near[...])
    above = jnp.where(core == 0, near[...], far[...])
    halo = jnp.concatenate([below, above], axis=0)
    projected[ROWS:, :] = (0.5 * dot(halo, edge_first[H:, :])).astype(BF16)

    for tile in range(ROWS // TILE):
        here = slice(tile * TILE, (tile + 1) * TILE)
        spans = range(tile * TILE, (tile + 1) * TILE, 128)
        chosen = jnp.concatenate(
            [columns(neighbors[0:1, s : s + 128] - ROWS, 2 * HALO) for s in spans], axis=0
        )
        total = gated(early[here, :] + dot(chosen, projected[ROWS:, :]))
        for k in range(1, 4):
            chosen = jnp.concatenate(
                [columns(neighbors[k : k + 1, s : s + 128], ROWS + 2 * HALO) for s in spans], axis=0
            )
            total = total + gated(self_part[here, :] + dot(chosen, projected[...]))
        if tile == 0:
            for copy in copies:
                copy.wait()
        updated[here, :] = node_update(
            features[here, :], node_part[here, :], total, second[...], node_other[...], last[...]
        )

    target = (device + 2 - 4 * core) * OWNED + lax.broadcasted_iota(jnp.int32, (OWNED, 128), 0)
    first[:, :H], first[:, H:] = pool(target, membership, updated[...])

def pool_body(updated, membership, base, own):
    device = lax.axis_index("dom")
    core = lax.rem(device, 2)
    row = lax.broadcasted_iota(jnp.int32, (CHIP, 128), 0)
    target = jnp.concatenate([(device - 2 + 3 * core) * OWNED + row, (device - core) * OWNED + row], axis=0)
    sums, counts = pool(target, membership, updated[...])
    base[:, :H], base[:, H:] = sums[:CHIP, :], counts[:CHIP, :]
    own[:, :H], own[:, H:] = sums[CHIP:, :], counts[CHIP:, :]


def own_body(
    coarse, links, edge_first, node_first, edge_second, node_second,
    early, self_part, node_part, edge_held, node_held, arrived,
):
    copies = [
        pltpu.make_async_copy(edge_second, edge_held, arrived.at[0]),
        pltpu.make_async_copy(node_second, node_held, arrived.at[1]),
    ]
    for copy in copies:
        copy.start()
    start = lax.div(lax.axis_index("dom"), 2) * CHIP
    rows = coarse[...]
    projected = (0.5 * dot(rows, edge_first[H:, :])).astype(BF16)
    self_part[...] = 0.5 * dot(rows, edge_first[:H, :])
    node_part[...] = 0.5 * dot(rows, node_first[:H, :])
    chosen = jnp.concatenate([columns(links[k : k + 1, :] - start, CHIP) for k in range(8)], axis=0)
    early[...] = dot(chosen, projected)
    for copy in copies:
        copy.wait()


def far_body(early, far, links, edge_first, other):
    device = lax.axis_index("dom")
    start = (lax.div(device, 2) - 1 + 2 * lax.rem(device, 2)) * CHIP
    projected = (0.5 * dot(far[...], edge_first[H:, :])).astype(BF16)
    chosen = jnp.concatenate([columns(links[k : k + 1, :] - start, CHIP) for k in range(8)], axis=0)
    other[...] = early[...] + dot(chosen, projected)


def coarse_body(
    coarse, early, self_part, node_part, near, links, edge_first, edge_second, node_first, node_second, updated
):
    device = lax.axis_index("dom")
    start = (lax.div(device, 2) + 1 - 2 * lax.rem(device, 2)) * CHIP
    projected = (0.5 * dot(near[...], edge_first[H:, :])).astype(BF16)
    chosen = jnp.concatenate([columns(links[k : k + 1, :] - start, CHIP) for k in range(8)], axis=0)
    other = early[...] + dot(chosen, projected)
    total = jnp.zeros((CHIP, H), F32)
    for k in range(8):
        total = total + gated(self_part[...] + other[k * CHIP : (k + 1) * CHIP, :])
    updated[...] = node_update(
        coarse[...], node_part[...], total, edge_second[...], node_first[H:, :], node_second[...]
    )


def spread_body(fine, coarse, membership, partial, far_rows, near_rows):
    device = lax.axis_index("dom")
    core = lax.rem(device, 2)
    chip = lax.div(device, 2)
    for j in range(ROWS // 256):
        here = slice(j * 256, (j + 1) * 256)

        def rows_of(which):
            return jnp.concatenate(
                [columns(membership[2 * j + i : 2 * j + i + 1, :] - which * CHIP, CHIP) for i in range(2)], axis=0
            )

        partial[here, :] = fine[here, :].astype(F32) + dot(rows_of(chip), coarse[...])
        far_rows[here, :] = rows_of(chip - 1 + 2 * core)
        near_rows[here, :] = rows_of(chip + 1 - 2 * core)


def unpool_body(partial, far_rows, near_rows, far, near, result, made, sent):
    lookup = jnp.concatenate([far[...], near[...]], axis=0)
    copies = []
    for j in range(ROWS // 256):
        here = slice(j * 256, (j + 1) * 256)
        chosen = jnp.concatenate([far_rows[here, :], near_rows[here, :]], axis=1)
        made[here, :] = (partial[here, :] + dot(chosen, lookup)).astype(BF16)
        copy = pltpu.make_async_copy(
            made.at[pl.ds(j * 256, 256), :], result.at[pl.ds(j * 256, 256), :], sent.at[j]
        )
        copy.start()
        copies.append(copy)
    for copy in copies:
        copy.wait()


VMEM = pl.BlockSpec(memory_space=pltpu.VMEM)
ANY = pl.BlockSpec(memory_space=pltpu.HBM)


def call(body, outs, scratch, flops, args, apart=(), out_spec=VMEM):
    args = [pltpu.with_memory_space_constraint(a, pltpu.HBM) if i in apart else a for i, a in enumerate(args)]
    return pl.pallas_call(
        body,
        out_shape=[jax.ShapeDtypeStruct(shape, kind) for shape, kind in outs],
        in_specs=[ANY if i in apart else VMEM for i in range(len(args))],
        out_specs=[out_spec] * len(outs),
        scratch_shapes=scratch,
        compiler_params=pltpu.CompilerParams(vmem_limit_bytes=24 * 1024 * 1024),
        cost_estimate=pl.CostEstimate(flops=flops, bytes_accessed=4 * 1024 * 1024, transcendentals=0),
    )(*args)


def halo_rows(*args):
    return call(
        halo_body,
        [((ROWS, H), BF16), ((2 * H, H), BF16), ((HALO, H), BF16), ((HALO, H), BF16)],
        [
            pltpu.VMEM((2, HALO), jnp.int32),
            pltpu.SemaphoreType.DMA(()),
            pltpu.SemaphoreType.DMA((4,)),
            pltpu.SemaphoreType.DMA((4,)),
        ],
        300000000,
        args,
        (0, 1, 2),
    )


def local_parts(*args):
    return call(
        local_body,
        [((ROWS, H), BF16), ((ROWS, H), F32), ((ROWS, H), F32), ((ROWS, H), F32)],
        [pltpu.VMEM((H, H), BF16), pltpu.SemaphoreType.DMA(())],
        2600000000,
        args,
        (3,),
    )


def fine_stage(*args):
    return call(
        fine_body,
        [((ROWS, H), BF16), ((OWNED, WIDE), BF16)],
        [
            pltpu.VMEM((ROWS + 2 * HALO, H), BF16),
            pltpu.VMEM((H, H), BF16),
            pltpu.VMEM((H, H), BF16),
            pltpu.VMEM((H, H), BF16),
            pltpu.SemaphoreType.DMA((3,)),
        ],
        7000000000,
        args,
        (10, 11, 12),
    )


def pooled(*args):
    return call(pool_body, [((CHIP, WIDE), BF16), ((CHIP, WIDE), BF16)], [], 400000000, args)


def own_parts(*args):
    return call(
        own_body,
        [((8 * CHIP, H), F32), ((CHIP, H), F32), ((CHIP, H), F32), ((H, H), BF16), ((H, H), BF16)],
        [pltpu.SemaphoreType.DMA((2,))],
        400000000,
        args,
        (4, 5),
    )


def far_parts(*args):
    return call(far_body, [((8 * CHIP, H), F32)], [], 200000000, args)[0]


def coarse_stage(*args):
    return call(coarse_body, [((CHIP, H), BF16)], [], 1000000000, args)[0]


def spread(*args):
    return call(spread_body, [((ROWS, H), F32), ((ROWS, CHIP), BF16), ((ROWS, CHIP), BF16)], [], 400000000, args)


def unpooled(*args):
    return call(
        unpool_body,
        [((ROWS, H), BF16)],
        [pltpu.VMEM((ROWS, H), BF16), pltpu.SemaphoreType.DMA((4,))],
        400000000,
        args,
        (),
        ANY,
    )[0]


def shards(
    features,
    send_rows,
    neighbors,
    membership,
    coarse_links,
    edge_first,
    edge_second,
    node_first,
    node_second,
    coarse_edge_first,
    coarse_edge_second,
    coarse_node_first,
    coarse_node_second,
):
    core = lax.rem(lax.axis_index("dom"), 2)
    members = membership.reshape(ROWS // 128, 128)
    my_links = coarse_links.T
    their_links = sibling(my_links)
    held, edge_held, near, far = halo_rows(features, send_rows, edge_first)
    near, far = sibling(near), across(far)
    projected, self_part, early, node_part = local_parts(held, neighbors.T, edge_held, node_first)
    near, far, their_links = lax.optimization_barrier((near, far, their_links))
    updated, first = fine_stage(
        held, projected, self_part, early, node_part, near, far, neighbors.T, members,
        edge_held, edge_second, node_first, node_second,
    )
    links = jnp.where(
        core == 0,
        jnp.concatenate([my_links, their_links], axis=1),
        jnp.concatenate([their_links, my_links], axis=1),
    )
    first = sibling(first)
    base, own = pooled(updated, members)
    nothing = jnp.zeros_like(first)
    extra = jnp.where(
        core == 0, jnp.concatenate([nothing, first], axis=0), jnp.concatenate([first, nothing], axis=0)
    ).astype(F32)
    arrived = across((base.astype(F32) + extra).astype(BF16))
    mine = (own.astype(F32) + arrived.astype(F32)).astype(BF16)
    theirs = sibling(mine)
    sums = mine.astype(F32) + theirs.astype(F32)
    counts = 64.0 * sums[:, H : H + 1] + sums[:, H + 64 : H + 65]
    coarse = (sums[:, :H] / counts).astype(BF16)

    far = across(coarse)
    early, self_part, node_part, edge_held, node_held = lax.optimization_barrier(
        own_parts(coarse, links, coarse_edge_first, coarse_node_first, coarse_edge_second, coarse_node_second)
    )
    far, early = lax.optimization_barrier((far, early))
    near = sibling(far)
    early = far_parts(early, far, links, coarse_edge_first)
    coarse_new = coarse_stage(
        coarse, early, self_part, node_part, near, links, coarse_edge_first, edge_held, coarse_node_first, node_held
    )
    far = across(coarse_new)
    partial, far_rows, near_rows = spread(updated, coarse_new, members)
    far, partial = lax.optimization_barrier((far, partial))
    near = sibling(far)
    return unpooled(partial, far_rows, near_rows, far, near)


def solution(mesh):
    placed = (
        P(("grp", "dom"), None),
        P(("grp", "dom"), None),
        P(("grp", "dom"), None),
        P(("grp", "dom")),
        P(("grp", "dom"), None),
        P(),
        P(),
        P(),
        P(),
        P(),
        P(),
        P(),
        P(),
    )
    return jax.shard_map(
        shards, mesh=mesh, in_specs=placed, out_specs=P(("grp", "dom"), None), check_vma=False
    )
```

time: 62.4 us -> 46.3 us (0.74)
  the two profiles are of different devices: /device:TPU:1 before, /device:TPU:39 now
where the time goes in v2:
time: 46.3 us; the launch traced here: 46 us
  Pallas kernels  18.5 us (40%)
  waiting for transfers between devices  14.9 us (32%)
  starting transfers between devices  11.8 us (25%)
  other arithmetic  0.47 us (1%)
    pallas_call x9, Pallas kernels, call(): pl.pallas_call(body, out_shape=[jax.ShapeDtypeStruct(shape, kind) for sha...  18.5 us
    ppermute x4, waiting for transfers between devices, across(): return lax.ppermute(value, ('grp', 'dom'), facing(lax.axis_size('grp')))  11.9 us
    ppermute x6, starting transfers between devices, sibling(): return lax.ppermute(value, 'dom', SIBLING)  10 us
    ppermute x6, waiting for transfers between devices, sibling(): return lax.ppermute(value, 'dom', SIBLING)  2.96 us
    ppermute x4, starting transfers between devices, across(): return lax.ppermute(value, ('grp', 'dom'), facing(lax.axis_size('grp')))  1.74 us
  transfers between devices with their start and end apart: 10, of which 7 were waited for; matrix products, arithmetic and copies ran while one was open for 0% of the time, Pallas kernels for 13%

profile of v2, /device:TPU:39, one launch (start us, length us, event | category | flops | bytes accessed | tf_op | source)
XLA Modules:
  0.0 46.0 jit_solution(8186118331451101062)
XLA Ops:
  0.0 0.0 copy-start.4
  0.0 0.0 copy-start.2
  0.0 2.0 %shard_map.127 = (bf16[1024,512]{1,0:T(8,128)(2,1)S(1)}, bf16[1024,512]{1,0:T(8,128)(2,1)S(1)}, bf16[128,512]{1,0:T(8,128)(2,1)S(1)}, bf16[128,512]{1,0:T(8,128)(2,1)S(1)}) custom-call(bf16[1024,512]{1,0:T(8,128)(2,1)} %features.1, s32[2,128]{1,0:T(2,128)} %send_rows.1, bf16[1024,512]{1,0:T(8,128)(2,1)} %edge_first.4), custom_call_target="tpu_custom_call" | custom-call | flops 300000000 | bytes 4194304 | tf_op jit(solution)/shard_map/pallas_call | solution.py:262
  2.0 0.8 %collective-permute-start = (bf16[128,512]{1,0:T(8,128)(2,1)S(1)}, bf16[128,512]{1,0:T(8,128)(2,1)S(1)}, u32[]{:S(2)}, u32[]{:S(2)}) collective-permute-start(bf16[128,512]{1,0:T(8,128)(2,1)S(1)} %get-tuple-element.38), channel_id=1, source_target_pairs={{0,1},{1,0},{2,3},{3,2},{4,5},{5,4},{6,7},{7,6},{8,9},{9,8},{10,11... | collective-permute-start | bytes 393224 | tf_op jit(solution)/shard_map/ppermute | solution.py:33
  2.7 1.3 %collective-permute-start.1 = (bf16[128,512]{1,0:T(8,128)(2,1)S(1)}, bf16[128,512]{1,0:T(8,128)(2,1)S(1)}, u32[]{:S(2)}, u32[]{:S(2)}) collective-permute-start(bf16[128,512]{1,0:T(8,128)(2,1)S(1)} %get-tuple-element.39), channel_id=1, source_target_pairs={{0,32},{1,2},{2,1},{3,4},{4,3},{5,6},{6,5},{7,8},{8,7},{9,10},{10,... | collective-permute-start | bytes 393224 | tf_op jit(solution)/shard_map/ppermute | solution.py:37
  4.0 0.0 copy-done.4
  4.0 2.1 %collective-permute-start.2 = (s32[8,64]{1,0:T(8,128)S(1)}, s32[8,64]{1,0:T(8,128)S(1)}, u32[]{:S(2)}, u32[]{:S(2)}) collective-permute-start(s32[8,64]{1,0:T(8,128)S(1)} %bitcast.8), channel_id=1, source_target_pairs={{0,1},{1,0},{2,3},{3,2},{4,5},{5,4},{6,7},{7,6},{8,9},{9,8},{10,11... | collective-permute-start | bytes 6152 | tf_op jit(solution)/shard_map/ppermute | solution.py:33
  6.1 0.0 copy-done.2
  6.1 0.0 copy-start.3
  6.1 3.1 %shard_map.128 = (bf16[1024,512]{1,0:T(8,128)(2,1)S(1)}, f32[1024,512]{1,0:T(8,128)S(1)}, f32[1024,512]{1,0:T(8,128)S(1)}, f32[1024,512]{1,0:T(8,128)S(1)}) custom-call(bf16[1024,512]{1,0:T(8,128)(2,1)S(1)} %get-tuple-element.32.features, s32[4,1024]{1,0:T(4,128)S(1)} %bitcast.3, bf16[1024,512]{1,0:T(8,128)(2,1)S(1)} %get-tuple-element.33.edge_first, ...), custom_call_target="tpu_custom_call" | custom-call | flops 2600000000 | bytes 4194304 | tf_op jit(solution)/shard_map/pallas_call | solution.py:262
  9.2 0.0 collective-permute-done.2
  9.2 0.0 collective-permute-done.near
  9.2 0.0 collective-permute-done.1.far
  9.2 0.0 copy-done.3
  9.2 7.6 %shard_map.129 = (bf16[1024,512]{1,0:T(8,128)(2,1)S(1)}, bf16[64,640]{1,0:T(8,128)(2,1)S(1)}) custom-call(bf16[1024,512]{1,0:T(8,128)(2,1)S(1)} %get-tuple-element.32.features, bf16[1024,512]{1,0:T(8,128)(2,1)S(1)} %get-tuple-element.34.local, f32[1024,512]{1,0:T(8,128)S(1)} %get-tuple-element.35.self_part, f32[1024,512]{1,0:T(8,128)S(1)} %get-tuple-element.36.early, ...), custom_call_target="tpu_custom_call" | custom-call | flops 7000000000 | bytes 4194304 | tf_op jit(solution)/shard_map/pallas_call | solution.py:262
  16.9 0.0 copy-start
  16.9 0.0 copy-start.1
  16.9 0.2 collective-permute-start.3
  17.1 0.6 %shard_map.130 = (bf16[128,640]{1,0:T(8,128)(2,1)S(1)}, bf16[128,640]{1,0:T(8,128)(2,1)S(1)}) custom-call(bf16[1024,512]{1,0:T(8,128)(2,1)S(1)} %get-tuple-element.42.updated.fine, s32[8,128]{1,0:T(8,128)S(1)} %bitcast.6), custom_call_target="tpu_custom_call" | custom-call | flops 400000000 | bytes 4194304 | tf_op jit(solution)/shard_map/pallas_call | solution.py:262
  17.6 0.6 %collective-permute-done.3 = bf16[64,640]{1,0:T(8,128)(2,1)S(1)} collective-permute-done((bf16[64,640]{1,0:T(8,128)(2,1)S(1)}, bf16[64,640]{1,0:T(8,128)(2,1)S(1)}, u32[]{:S(2)}, u32[]{:S(2)}) %collective-permute-start.3) | collective-permute-done | bytes 81952 | tf_op jit(solution)/shard_map/ppermute | solution.py:33
  18.3 0.1 collective-permute-start.4
  18.4 5.0 %collective-permute-done.4 = bf16[128,640]{1,0:T(8,128)(2,1)S(1)} collective-permute-done((bf16[128,640]{1,0:T(8,128)(2,1)S(1)}, bf16[128,640]{1,0:T(8,128)(2,1)S(1)}, u32[]{:S(2)}, u32[]{:S(2)}) %collective-permute-start.4) | collective-permute-done | bytes 163872 | tf_op jit(solution)/shard_map/ppermute | solution.py:37
  23.5 2.1 %collective-permute-start.5 = (bf16[128,640]{1,0:T(8,128)(2,1)S(1)}, bf16[128,640]{1,0:T(8,128)(2,1)S(1)}, u32[]{:S(2)}, u32[]{:S(2)}) collective-permute-start(bf16[128,640]{1,0:T(8,128)(2,1)S(1)} %add_convert_fusion), channel_id=1, source_target_pairs={{0,1},{1,0},{2,3},{3,2},{4,5},{5,4},{6,7},{7,6},{8,9},{9,8},{10,11... | collective-permute-start | bytes 491528 | tf_op jit(solution)/shard_map/ppermute | solution.py:33
  25.5 1.0 %collective-permute-done.5 = bf16[128,640]{1,0:T(8,128)(2,1)S(1)} collective-permute-done((bf16[128,640]{1,0:T(8,128)(2,1)S(1)}, bf16[128,640]{1,0:T(8,128)(2,1)S(1)}, u32[]{:S(2)}, u32[]{:S(2)}) %collective-permute-start.5) | collective-permute-done | bytes 163872 | tf_op jit(solution)/shard_map/ppermute | solution.py:33
  26.6 0.2 fusion.1
  26.8 0.1 fusion.coarse
  26.9 0.3 collective-permute-start.6
  27.2 0.1 add_select_fusion.links
  27.2 0.0 copy-done
  27.2 0.0 copy-done.1
  27.3 1.2 %shard_map.131 = (f32[1024,512]{1,0:T(8,128)S(1)}, f32[128,512]{1,0:T(8,128)S(1)}, f32[128,512]{1,0:T(8,128)S(1)}, bf16[512,512]{1,0:T(8,128)(2,1)S(1)}, bf16[512,512]{1,0:T(8,128)(2,1)S(1)}) custom-call(bf16[128,512]{1,0:T(8,128)(2,1)S(1)} %fusion.coarse, s32[8,128]{1,0:T(8,128)S(1)} %add_select_fusion.links, bf16[1024,512]{1,0:T(8,128)(2,1)S(1)} %copy-done, ...), custom_call_target="tpu_custom_call" | custom-call | flops 400000000 | bytes 4194304 | tf_op jit(solution)/shard_map/pallas_call | solution.py:262
  28.5 3.0 %collective-permute-done.6.far = bf16[128,512]{1,0:T(8,128)(2,1)S(1)} collective-permute-done((bf16[128,512]{1,0:T(8,128)(2,1)S(1)}, bf16[128,512]{1,0:T(8,128)(2,1)S(1)}, u32[]{:S(2)}, u32[]{:S(2)}) %collective-permute-start.6) | collective-permute-done | bytes 131104 | tf_op jit(solution)/shard_map/ppermute | solution.py:37
  31.5 2.5 %collective-permute-start.7 = (bf16[128,512]{1,0:T(8,128)(2,1)S(1)}, bf16[128,512]{1,0:T(8,128)(2,1)S(1)}, u32[]{:S(2)}, u32[]{:S(2)}) collective-permute-start(bf16[128,512]{1,0:T(8,128)(2,1)S(1)} %collective-permute-done.6.far), channel_id=1, source_target_pairs={{0,1},{1,0},{2,3},{3,2},{4,5},{5,4},{6,7},{7,6},{8,9},{9,8},{10,11... | collective-permute-start | bytes 393224 | tf_op jit(solution)/shard_map/ppermute | solution.py:33
  34.0 0.6 %shard_map.132.early = f32[1024,512]{1,0:T(8,128)S(1)} custom-call(f32[1024,512]{1,0:T(8,128)S(1)} %get-tuple-element.48.early, bf16[128,512]{1,0:T(8,128)(2,1)S(1)} %collective-permute-done.6.far, s32[8,128]{1,0:T(8,128)S(1)} %add_select_fusion.links, bf16[1024,512]{1,0:T(8,128)(2,1)S(1)} %copy-done), custom_call_target="tpu_custom_call" | custom-call | flops 200000000 | bytes 4194304 | tf_op jit(solution)/shard_map/pallas_call | solution.py:262
  34.7 0.3 collective-permute-done.7.near
  35.0 1.6 %shard_map.133.coarse = bf16[128,512]{1,0:T(8,128)(2,1)S(1)} custom-call(bf16[128,512]{1,0:T(8,128)(2,1)S(1)} %fusion.coarse, f32[1024,512]{1,0:T(8,128)S(1)} %shard_map.132.early, f32[128,512]{1,0:T(8,128)S(1)} %get-tuple-element.50.self_part, f32[128,512]{1,0:T(8,128)S(1)} %get-tuple-element.51.node_part, ...), custom_call_target="tpu_custom_call" | custom-call | flops 1000000000 | bytes 4194304 | tf_op jit(solution)/shard_map/pallas_call | solution.py:262
  36.7 0.1 collective-permute-start.8
  36.8 0.5 %shard_map.134 = (f32[1024,512]{1,0:T(8,128)S(1)}, bf16[1024,128]{1,0:T(8,128)(2,1)S(1)}, bf16[1024,128]{1,0:T(8,128)(2,1)S(1)}) custom-call(bf16[1024,512]{1,0:T(8,128)(2,1)S(1)} %get-tuple-element.42.updated.fine, bf16[128,512]{1,0:T(8,128)(2,1)S(1)} %shard_map.133.coarse, s32[8,128]{1,0:T(8,128)S(1)} %bitcast.7), custom_call_target="tpu_custom_call" | custom-call | flops 400000000 | bytes 4194304 | tf_op jit(solution)/shard_map/pallas_call | solution.py:262
  37.3 3.9 %collective-permute-done.8.far = bf16[128,512]{1,0:T(8,128)(2,1)S(1)} collective-permute-done((bf16[128,512]{1,0:T(8,128)(2,1)S(1)}, bf16[128,512]{1,0:T(8,128)(2,1)S(1)}, u32[]{:S(2)}, u32[]{:S(2)}) %collective-permute-start.8) | collective-permute-done | bytes 131104 | tf_op jit(solution)/shard_map/ppermute | solution.py:37
  41.1 2.5 %collective-permute-start.9 = (bf16[128,512]{1,0:T(8,128)(2,1)S(1)}, bf16[128,512]{1,0:T(8,128)(2,1)S(1)}, u32[]{:S(2)}, u32[]{:S(2)}) collective-permute-start(bf16[128,512]{1,0:T(8,128)(2,1)S(1)} %collective-permute-done.8.far), channel_id=1, source_target_pairs={{0,1},{1,0},{2,3},{3,2},{4,5},{5,4},{6,7},{7,6},{8,9},{9,8},{10,11... | collective-permute-start | bytes 393224 | tf_op jit(solution)/shard_map/ppermute | solution.py:33
  43.6 1.0 %collective-permute-done.9.near = bf16[128,512]{1,0:T(8,128)(2,1)S(1)} collective-permute-done((bf16[128,512]{1,0:T(8,128)(2,1)S(1)}, bf16[128,512]{1,0:T(8,128)(2,1)S(1)}, u32[]{:S(2)}, u32[]{:S(2)}) %collective-permute-start.9) | collective-permute-done | bytes 131104 | tf_op jit(solution)/shard_map/ppermute | solution.py:33
  44.6 1.2 %shard_map.135 = bf16[1024,512]{1,0:T(8,128)(2,1)} custom-call(f32[1024,512]{1,0:T(8,128)S(1)} %get-tuple-element.55.partial, bf16[1024,128]{1,0:T(8,128)(2,1)S(1)} %get-tuple-element.56.far_rows, bf16[1024,128]{1,0:T(8,128)(2,1)S(1)} %get-tuple-element.57.near_rows, bf16[128,512]{1,0:T(8,128)(2,1)S(1)} %collective-permute-done.8.far, ...), custom_call_target="tpu_custom_call" | custom-call | flops 400000000 | bytes 4194304 | tf_op jit(solution)/shard_map/pallas_call | solution.py:262
  (3 shorter events, 0.1 us)
Async XLA Ops:
  0.0 4.0 %copy-start.4 = (s32[64,8]{0,1:T(8,128)S(1)}, s32[64,8]{0,1:T(8,128)}, u32[]{:S(2)}) copy-start(s32[64,8]{0,1:T(8,128)} %param.17) | copy-start | bytes 6148
  0.0 6.1 %copy-start.2 = (s32[1024,4]{0,1:T(4,128)S(1)}, s32[1024,4]{0,1:T(4,128)}, u32[]{:S(2)}) copy-start(s32[1024,4]{0,1:T(4,128)} %param.15) | copy-start | bytes 49156
  2.0 7.2 %collective-permute-start = (bf16[128,512]{1,0:T(8,128)(2,1)S(1)}, bf16[128,512]{1,0:T(8,128)(2,1)S(1)}, u32[]{:S(2)}, u32[]{:S(2)}) collective-permute-start(bf16[128,512]{1,0:T(8,128)(2,1)S(1)} %get-tuple-element.38), channel_id=1, source_target_pairs={{0,1},{1,0},{2,3},{3,2},{4,5},{5,4},{6,7},{7,6},{8,9},{9,8},{10,11... | collective-permute-start | bytes 393224 | tf_op jit(solution)/shard_map/ppermute | solution.py:33
  2.7 6.5 %collective-permute-start.1 = (bf16[128,512]{1,0:T(8,128)(2,1)S(1)}, bf16[128,512]{1,0:T(8,128)(2,1)S(1)}, u32[]{:S(2)}, u32[]{:S(2)}) collective-permute-start(bf16[128,512]{1,0:T(8,128)(2,1)S(1)} %get-tuple-element.39), channel_id=1, source_target_pairs={{0,32},{1,2},{2,1},{3,4},{4,3},{5,6},{6,5},{7,8},{8,7},{9,10},{10,... | collective-permute-start | bytes 393224 | tf_op jit(solution)/shard_map/ppermute | solution.py:37
  4.0 5.2 %collective-permute-start.2 = (s32[8,64]{1,0:T(8,128)S(1)}, s32[8,64]{1,0:T(8,128)S(1)}, u32[]{:S(2)}, u32[]{:S(2)}) collective-permute-start(s32[8,64]{1,0:T(8,128)S(1)} %bitcast.8), channel_id=1, source_target_pairs={{0,1},{1,0},{2,3},{3,2},{4,5},{5,4},{6,7},{7,6},{8,9},{9,8},{10,11... | collective-permute-start | bytes 6152 | tf_op jit(solution)/shard_map/ppermute | solution.py:33
  6.1 3.1 %copy-start.3 = (s32[1024]{0:T(1024)S(1)}, s32[1024]{0:T(1024)}, u32[]{:S(2)}) copy-start(s32[1024]{0:T(1024)} %param.16) | copy-start | bytes 12292
  16.9 10.4 %copy-start = (bf16[1024,512]{1,0:T(8,128)(2,1)S(1)}, bf16[1024,512]{1,0:T(8,128)(2,1)}, u32[]{:S(2)}) copy-start(bf16[1024,512]{1,0:T(8,128)(2,1)} %edge_first.7) | copy-start | bytes 3145732
  16.9 10.4 %copy-start.1 = (bf16[1024,512]{1,0:T(8,128)(2,1)S(1)}, bf16[1024,512]{1,0:T(8,128)(2,1)}, u32[]{:S(2)}) copy-start(bf16[1024,512]{1,0:T(8,128)(2,1)} %node_first.7) | copy-start | bytes 3145732
  16.9 1.4 %collective-permute-start.3 = (bf16[64,640]{1,0:T(8,128)(2,1)S(1)}, bf16[64,640]{1,0:T(8,128)(2,1)S(1)}, u32[]{:S(2)}, u32[]{:S(2)}) collective-permute-start(bf16[64,640]{1,0:T(8,128)(2,1)S(1)} %get-tuple-element.45), channel_id=1, source_target_pairs={{0,1},{1,0},{2,3},{3,2},{4,5},{5,4},{6,7},{7,6},{8,9},{9,8},{10,11... | collective-permute-start | bytes 245768 | tf_op jit(solution)/shard_map/ppermute | solution.py:33
  18.3 5.1 %collective-permute-start.4 = (bf16[128,640]{1,0:T(8,128)(2,1)S(1)}, bf16[128,640]{1,0:T(8,128)(2,1)S(1)}, u32[]{:S(2)}, u32[]{:S(2)}) collective-permute-start(bf16[128,640]{1,0:T(8,128)(2,1)S(1)} %add_convert_fusion.1), channel_id=1, source_target_pairs={{0,32},{1,2},{2,1},{3,4},{4,3},{5,6},{6,5},{7,8},{8,7},{9,10},{10,... | collective-permute-start | bytes 491528 | tf_op jit(solution)/shard_map/ppermute | solution.py:37
  23.5 3.1 %collective-permute-start.5 = (bf16[128,640]{1,0:T(8,128)(2,1)S(1)}, bf16[128,640]{1,0:T(8,128)(2,1)S(1)}, u32[]{:S(2)}, u32[]{:S(2)}) collective-permute-start(bf16[128,640]{1,0:T(8,128)(2,1)S(1)} %add_convert_fusion), channel_id=1, source_target_pairs={{0,1},{1,0},{2,3},{3,2},{4,5},{5,4},{6,7},{7,6},{8,9},{9,8},{10,11... | collective-permute-start | bytes 491528 | tf_op jit(solution)/shard_map/ppermute | solution.py:33
  26.9 4.7 %collective-permute-start.6 = (bf16[128,512]{1,0:T(8,128)(2,1)S(1)}, bf16[128,512]{1,0:T(8,128)(2,1)S(1)}, u32[]{:S(2)}, u32[]{:S(2)}) collective-permute-start(bf16[128,512]{1,0:T(8,128)(2,1)S(1)} %fusion.coarse), channel_id=1, source_target_pairs={{0,32},{1,2},{2,1},{3,4},{4,3},{5,6},{6,5},{7,8},{8,7},{9,10},{10,... | collective-permute-start | bytes 393224 | tf_op jit(solution)/shard_map/ppermute | solution.py:37
  31.5 3.5 %collective-permute-start.7 = (bf16[128,512]{1,0:T(8,128)(2,1)S(1)}, bf16[128,512]{1,0:T(8,128)(2,1)S(1)}, u32[]{:S(2)}, u32[]{:S(2)}) collective-permute-start(bf16[128,512]{1,0:T(8,128)(2,1)S(1)} %collective-permute-done.6.far), channel_id=1, source_target_pairs={{0,1},{1,0},{2,3},{3,2},{4,5},{5,4},{6,7},{7,6},{8,9},{9,8},{10,11... | collective-permute-start | bytes 393224 | tf_op jit(solution)/shard_map/ppermute | solution.py:33
  36.7 4.5 %collective-permute-start.8 = (bf16[128,512]{1,0:T(8,128)(2,1)S(1)}, bf16[128,512]{1,0:T(8,128)(2,1)S(1)}, u32[]{:S(2)}, u32[]{:S(2)}) collective-permute-start(bf16[128,512]{1,0:T(8,128)(2,1)S(1)} %shard_map.133.coarse), channel_id=1, source_target_pairs={{0,32},{1,2},{2,1},{3,4},{4,3},{5,6},{6,5},{7,8},{8,7},{9,10},{10,... | collective-permute-start | bytes 393224 | tf_op jit(solution)/shard_map/ppermute | solution.py:37
  41.1 3.5 %collective-permute-start.9 = (bf16[128,512]{1,0:T(8,128)(2,1)S(1)}, bf16[128,512]{1,0:T(8,128)(2,1)S(1)}, u32[]{:S(2)}, u32[]{:S(2)}) collective-permute-start(bf16[128,512]{1,0:T(8,128)(2,1)S(1)} %collective-permute-done.8.far), channel_id=1, source_target_pairs={{0,1},{1,0},{2,3},{3,2},{4,5},{5,4},{6,7},{7,6},{8,9},{9,8},{10,11... | collective-permute-start | bytes 393224 | tf_op jit(solution)/shard_map/ppermute | solution.py:33

commit v3 on v2

--- a/solution.py
+++ b/solution.py
@@ -11,7 +11,7 @@
 OWNED = 64
 CHIP = 128
 TILE = 512
-WIDE = H + 128
+PACK = 2 * CHIP + 16
 DOM = 32
 F32 = jnp.float32
 BF16 = jnp.bfloat16
@@ -19,12 +19,12 @@
 SIBLING = [(i, i ^ 1) for i in range(DOM)]
 
 
-def facing(parts):
+def facing(parts, step):
     pairs = []
     for part in range(parts):
         other = part ^ 1 if (part ^ 1) < parts else part
         for i in range(DOM):
-            j = i + 1 if i % 2 else i - 1
+            j = i + 2 * step - 1 if i % 2 else i - 2 * step + 1
             pairs.append((part * DOM + i, part * DOM + j if 0 <= j < DOM else other * DOM + i))
     return pairs
 
@@ -33,8 +33,15 @@
     return lax.ppermute(value, "dom", SIBLING)
 
 
-def across(value):
-    return lax.ppermute(value, ("grp", "dom"), facing(lax.axis_size("grp")))
+def across(value, step=1):
+    return lax.ppermute(value, ("grp", "dom"), facing(lax.axis_size("grp"), step))
+
+
+def place():
+    device = lax.axis_index("dom")
+    core = lax.rem(device, 2)
+    chip = lax.div(device, 2)
+    return core, chip, chip - 1 + 2 * core, chip + 1 - 2 * core
 
 
 def dot(a, b):
@@ -108,7 +115,9 @@
     node_part[...] = 0.5 * dot(features[...], node_self[...])
 
 
-def pool(target, membership, updated):
+def pool(chips, membership, updated):
+    row = lax.broadcasted_iota(jnp.int32, (CHIP, 128), 0)
+    target = jnp.concatenate([chip * CHIP + row for chip in chips], axis=0)
     belongs = jnp.concatenate(
         [
             jnp.where(membership[j : j + 1, :] == target, jnp.ones((), F32), jnp.zeros((), F32)).astype(BF16)
@@ -116,10 +125,18 @@
         ],
         axis=1,
     )
-    count = dot(belongs, jnp.ones((ROWS, 128), BF16))
+    count = lax.dot_general(
+        jnp.ones((16, ROWS), BF16), belongs, (((1,), (1,)), ((), ())), preferred_element_type=F32
+    )
     high = jnp.floor(count * (1.0 / 64.0))
-    lane = lax.broadcasted_iota(jnp.int32, count.shape, 1)
-    return dot(belongs, updated).astype(BF16), jnp.where(lane < 64, high, count - 64.0 * high).astype(BF16)
+    digit = lax.broadcasted_iota(jnp.int32, count.shape, 0)
+    return dot(belongs, updated).astype(BF16), jnp.where(digit == 0, high, count - 64.0 * high).astype(BF16)
+
+
+def divided(sums, count):
+    whole = jnp.maximum(64.0 * count[0:1, :] + count[1:2, :], 1.0)
+    column = jnp.transpose(jnp.broadcast_to(whole, (CHIP, 128)))
+    return (sums / jnp.concatenate([column] * (H // 128), axis=1)).astype(BF16)
 
 
 def fine_body(
@@ -162,62 +179,81 @@
             features[here, :], node_part[here, :], total, second[...], node_other[...], last[...]
         )
 
-    target = (device + 2 - 4 * core) * OWNED + lax.broadcasted_iota(jnp.int32, (OWNED, 128), 0)
-    first[:, :H], first[:, H:] = pool(target, membership, updated[...])
-
-def pool_body(updated, membership, base, own):
-    device = lax.axis_index("dom")
-    core = lax.rem(device, 2)
-    row = lax.broadcasted_iota(jnp.int32, (CHIP, 128), 0)
-    target = jnp.concatenate([(device - 2 + 3 * core) * OWNED + row, (device - core) * OWNED + row], axis=0)
-    sums, counts = pool(target, membership, updated[...])
-    base[:, :H], base[:, H:] = sums[:CHIP, :], counts[:CHIP, :]
-    own[:, :H], own[:, H:] = sums[CHIP:, :], counts[CHIP:, :]
-
-
-def own_body(
-    coarse, links, edge_first, node_first, edge_second, node_second,
-    early, self_part, node_part, edge_held, node_held, arrived,
+    _, chip, _, near_chip = place()
+    first[: 2 * CHIP, :], counts = pool((near_chip, chip), membership, updated[...])
+    first[2 * CHIP :, :] = jnp.concatenate([counts, jnp.zeros((16, H - 2 * CHIP), BF16)], axis=1)
+
+
+def keep_body(updated, membership, first, keep):
+    _, _, far_chip, _ = place()
+    keep[:CHIP, :], counts = pool((far_chip,), membership, updated[...])
+    keep[CHIP:, :] = first[CHIP:, :]
+    keep[2 * CHIP :, :CHIP] = counts
+
+
+def totals_body(mine, one, two, passed):
+    core, chip, _, _ = place()
+    reach = jnp.where(core == 0, chip, DOM // 2 - 1 - chip)
+    has_one = jnp.where(reach >= 1, 1.0, 0.0)
+    has_two = jnp.where(reach >= 2, 1.0, 0.0)
+    counts = slice(2 * CHIP, PACK)
+    sums = mine[:CHIP, :].astype(F32) + has_one * one[CHIP : 2 * CHIP, :].astype(F32)
+    sums = sums + has_two * two[:CHIP, :].astype(F32)
+    count = mine[counts, :CHIP].astype(F32) + has_one * one[counts, CHIP : 2 * CHIP].astype(F32)
+    count = count + has_two * two[CHIP:, :CHIP].astype(F32)
+    passed[:CHIP, :] = divided(sums, count)
+    passed[CHIP : 2 * CHIP, :] = (has_one * one[:CHIP, :].astype(F32)).astype(BF16)
+    passed[counts, :] = (has_one * one[counts, :].astype(F32)).astype(BF16)
+
+
+def links_body(
+    links, edge_first, edge_second, node_first, node_second,
+    own_rows, far_rows, near_rows, edge_first_held, edge_second_held, node_first_held, node_second_held, arrived,
 ):
     copies = [
-        pltpu.make_async_copy(edge_second, edge_held, arrived.at[0]),
-        pltpu.make_async_copy(node_second, node_held, arrived.at[1]),
+        pltpu.make_async_copy(source, target, arrived.at[i])
+        for i, (source, target) in enumerate(
+            (
+                (edge_first, edge_first_held),
+                (edge_second, edge_second_held),
+                (node_first, node_first_held),
+                (node_second, node_second_held),
+            )
+        )
     ]
     for copy in copies:
         copy.start()
-    start = lax.div(lax.axis_index("dom"), 2) * CHIP
-    rows = coarse[...]
-    projected = (0.5 * dot(rows, edge_first[H:, :])).astype(BF16)
-    self_part[...] = 0.5 * dot(rows, edge_first[:H, :])
-    node_part[...] = 0.5 * dot(rows, node_first[:H, :])
-    chosen = jnp.concatenate([columns(links[k : k + 1, :] - start, CHIP) for k in range(8)], axis=0)
-    early[...] = dot(chosen, projected)
+    _, chip, far_chip, near_chip = place()
+    for rows, which in ((own_rows, chip), (far_rows, far_chip), (near_rows, near_chip)):
+        for k in range(8):
+            rows[k * CHIP : (k + 1) * CHIP, :] = columns(links[k : k + 1, :] - which * CHIP, CHIP)
     for copy in copies:
         copy.wait()
 
 
-def far_body(early, far, links, edge_first, other):
-    device = lax.axis_index("dom")
-    start = (lax.div(device, 2) - 1 + 2 * lax.rem(device, 2)) * CHIP
-    projected = (0.5 * dot(far[...], edge_first[H:, :])).astype(BF16)
-    chosen = jnp.concatenate([columns(links[k : k + 1, :] - start, CHIP) for k in range(8)], axis=0)
-    other[...] = early[...] + dot(chosen, projected)
+def far_body(passed, far_rows, edge_first, other):
+    projected = (0.5 * dot(passed[:CHIP, :], edge_first[H:, :])).astype(BF16)
+    other[...] = dot(far_rows[...], projected)
 
 
 def coarse_body(
-    coarse, early, self_part, node_part, near, links, edge_first, edge_second, node_first, node_second, updated
+    mine, passed, got, early, own_rows, near_rows, edge_first, edge_second, node_first, node_second, updated
 ):
-    device = lax.axis_index("dom")
-    start = (lax.div(device, 2) + 1 - 2 * lax.rem(device, 2)) * CHIP
-    projected = (0.5 * dot(near[...], edge_first[H:, :])).astype(BF16)
-    chosen = jnp.concatenate([columns(links[k : k + 1, :] - start, CHIP) for k in range(8)], axis=0)
-    other = early[...] + dot(chosen, projected)
+    counts = slice(2 * CHIP, PACK)
+    between = passed[CHIP : 2 * CHIP, :].astype(F32) + got[CHIP : 2 * CHIP, :].astype(F32)
+    count = passed[counts, :CHIP].astype(F32) + got[counts, :CHIP].astype(F32)
+    coarse = divided(
+        mine[CHIP : 2 * CHIP, :].astype(F32) + between, mine[counts, CHIP : 2 * CHIP].astype(F32) + count
+    )
+    self_part = 0.5 * dot(coarse, edge_first[:H, :])
+    node_part = 0.5 * dot(coarse, node_first[:H, :])
+    both = jnp.concatenate([coarse, got[:CHIP, :]], axis=0)
+    projected = (0.5 * dot(both, edge_first[H:, :])).astype(BF16)
+    other = early[...] + dot(jnp.concatenate([own_rows[...], near_rows[...]], axis=1), projected)
     total = jnp.zeros((CHIP, H), F32)
     for k in range(8):
-        total = total + gated(self_part[...] + other[k * CHIP : (k + 1) * CHIP, :])
-    updated[...] = node_update(
-        coarse[...], node_part[...], total, edge_second[...], node_first[H:, :], node_second[...]
-    )
+        total = total + gated(self_part + other[k * CHIP : (k + 1) * CHIP, :])
+    updated[...] = node_update(coarse, node_part, total, edge_second[...], node_first[H:, :], node_second[...])
 
 
 def spread_body(fine, coarse, membership, partial, far_rows, near_rows):
@@ -300,7 +336,7 @@
 def fine_stage(*args):
     return call(
         fine_body,
-        [((ROWS, H), BF16), ((OWNED, WIDE), BF16)],
+        [((ROWS, H), BF16), ((PACK, H), BF16)],
         [
             pltpu.VMEM((ROWS + 2 * HALO, H), BF16),
             pltpu.VMEM((H, H), BF16),
@@ -314,18 +350,22 @@
     )
 
 
-def pooled(*args):
-    return call(pool_body, [((CHIP, WIDE), BF16), ((CHIP, WIDE), BF16)], [], 400000000, args)
-
-
-def own_parts(*args):
+def kept(*args):
+    return call(keep_body, [((PACK, H), BF16)], [], 200000000, args)[0]
+
+
+def totals(*args):
+    return call(totals_body, [((PACK, H), BF16)], [], 100000000, args)[0]
+
+
+def link_rows(*args):
     return call(
-        own_body,
-        [((8 * CHIP, H), F32), ((CHIP, H), F32), ((CHIP, H), F32), ((H, H), BF16), ((H, H), BF16)],
-        [pltpu.SemaphoreType.DMA((2,))],
+        links_body,
+        [((8 * CHIP, CHIP), BF16)] * 3 + [((2 * H, H), BF16), ((H, H), BF16)] * 2,
+        [pltpu.SemaphoreType.DMA((4,))],
         400000000,
         args,
-        (4, 5),
+        (1, 2, 3, 4),
     )
 
 
@@ -385,29 +425,17 @@
         jnp.concatenate([my_links, their_links], axis=1),
         jnp.concatenate([their_links, my_links], axis=1),
     )
-    first = sibling(first)
-    base, own = pooled(updated, members)
-    nothing = jnp.zeros_like(first)
-    extra = jnp.where(
-        core == 0, jnp.concatenate([nothing, first], axis=0), jnp.concatenate([first, nothing], axis=0)
-    ).astype(F32)
-    arrived = across((base.astype(F32) + extra).astype(BF16))
-    mine = (own.astype(F32) + arrived.astype(F32)).astype(BF16)
-    theirs = sibling(mine)
-    sums = mine.astype(F32) + theirs.astype(F32)
-    counts = 64.0 * sums[:, H : H + 1] + sums[:, H + 64 : H + 65]
-    coarse = (sums[:, :H] / counts).astype(BF16)
-
-    far = across(coarse)
-    early, self_part, node_part, edge_held, node_held = lax.optimization_barrier(
-        own_parts(coarse, links, coarse_edge_first, coarse_node_first, coarse_edge_second, coarse_node_second)
-    )
-    far, early = lax.optimization_barrier((far, early))
-    near = sibling(far)
-    early = far_parts(early, far, links, coarse_edge_first)
-    coarse_new = coarse_stage(
-        coarse, early, self_part, node_part, near, links, coarse_edge_first, edge_held, coarse_node_first, node_held
-    )
+    mine = (kept(updated, members, first).astype(F32) + sibling(first).astype(F32)).astype(BF16)
+    two = across(jnp.concatenate([mine[:CHIP], mine[2 * CHIP :]], axis=0), 2)
+    one = across(mine, 1)
+    prepared = link_rows(links, coarse_edge_first, coarse_edge_second, coarse_node_first, coarse_node_second)
+    one, two, prepared = lax.optimization_barrier((one, two, prepared))
+    own_rows, far_rows, near_rows = prepared[:3]
+    weights = prepared[3:]
+    passed = totals(mine, one, two)
+    got = sibling(passed)
+    early = far_parts(passed, far_rows, weights[0])
+    coarse_new = coarse_stage(mine, passed, got, early, own_rows, near_rows, *weights)
     far = across(coarse_new)
     partial, far_rows, near_rows = spread(updated, coarse_new, members)
     far, partial = lax.optimization_barrier((far, partial))

time: 46.3 us -> 43.1 us (0.931)
  waiting for transfers between devices: 14.9 us -> 11.1 us
  Pallas kernels: 18.5 us -> 19.4 us
    ppermute x4, waiting for transfers between devices: 11.9 us -> 8.48 us  [across(): lax.ppermute(value, ('grp', 'dom'), facing(lax.axis_size('grp'), step))]
    ppermute x4, starting transfers between devices: 1.74 us -> 3.45 us  [across(): lax.ppermute(value, ('grp', 'dom'), facing(lax.axis_size('grp'), step))]
    ppermute x6 -> x5, starting transfers between devices: 10 us -> 8.39 us  [sibling(): return lax.ppermute(value, 'dom', SIBLING)]
    pallas_call x9 -> x10, Pallas kernels: 18.5 us -> 19.4 us  [call(): pl.pallas_call(body, out_shape=[jax.ShapeDtypeStruct(shape, kind) for sha...]
    ppermute x6 -> x5, waiting for transfers between devices: 2.96 us -> 2.61 us  [sibling(): return lax.ppermute(value, 'dom', SIBLING)]
  transfers between devices with their start and end apart: 10 -> 9, of which waited for: 7 -> 5; matrix products, arithmetic and copies ran while one was open for 0% -> 0% of each run, Pallas kernels for 13% -> 15%
where the time goes in v3:
time: 43.1 us; the launch traced here: 42.8 us
  Pallas kernels  19.4 us (45%)
  starting transfers between devices  11.8 us (27%)
  waiting for transfers between devices  11.1 us (26%)
    pallas_call x10, Pallas kernels, call(): pl.pallas_call(body, out_shape=[jax.ShapeDtypeStruct(shape, kind) for sha...  19.4 us
    ppermute x4, waiting for transfers between devices, across(): lax.ppermute(value, ('grp', 'dom'), facing(lax.axis_size('grp'), step))  8.48 us
    ppermute x5, starting transfers between devices, sibling(): return lax.ppermute(value, 'dom', SIBLING)  8.39 us
    ppermute x4, starting transfers between devices, across(): lax.ppermute(value, ('grp', 'dom'), facing(lax.axis_size('grp'), step))  3.45 us
    ppermute x5, waiting for transfers between devices, sibling(): return lax.ppermute(value, 'dom', SIBLING)  2.61 us
  transfers between devices with their start and end apart: 9, of which 5 were waited for; matrix products, arithmetic and copies ran while one was open for 0% of the time, Pallas kernels for 15%

profile of v3, /device:TPU:39, one launch (start us, length us, event | category | flops | bytes accessed | tf_op | source)
XLA Modules:
  0.0 42.8 jit_solution(12508597584307090397)
XLA Ops:
  0.0 0.0 copy-start.2
  0.0 0.0 copy-start.1
  0.0 2.0 %shard_map.127 = (bf16[1024,512]{1,0:T(8,128)(2,1)S(1)}, bf16[1024,512]{1,0:T(8,128)(2,1)S(1)}, bf16[128,512]{1,0:T(8,128)(2,1)S(1)}, bf16[128,512]{1,0:T(8,128)(2,1)S(1)}) custom-call(bf16[1024,512]{1,0:T(8,128)(2,1)} %features.1, s32[2,128]{1,0:T(2,128)} %send_rows.1, bf16[1024,512]{1,0:T(8,128)(2,1)} %edge_first.2), custom_call_target="tpu_custom_call" | custom-call | flops 300000000 | bytes 4194304 | tf_op jit(solution)/shard_map/pallas_call | solution.py:298
  2.0 0.8 %collective-permute-start = (bf16[128,512]{1,0:T(8,128)(2,1)S(1)}, bf16[128,512]{1,0:T(8,128)(2,1)S(1)}, u32[]{:S(2)}, u32[]{:S(2)}) collective-permute-start(bf16[128,512]{1,0:T(8,128)(2,1)S(1)} %get-tuple-element.45), channel_id=1, source_target_pairs={{0,1},{1,0},{2,3},{3,2},{4,5},{5,4},{6,7},{7,6},{8,9},{9,8},{10,11... | collective-permute-start | bytes 393224 | tf_op jit(solution)/shard_map/ppermute | solution.py:33
  2.7 1.3 %collective-permute-start.1 = (bf16[128,512]{1,0:T(8,128)(2,1)S(1)}, bf16[128,512]{1,0:T(8,128)(2,1)S(1)}, u32[]{:S(2)}, u32[]{:S(2)}) collective-permute-start(bf16[128,512]{1,0:T(8,128)(2,1)S(1)} %get-tuple-element.46), channel_id=1, source_target_pairs={{0,32},{1,2},{2,1},{3,4},{4,3},{5,6},{6,5},{7,8},{8,7},{9,10},{10,... | collective-permute-start | bytes 393224 | tf_op jit(solution)/shard_map/ppermute | solution.py:37
  4.0 0.0 copy-done.2
  4.0 2.1 %collective-permute-start.2 = (s32[8,64]{1,0:T(8,128)S(1)}, s32[8,64]{1,0:T(8,128)S(1)}, u32[]{:S(2)}, u32[]{:S(2)}) collective-permute-start(s32[8,64]{1,0:T(8,128)S(1)} %bitcast.8), channel_id=1, source_target_pairs={{0,1},{1,0},{2,3},{3,2},{4,5},{5,4},{6,7},{7,6},{8,9},{9,8},{10,11... | collective-permute-start | bytes 6152 | tf_op jit(solution)/shard_map/ppermute | solution.py:33
  6.1 0.0 copy-done.1
  6.1 0.0 copy-start
  6.1 3.1 %shard_map.128 = (bf16[1024,512]{1,0:T(8,128)(2,1)S(1)}, f32[1024,512]{1,0:T(8,128)S(1)}, f32[1024,512]{1,0:T(8,128)S(1)}, f32[1024,512]{1,0:T(8,128)S(1)}) custom-call(bf16[1024,512]{1,0:T(8,128)(2,1)S(1)} %get-tuple-element.39.features, s32[4,1024]{1,0:T(4,128)S(1)} %bitcast.6, bf16[1024,512]{1,0:T(8,128)(2,1)S(1)} %get-tuple-element.40.edge_first, ...), custom_call_target="tpu_custom_call" | custom-call | flops 2600000000 | bytes 4194304 | tf_op jit(solution)/shard_map/pallas_call | solution.py:298
  9.2 0.0 collective-permute-done.2
  9.2 0.0 collective-permute-done.near
  9.2 0.0 collective-permute-done.1.far
  9.2 0.0 copy-done
  9.2 7.7 %shard_map.129 = (bf16[1024,512]{1,0:T(8,128)(2,1)S(1)}, bf16[272,512]{1,0:T(8,128)(2,1)S(1)}) custom-call(bf16[1024,512]{1,0:T(8,128)(2,1)S(1)} %get-tuple-element.39.features, bf16[1024,512]{1,0:T(8,128)(2,1)S(1)} %get-tuple-element.41.local, f32[1024,512]{1,0:T(8,128)S(1)} %get-tuple-element.42.self_part, f32[1024,512]{1,0:T(8,128)S(1)} %get-tuple-element.43.early, ...), custom_call_target="tpu_custom_call" | custom-call | flops 7000000000 | bytes 4194304 | tf_op jit(solution)/shard_map/pallas_call | solution.py:298
  17.0 0.2 collective-permute-start.3
  17.2 0.4 shard_map.130
  17.6 1.1 %collective-permute-done.3 = bf16[272,512]{1,0:T(8,128)(2,1)S(1)} collective-permute-done((bf16[272,512]{1,0:T(8,128)(2,1)S(1)}, bf16[272,512]{1,0:T(8,128)(2,1)S(1)}, u32[]{:S(2)}, u32[]{:S(2)}) %collective-permute-start.3) | collective-permute-done | bytes 278560 | tf_op jit(solution)/shard_map/ppermute | solution.py:33
  18.6 0.1 add_convert_fusion.mine
  18.7 0.1 collective-permute-start.4
  18.9 1.6 %collective-permute-start.5 = (bf16[144,512]{1,0:T(8,128)(2,1)S(1)}, bf16[144,512]{1,0:T(8,128)(2,1)S(1)}, u32[]{:S(2)}, u32[]{:S(2)}) collective-permute-start(bf16[144,512]{1,0:T(8,128)(2,1)S(1)} %pad_maximum_fusion), channel_id=1, source_target_pairs={{0,32},{1,4},{2,34},{3,6},{4,1},{5,8},{6,3},{7,10},{8,5},{9,12},{1... | collective-permute-start | bytes 442376 | tf_op jit(solution)/shard_map/ppermute | solution.py:37
  20.5 0.1 add_select_fusion.links
  20.6 1.9 %shard_map.131 = (bf16[1024,128]{1,0:T(8,128)(2,1)S(1)}, bf16[1024,128]{1,0:T(8,128)(2,1)S(1)}, bf16[1024,128]{1,0:T(8,128)(2,1)S(1)}, bf16[1024,512]{1,0:T(8,12...) custom-call(s32[8,128]{1,0:T(8,128)S(1)} %add_select_fusion.links, ...), custom_call_target="tpu_custom_call" | custom-call | flops 400000000 | bytes 4194304 | tf_op jit(solution)/shard_map/pallas_call | solution.py:298
  22.5 5.0 %collective-permute-done.5.two = bf16[144,512]{1,0:T(8,128)(2,1)S(1)} collective-permute-done((bf16[144,512]{1,0:T(8,128)(2,1)S(1)}, bf16[144,512]{1,0:T(8,128)(2,1)S(1)}, u32[]{:S(2)}, u32[]{:S(2)}) %collective-permute-start.5) | collective-permute-done | bytes 147488 | tf_op jit(solution)/shard_map/ppermute | solution.py:37
  27.4 0.0 collective-permute-done.4.one
  27.4 0.1 shard_map.132.passed
  27.5 2.9 %collective-permute-start.6 = (bf16[272,512]{1,0:T(8,128)(2,1)S(1)}, bf16[272,512]{1,0:T(8,128)(2,1)S(1)}, u32[]{:S(2)}, u32[]{:S(2)}) collective-permute-start(bf16[272,512]{1,0:T(8,128)(2,1)S(1)} %shard_map.132.passed), channel_id=1, source_target_pairs={{0,1},{1,0},{2,3},{3,2},{4,5},{5,4},{6,7},{7,6},{8,9},{9,8},{10,11... | collective-permute-start | bytes 835592 | tf_op jit(solution)/shard_map/ppermute | solution.py:33
  30.4 0.6 %shard_map.133.early = f32[1024,512]{1,0:T(8,128)S(1)} custom-call(bf16[272,512]{1,0:T(8,128)(2,1)S(1)} %shard_map.132.passed, bf16[1024,128]{1,0:T(8,128)(2,1)S(1)} %get-tuple-element.61.far_rows, bf16[1024,512]{1,0:T(8,128)(2,1)S(1)} %get-tuple-element.62.edge_first), custom_call_target="tpu_custom_call" | custom-call | flops 200000000 | bytes 4194304 | tf_op jit(solution)/shard_map/pallas_call | solution.py:298
  31.0 0.6 %collective-permute-done.6.got = bf16[272,512]{1,0:T(8,128)(2,1)S(1)} collective-permute-done((bf16[272,512]{1,0:T(8,128)(2,1)S(1)}, bf16[272,512]{1,0:T(8,128)(2,1)S(1)}, u32[]{:S(2)}, u32[]{:S(2)}) %collective-permute-start.6) | collective-permute-done | bytes 278560 | tf_op jit(solution)/shard_map/ppermute | solution.py:33
  31.6 1.8 %shard_map.134.coarse = bf16[128,512]{1,0:T(8,128)(2,1)S(1)} custom-call(bf16[272,512]{1,0:T(8,128)(2,1)S(1)} %add_convert_fusion.mine, bf16[272,512]{1,0:T(8,128)(2,1)S(1)} %shard_map.132.passed, bf16[272,512]{1,0:T(8,128)(2,1)S(1)} %collective-permute-done.6.got, f32[1024,512]{1,0:T(8,128)S(1)} %shard_map.133.early, ...), custom_call_target="tpu_custom_call" | custom-call | flops 1000000000 | bytes 4194304 | tf_op jit(solution)/shard_map/pallas_call | solution.py:298
  33.4 0.4 %collective-permute-start.7 = (bf16[128,512]{1,0:T(8,128)(2,1)S(1)}, bf16[128,512]{1,0:T(8,128)(2,1)S(1)}, u32[]{:S(2)}, u32[]{:S(2)}) collective-permute-start(bf16[128,512]{1,0:T(8,128)(2,1)S(1)} %shard_map.134.coarse), channel_id=1, source_target_pairs={{0,32},{1,2},{2,1},{3,4},{4,3},{5,6},{6,5},{7,8},{8,7},{9,10},{10,... | collective-permute-start | bytes 393224 | tf_op jit(solution)/shard_map/ppermute | solution.py:37
  33.9 0.5 %shard_map.135 = (f32[1024,512]{1,0:T(8,128)S(1)}, bf16[1024,128]{1,0:T(8,128)(2,1)S(1)}, bf16[1024,128]{1,0:T(8,128)(2,1)S(1)}) custom-call(bf16[1024,512]{1,0:T(8,128)(2,1)S(1)} %get-tuple-element.49.updated.fine, bf16[128,512]{1,0:T(8,128)(2,1)S(1)} %shard_map.134.coarse, s32[8,128]{1,0:T(8,128)S(1)} %bitcast.5), custom_call_target="tpu_custom_call" | custom-call | flops 400000000 | bytes 4194304 | tf_op jit(solution)/shard_map/pallas_call | solution.py:298
  34.4 3.5 %collective-permute-done.7.far = bf16[128,512]{1,0:T(8,128)(2,1)S(1)} collective-permute-done((bf16[128,512]{1,0:T(8,128)(2,1)S(1)}, bf16[128,512]{1,0:T(8,128)(2,1)S(1)}, u32[]{:S(2)}, u32[]{:S(2)}) %collective-permute-start.7) | collective-permute-done | bytes 131104 | tf_op jit(solution)/shard_map/ppermute | solution.py:37
  37.9 2.5 %collective-permute-start.8 = (bf16[128,512]{1,0:T(8,128)(2,1)S(1)}, bf16[128,512]{1,0:T(8,128)(2,1)S(1)}, u32[]{:S(2)}, u32[]{:S(2)}) collective-permute-start(bf16[128,512]{1,0:T(8,128)(2,1)S(1)} %collective-permute-done.7.far), channel_id=1, source_target_pairs={{0,1},{1,0},{2,3},{3,2},{4,5},{5,4},{6,7},{7,6},{8,9},{9,8},{10,11... | collective-permute-start | bytes 393224 | tf_op jit(solution)/shard_map/ppermute | solution.py:33
  40.4 1.0 %collective-permute-done.8.near = bf16[128,512]{1,0:T(8,128)(2,1)S(1)} collective-permute-done((bf16[128,512]{1,0:T(8,128)(2,1)S(1)}, bf16[128,512]{1,0:T(8,128)(2,1)S(1)}, u32[]{:S(2)}, u32[]{:S(2)}) %collective-permute-start.8) | collective-permute-done | bytes 131104 | tf_op jit(solution)/shard_map/ppermute | solution.py:33
  41.4 1.2 %shard_map.136 = bf16[1024,512]{1,0:T(8,128)(2,1)} custom-call(f32[1024,512]{1,0:T(8,128)S(1)} %get-tuple-element.69.partial, bf16[1024,128]{1,0:T(8,128)(2,1)S(1)} %get-tuple-element.70.far_rows, bf16[1024,128]{1,0:T(8,128)(2,1)S(1)} %get-tuple-element.71.near_rows, bf16[128,512]{1,0:T(8,128)(2,1)S(1)} %collective-permute-done.7.far, ...), custom_call_target="tpu_custom_call" | custom-call | flops 400000000 | bytes 4194304 | tf_op jit(solution)/shard_map/pallas_call | solution.py:298
  (3 shorter events, 0.0 us)
Async XLA Ops:
  0.0 4.0 %copy-start.2 = (s32[64,8]{0,1:T(8,128)S(1)}, s32[64,8]{0,1:T(8,128)}, u32[]{:S(2)}) copy-start(s32[64,8]{0,1:T(8,128)} %param.17) | copy-start | bytes 6148
  0.0 6.1 %copy-start.1 = (s32[1024,4]{0,1:T(4,128)S(1)}, s32[1024,4]{0,1:T(4,128)}, u32[]{:S(2)}) copy-start(s32[1024,4]{0,1:T(4,128)} %param.15) | copy-start | bytes 49156
  2.0 7.2 %collective-permute-start = (bf16[128,512]{1,0:T(8,128)(2,1)S(1)}, bf16[128,512]{1,0:T(8,128)(2,1)S(1)}, u32[]{:S(2)}, u32[]{:S(2)}) collective-permute-start(bf16[128,512]{1,0:T(8,128)(2,1)S(1)} %get-tuple-element.45), channel_id=1, source_target_pairs={{0,1},{1,0},{2,3},{3,2},{4,5},{5,4},{6,7},{7,6},{8,9},{9,8},{10,11... | collective-permute-start | bytes 393224 | tf_op jit(solution)/shard_map/ppermute | solution.py:33
  2.7 6.5 %collective-permute-start.1 = (bf16[128,512]{1,0:T(8,128)(2,1)S(1)}, bf16[128,512]{1,0:T(8,128)(2,1)S(1)}, u32[]{:S(2)}, u32[]{:S(2)}) collective-permute-start(bf16[128,512]{1,0:T(8,128)(2,1)S(1)} %get-tuple-element.46), channel_id=1, source_target_pairs={{0,32},{1,2},{2,1},{3,4},{4,3},{5,6},{6,5},{7,8},{8,7},{9,10},{10,... | collective-permute-start | bytes 393224 | tf_op jit(solution)/shard_map/ppermute | solution.py:37
  4.0 5.2 %collective-permute-start.2 = (s32[8,64]{1,0:T(8,128)S(1)}, s32[8,64]{1,0:T(8,128)S(1)}, u32[]{:S(2)}, u32[]{:S(2)}) collective-permute-start(s32[8,64]{1,0:T(8,128)S(1)} %bitcast.8), channel_id=1, source_target_pairs={{0,1},{1,0},{2,3},{3,2},{4,5},{5,4},{6,7},{7,6},{8,9},{9,8},{10,11... | collective-permute-start | bytes 6152 | tf_op jit(solution)/shard_map/ppermute | solution.py:33
  6.1 3.1 %copy-start = (s32[1024]{0:T(1024)S(1)}, s32[1024]{0:T(1024)}, u32[]{:S(2)}) copy-start(s32[1024]{0:T(1024)} %param.16) | copy-start | bytes 12292
  17.0 1.6 %collective-permute-start.3 = (bf16[272,512]{1,0:T(8,128)(2,1)S(1)}, bf16[272,512]{1,0:T(8,128)(2,1)S(1)}, u32[]{:S(2)}, u32[]{:S(2)}) collective-permute-start(bf16[272,512]{1,0:T(8,128)(2,1)S(1)} %get-tuple-element.50.first), channel_id=1, source_target_pairs={{0,1},{1,0},{2,3},{3,2},{4,5},{5,4},{6,7},{7,6},{8,9},{9,8},{10,11... | collective-permute-start | bytes 835592 | tf_op jit(solution)/shard_map/ppermute | solution.py:33
  18.7 8.7 %collective-permute-start.4 = (bf16[272,512]{1,0:T(8,128)(2,1)S(1)}, bf16[272,512]{1,0:T(8,128)(2,1)S(1)}, u32[]{:S(2)}, u32[]{:S(2)}) collective-permute-start(bf16[272,512]{1,0:T(8,128)(2,1)S(1)} %add_convert_fusion.mine), channel_id=1, source_target_pairs={{0,32},{1,2},{2,1},{3,4},{4,3},{5,6},{6,5},{7,8},{8,7},{9,10},{10,... | collective-permute-start | bytes 835592 | tf_op jit(solution)/shard_map/ppermute | solution.py:37
  18.9 8.5 %collective-permute-start.5 = (bf16[144,512]{1,0:T(8,128)(2,1)S(1)}, bf16[144,512]{1,0:T(8,128)(2,1)S(1)}, u32[]{:S(2)}, u32[]{:S(2)}) collective-permute-start(bf16[144,512]{1,0:T(8,128)(2,1)S(1)} %pad_maximum_fusion), channel_id=1, source_target_pairs={{0,32},{1,4},{2,34},{3,6},{4,1},{5,8},{6,3},{7,10},{8,5},{9,12},{1... | collective-permute-start | bytes 442376 | tf_op jit(solution)/shard_map/ppermute | solution.py:37
  27.5 4.0 %collective-permute-start.6 = (bf16[272,512]{1,0:T(8,128)(2,1)S(1)}, bf16[272,512]{1,0:T(8,128)(2,1)S(1)}, u32[]{:S(2)}, u32[]{:S(2)}) collective-permute-start(bf16[272,512]{1,0:T(8,128)(2,1)S(1)} %shard_map.132.passed), channel_id=1, source_target_pairs={{0,1},{1,0},{2,3},{3,2},{4,5},{5,4},{6,7},{7,6},{8,9},{9,8},{10,11... | collective-permute-start | bytes 835592 | tf_op jit(solution)/shard_map/ppermute | solution.py:33
  33.4 4.5 %collective-permute-start.7 = (bf16[128,512]{1,0:T(8,128)(2,1)S(1)}, bf16[128,512]{1,0:T(8,128)(2,1)S(1)}, u32[]{:S(2)}, u32[]{:S(2)}) collective-permute-start(bf16[128,512]{1,0:T(8,128)(2,1)S(1)} %shard_map.134.coarse), channel_id=1, source_target_pairs={{0,32},{1,2},{2,1},{3,4},{4,3},{5,6},{6,5},{7,8},{8,7},{9,10},{10,... | collective-permute-start | bytes 393224 | tf_op jit(solution)/shard_map/ppermute | solution.py:37
  37.9 3.5 %collective-permute-start.8 = (bf16[128,512]{1,0:T(8,128)(2,1)S(1)}, bf16[128,512]{1,0:T(8,128)(2,1)S(1)}, u32[]{:S(2)}, u32[]{:S(2)}) collective-permute-start(bf16[128,512]{1,0:T(8,128)(2,1)S(1)} %collective-permute-done.7.far), channel_id=1, source_target_pairs={{0,1},{1,0},{2,3},{3,2},{4,5},{5,4},{6,7},{7,6},{8,9},{9,8},{10,11... | collective-permute-start | bytes 393224 | tf_op jit(solution)/shard_map/ppermute | solution.py:33

commit v4 on v3

--- a/solution.py
+++ b/solution.py
@@ -68,10 +68,13 @@
     return centred * lax.rsqrt(variance + 1e-05)
 
 
-def node_update(rows, node_part, total, edge_second, node_other, node_second):
-    aggregate = dot(total.astype(BF16), edge_second).astype(BF16)
-    hidden = gated(node_part + 0.5 * dot(aggregate, node_other)).astype(BF16)
+def node_update(rows, node_part, total, through, node_second):
+    hidden = gated(node_part + dot(total.astype(BF16), through)).astype(BF16)
     return (rows.astype(F32) + layer_norm(dot(hidden, node_second))).astype(BF16)
+
+
+def product(edge_second, node_other):
+    return (0.5 * dot(edge_second, node_other)).astype(BF16)
 
 
 def pieces(source, target, arrived, count):
@@ -82,12 +85,12 @@
     ]
 
 
-def halo_body(features, send_rows, edge_first, held, edge_held, near, far, ids, ids_arrived, arrived, edge_arrived):
+def halo_body(features, send_rows, edge_first, held, edge_other, near, far, ids, ids_arrived, arrived, edge_arrived):
     core = lax.rem(lax.axis_index("dom"), 2)
     ids_copy = pltpu.make_async_copy(send_rows, ids, ids_arrived)
     ids_copy.start()
     copies = pieces(features, held, arrived, 4)
-    edge_copies = pieces(edge_first, edge_held, edge_arrived, 4)
+    edge_copies = pieces(edge_first.at[pl.ds(H, H), :], edge_other, edge_arrived, 2)
     for copy in copies + edge_copies:
         copy.start()
     ids_copy.wait()
@@ -104,15 +107,29 @@
         copy.wait()
 
 
-def local_body(features, neighbors, edge_first, node_first, projected, self_part, early, node_part, node_self, arrived):
-    copy = pltpu.make_async_copy(node_first.at[pl.ds(0, H), :], node_self, arrived)
-    copy.start()
-    projected[...] = (0.5 * dot(features[...], edge_first[H:, :])).astype(BF16)
-    self_part[...] = 0.5 * dot(features[...], edge_first[:H, :])
-    chosen = jnp.concatenate([columns(neighbors[0:1, s : s + 128], ROWS) for s in range(0, ROWS, 128)], axis=0)
-    early[...] = self_part[...] + dot(chosen, projected[...])
-    copy.wait()
-    node_part[...] = 0.5 * dot(features[...], node_self[...])
+def local_body(
+    features, neighbors, edge_other, edge_first, node_first, edge_second, node_second,
+    projected, self_part, early, node_part, through, last, ids, edge_self, node_held, second, arrived, first_arrived,
+):
+    ids_copy = pltpu.make_async_copy(neighbors, ids, first_arrived.at[0])
+    edge_copy = pltpu.make_async_copy(edge_first.at[pl.ds(0, H), :], edge_self, first_arrived.at[1])
+    copies = [
+        pltpu.make_async_copy(node_first, node_held, arrived.at[0]),
+        pltpu.make_async_copy(edge_second, second, arrived.at[1]),
+        pltpu.make_async_copy(node_second, last, arrived.at[2]),
+    ]
+    for copy in [ids_copy, edge_copy] + copies:
+        copy.start()
+    projected[...] = (0.5 * dot(features[...], edge_other[...])).astype(BF16)
+    ids_copy.wait()
+    chosen = jnp.concatenate([columns(ids[0:1, s : s + 128], ROWS) for s in range(0, ROWS, 128)], axis=0)
+    early[...] = dot(chosen, projected[...])
+    edge_copy.wait()
+    self_part[...] = 0.5 * dot(features[...], edge_self[...])
+    for copy in copies:
+        copy.wait()
+    node_part[...] = 0.5 * dot(features[...], node_held[:H, :])
+    through[...] = product(second[...], node_held[H:, :])
 
 
 def pool(chips, membership, updated):
@@ -140,25 +157,16 @@
 
 
 def fine_body(
-    features, local, self_part, early, node_part, near, far, neighbors, membership,
-    edge_first, edge_second, node_first, node_second,
-    updated, first,
-    projected, second, node_other, last, arrived,
+    features, local, self_part, early, node_part, near, far, neighbors, membership, edge_other, through, last,
+    updated, first, projected,
 ):
-    copies = [
-        pltpu.make_async_copy(edge_second, second, arrived.at[0]),
-        pltpu.make_async_copy(node_first.at[pl.ds(H, H), :], node_other, arrived.at[1]),
-        pltpu.make_async_copy(node_second, last, arrived.at[2]),
-    ]
-    for copy in copies:
-        copy.start()
     device = lax.axis_index("dom")
     core = lax.rem(device, 2)
     projected[0:ROWS, :] = local[...]
     below = jnp.where(core == 0, far[...], near[...])
     above = jnp.where(core == 0, near[...], far[...])
     halo = jnp.concatenate([below, above], axis=0)
-    projected[ROWS:, :] = (0.5 * dot(halo, edge_first[H:, :])).astype(BF16)
+    projected[ROWS:, :] = (0.5 * dot(halo, edge_other[...])).astype(BF16)
 
     for tile in range(ROWS // TILE):
         here = slice(tile * TILE, (tile + 1) * TILE)
@@ -166,18 +174,13 @@
         chosen = jnp.concatenate(
             [columns(neighbors[0:1, s : s + 128] - ROWS, 2 * HALO) for s in spans], axis=0
         )
-        total = gated(early[here, :] + dot(chosen, projected[ROWS:, :]))
+        total = gated(self_part[here, :] + early[here, :] + dot(chosen, projected[ROWS:, :]))
         for k in range(1, 4):
             chosen = jnp.concatenate(
                 [columns(neighbors[k : k + 1, s : s + 128], ROWS + 2 * HALO) for s in spans], axis=0
             )
             total = total + gated(self_part[here, :] + dot(chosen, projected[...]))
-        if tile == 0:
-            for copy in copies:
-                copy.wait()
-        updated[here, :] = node_update(
-            features[here, :], node_part[here, :], total, second[...], node_other[...], last[...]
-        )
+        updated[here, :] = node_update(features[here, :], node_part[here, :], total, through[...], last[...])
 
     _, chip, _, near_chip = place()
     first[: 2 * CHIP, :], counts = pool((near_chip, chip), membership, updated[...])
@@ -208,14 +211,14 @@
 
 def links_body(
     links, edge_first, edge_second, node_first, node_second,
-    own_rows, far_rows, near_rows, edge_first_held, edge_second_held, node_first_held, node_second_held, arrived,
+    own_rows, far_rows, near_rows, edge_first_held, node_first_held, node_second_held, through, second, arrived,
 ):
     copies = [
         pltpu.make_async_copy(source, target, arrived.at[i])
         for i, (source, target) in enumerate(
             (
                 (edge_first, edge_first_held),
-                (edge_second, edge_second_held),
+                (edge_second, second),
                 (node_first, node_first_held),
                 (node_second, node_second_held),
             )
@@ -229,6 +232,7 @@
             rows[k * CHIP : (k + 1) * CHIP, :] = columns(links[k : k + 1, :] - which * CHIP, CHIP)
     for copy in copies:
         copy.wait()
+    through[...] = product(second[...], node_first_held[H:, :])
 
 
 def far_body(passed, far_rows, edge_first, other):
@@ -237,7 +241,7 @@
 
 
 def coarse_body(
-    mine, passed, got, early, own_rows, near_rows, edge_first, edge_second, node_first, node_second, updated
+    mine, passed, got, early, own_rows, near_rows, edge_first, node_first, node_second, through, updated
 ):
     counts = slice(2 * CHIP, PACK)
     between = passed[CHIP : 2 * CHIP, :].astype(F32) + got[CHIP : 2 * CHIP, :].astype(F32)
@@ -253,7 +257,7 @@
     total = jnp.zeros((CHIP, H), F32)
     for k in range(8):
         total = total + gated(self_part + other[k * CHIP : (k + 1) * CHIP, :])
-    updated[...] = node_update(coarse, node_part, total, edge_second[...], node_first[H:, :], node_second[...])
+    updated[...] = node_update(coarse, node_part, total, through[...], node_second[...])
 
 
 def spread_body(fine, coarse, membership, partial, far_rows, near_rows):
@@ -309,12 +313,12 @@
 def halo_rows(*args):
     return call(
         halo_body,
-        [((ROWS, H), BF16), ((2 * H, H), BF16), ((HALO, H), BF16), ((HALO, H), BF16)],
+        [((ROWS, H), BF16), ((H, H), BF16), ((HALO, H), BF16), ((HALO, H), BF16)],
         [
             pltpu.VMEM((2, HALO), jnp.int32),
             pltpu.SemaphoreType.DMA(()),
             pltpu.SemaphoreType.DMA((4,)),
-            pltpu.SemaphoreType.DMA((4,)),
+            pltpu.SemaphoreType.DMA((2,)),
         ],
         300000000,
         args,
@@ -325,11 +329,17 @@
 def local_parts(*args):
     return call(
         local_body,
-        [((ROWS, H), BF16), ((ROWS, H), F32), ((ROWS, H), F32), ((ROWS, H), F32)],
-        [pltpu.VMEM((H, H), BF16), pltpu.SemaphoreType.DMA(())],
+        [((ROWS, H), BF16)] + [((ROWS, H), F32)] * 3 + [((H, H), BF16)] * 2 + [((4, ROWS), jnp.int32)],
+        [
+            pltpu.VMEM((H, H), BF16),
+            pltpu.VMEM((2 * H, H), BF16),
+            pltpu.VMEM((H, H), BF16),
+            pltpu.SemaphoreType.DMA((3,)),
+            pltpu.SemaphoreType.DMA((2,)),
+        ],
         2600000000,
         args,
-        (3,),
+        (1, 3, 4, 5, 6),
     )
 
 
@@ -337,16 +347,9 @@
     return call(
         fine_body,
         [((ROWS, H), BF16), ((PACK, H), BF16)],
-        [
-            pltpu.VMEM((ROWS + 2 * HALO, H), BF16),
-            pltpu.VMEM((H, H), BF16),
-            pltpu.VMEM((H, H), BF16),
-            pltpu.VMEM((H, H), BF16),
-            pltpu.SemaphoreType.DMA((3,)),
-        ],
+        [pltpu.VMEM((ROWS + 2 * HALO, H), BF16)],
         7000000000,
         args,
-        (10, 11, 12),
     )
 
 
@@ -361,8 +364,8 @@
 def link_rows(*args):
     return call(
         links_body,
-        [((8 * CHIP, CHIP), BF16)] * 3 + [((2 * H, H), BF16), ((H, H), BF16)] * 2,
-        [pltpu.SemaphoreType.DMA((4,))],
+        [((8 * CHIP, CHIP), BF16)] * 3 + [((2 * H, H), BF16)] * 2 + [((H, H), BF16)] * 2,
+        [pltpu.VMEM((H, H), BF16), pltpu.SemaphoreType.DMA((4,))],
         400000000,
         args,
         (1, 2, 3, 4),
@@ -412,13 +415,14 @@
     members = membership.reshape(ROWS // 128, 128)
     my_links = coarse_links.T
     their_links = sibling(my_links)
-    held, edge_held, near, far = halo_rows(features, send_rows, edge_first)
+    held, edge_other, near, far = halo_rows(features, send_rows, edge_first)
     near, far = sibling(near), across(far)
-    projected, self_part, early, node_part = local_parts(held, neighbors.T, edge_held, node_first)
+    projected, self_part, early, node_part, through, last, ids = local_parts(
+        held, neighbors.T, edge_other, edge_first, node_first, edge_second, node_second
+    )
     near, far, their_links = lax.optimization_barrier((near, far, their_links))
     updated, first = fine_stage(
-        held, projected, self_part, early, node_part, near, far, neighbors.T, members,
-        edge_held, edge_second, node_first, node_second,
+        held, projected, self_part, early, node_part, near, far, ids, members, edge_other, through, last
     )
     links = jnp.where(
         core == 0,

time: 43.1 us -> 42.5 us (0.986)
  waiting for transfers between devices: 11.1 us -> 10.5 us
    ppermute x4, waiting for transfers between devices: 8.48 us -> 7.77 us  [across(): lax.ppermute(value, ('grp', 'dom'), facing(lax.axis_size('grp'), step))]
  transfers between devices with their start and end apart: 9 -> 9, of which waited for: 5 -> 5; matrix products, arithmetic and copies ran while one was open for 0% -> 0% of each run, Pallas kernels for 15% -> 19%
where the time goes in v4:
time: 42.5 us; the launch traced here: 42.4 us
  Pallas kernels  19.4 us (46%)
  starting transfers between devices  12 us (28%)
  waiting for transfers between devices  10.5 us (25%)
    pallas_call x10, Pallas kernels, call(): pl.pallas_call(body, out_shape=[jax.ShapeDtypeStruct(shape, kind) for sha...  19.4 us
    ppermute x5, starting transfers between devices, sibling(): return lax.ppermute(value, 'dom', SIBLING)  8.41 us
    ppermute x4, waiting for transfers between devices, across(): lax.ppermute(value, ('grp', 'dom'), facing(lax.axis_size('grp'), step))  7.77 us
    ppermute x4, starting transfers between devices, across(): lax.ppermute(value, ('grp', 'dom'), facing(lax.axis_size('grp'), step))  3.6 us
    ppermute x5, waiting for transfers between devices, sibling(): return lax.ppermute(value, 'dom', SIBLING)  2.69 us
  transfers between devices with their start and end apart: 9, of which 5 were waited for; matrix products, arithmetic and copies ran while one was open for 0% of the time, Pallas kernels for 19%

profile of v4, /device:TPU:39, one launch (start us, length us, event | category | flops | bytes accessed | tf_op | source)
XLA Modules:
  0.0 42.4 jit_solution(6708458385311970520)
XLA Ops:
  0.0 0.0 copy-start.1
  0.0 1.8 %shard_map.127 = (bf16[1024,512]{1,0:T(8,128)(2,1)S(1)}, bf16[512,512]{1,0:T(8,128)(2,1)S(1)}, bf16[128,512]{1,0:T(8,128)(2,1)S(1)}, bf16[128,512]{1,0:T(8,128)(2,1)S(1)}) custom-call(bf16[1024,512]{1,0:T(8,128)(2,1)} %features.1, s32[2,128]{1,0:T(2,128)} %send_rows.1, bf16[1024,512]{1,0:T(8,128)(2,1)} %edge_first.4), custom_call_target="tpu_custom_call" | custom-call | flops 300000000 | bytes 4194304 | tf_op jit(solution)/shard_map/pallas_call | solution.py:302
  1.8 0.8 %collective-permute-start = (bf16[128,512]{1,0:T(8,128)(2,1)S(1)}, bf16[128,512]{1,0:T(8,128)(2,1)S(1)}, u32[]{:S(2)}, u32[]{:S(2)}) collective-permute-start(bf16[128,512]{1,0:T(8,128)(2,1)S(1)} %get-tuple-element.48), channel_id=1, source_target_pairs={{0,1},{1,0},{2,3},{3,2},{4,5},{5,4},{6,7},{7,6},{8,9},{9,8},{10,11... | collective-permute-start | bytes 393224 | tf_op jit(solution)/shard_map/ppermute | solution.py:33
  2.6 1.3 %collective-permute-start.1 = (bf16[128,512]{1,0:T(8,128)(2,1)S(1)}, bf16[128,512]{1,0:T(8,128)(2,1)S(1)}, u32[]{:S(2)}, u32[]{:S(2)}) collective-permute-start(bf16[128,512]{1,0:T(8,128)(2,1)S(1)} %get-tuple-element.49), channel_id=1, source_target_pairs={{0,32},{1,2},{2,1},{3,4},{4,3},{5,6},{6,5},{7,8},{8,7},{9,10},{10,... | collective-permute-start | bytes 393224 | tf_op jit(solution)/shard_map/ppermute | solution.py:37
  3.9 0.0 copy-done.1
  3.9 2.1 %collective-permute-start.2 = (s32[8,64]{1,0:T(8,128)S(1)}, s32[8,64]{1,0:T(8,128)S(1)}, u32[]{:S(2)}, u32[]{:S(2)}) collective-permute-start(s32[8,64]{1,0:T(8,128)S(1)} %bitcast.6), channel_id=1, source_target_pairs={{0,1},{1,0},{2,3},{3,2},{4,5},{5,4},{6,7},{7,6},{8,9},{9,8},{10,11... | collective-permute-start | bytes 6152 | tf_op jit(solution)/shard_map/ppermute | solution.py:33
  6.0 0.0 copy-start
  6.0 4.1 %shard_map.128 = (bf16[1024,512]{1,0:T(8,128)(2,1)S(1)}, f32[1024,512]{1,0:T(8,128)S(1)}, f32[1024,512]{1,0:T(8,128)S(1)}, f32[1024,512]{1,0:T(8,128)S(1)}, bf16...) custom-call(bf16[1024,512]{1,0:T(8,128)(2,1)S(1)} %get-tuple-element.42.features, ...), custom_call_target="tpu_custom_call" | custom-call | flops 2600000000 | bytes 4194304 | tf_op jit(solution)/shard_map/pallas_call | solution.py:302
  10.1 0.0 collective-permute-done.2
  10.1 0.0 collective-permute-done.near
  10.1 0.0 collective-permute-done.1.far
  10.1 0.0 copy-done
  10.1 6.7 %shard_map.129 = (bf16[1024,512]{1,0:T(8,128)(2,1)S(1)}, bf16[272,512]{1,0:T(8,128)(2,1)S(1)}) custom-call(bf16[1024,512]{1,0:T(8,128)(2,1)S(1)} %get-tuple-element.42.features, bf16[1024,512]{1,0:T(8,128)(2,1)S(1)} %get-tuple-element.44.local, f32[1024,512]{1,0:T(8,128)S(1)} %get-tuple-element.45.self_part, f32[1024,512]{1,0:T(8,128)S(1)} %get-tuple-element.46.early, ...), custom_call_target="tpu_custom_call" | custom-call | flops 7000000000 | bytes 4194304 | tf_op jit(solution)/shard_map/pallas_call | solution.py:302
  16.8 0.1 collective-permute-start.3
  16.9 0.4 shard_map.130
  17.3 1.1 %collective-permute-done.3 = bf16[272,512]{1,0:T(8,128)(2,1)S(1)} collective-permute-done((bf16[272,512]{1,0:T(8,128)(2,1)S(1)}, bf16[272,512]{1,0:T(8,128)(2,1)S(1)}, u32[]{:S(2)}, u32[]{:S(2)}) %collective-permute-start.3) | collective-permute-done | bytes 278560 | tf_op jit(solution)/shard_map/ppermute | solution.py:33
  18.4 0.1 add_convert_fusion.mine
  18.5 0.1 collective-permute-start.4
  18.7 1.6 %collective-permute-start.5 = (bf16[144,512]{1,0:T(8,128)(2,1)S(1)}, bf16[144,512]{1,0:T(8,128)(2,1)S(1)}, u32[]{:S(2)}, u32[]{:S(2)}) collective-permute-start(bf16[144,512]{1,0:T(8,128)(2,1)S(1)} %pad_maximum_fusion), channel_id=1, source_target_pairs={{0,32},{1,4},{2,34},{3,6},{4,1},{5,8},{6,3},{7,10},{8,5},{9,12},{1... | collective-permute-start | bytes 442376 | tf_op jit(solution)/shard_map/ppermute | solution.py:37
  20.3 0.1 add_select_fusion.links
  20.4 2.3 %shard_map.131 = (bf16[1024,128]{1,0:T(8,128)(2,1)S(1)}, bf16[1024,128]{1,0:T(8,128)(2,1)S(1)}, bf16[1024,128]{1,0:T(8,128)(2,1)S(1)}, bf16[1024,512]{1,0:T(8,12...) custom-call(s32[8,128]{1,0:T(8,128)S(1)} %add_select_fusion.links, ...), custom_call_target="tpu_custom_call" | custom-call | flops 400000000 | bytes 4194304 | tf_op jit(solution)/shard_map/pallas_call | solution.py:302
  22.7 4.4 %collective-permute-done.5.two = bf16[144,512]{1,0:T(8,128)(2,1)S(1)} collective-permute-done((bf16[144,512]{1,0:T(8,128)(2,1)S(1)}, bf16[144,512]{1,0:T(8,128)(2,1)S(1)}, u32[]{:S(2)}, u32[]{:S(2)}) %collective-permute-start.5) | collective-permute-done | bytes 147488 | tf_op jit(solution)/shard_map/ppermute | solution.py:37
  27.1 0.0 collective-permute-done.4.one
  27.1 0.1 shard_map.132.passed
  27.2 3.0 %collective-permute-start.6 = (bf16[272,512]{1,0:T(8,128)(2,1)S(1)}, bf16[272,512]{1,0:T(8,128)(2,1)S(1)}, u32[]{:S(2)}, u32[]{:S(2)}) collective-permute-start(bf16[272,512]{1,0:T(8,128)(2,1)S(1)} %shard_map.132.passed), channel_id=1, source_target_pairs={{0,1},{1,0},{2,3},{3,2},{4,5},{5,4},{6,7},{7,6},{8,9},{9,8},{10,11... | collective-permute-start | bytes 835592 | tf_op jit(solution)/shard_map/ppermute | solution.py:33
  30.2 0.6 %shard_map.133.early = f32[1024,512]{1,0:T(8,128)S(1)} custom-call(bf16[272,512]{1,0:T(8,128)(2,1)S(1)} %shard_map.132.passed, bf16[1024,128]{1,0:T(8,128)(2,1)S(1)} %get-tuple-element.67.far_rows, bf16[1024,512]{1,0:T(8,128)(2,1)S(1)} %get-tuple-element.68.edge_first), custom_call_target="tpu_custom_call" | custom-call | flops 200000000 | bytes 4194304 | tf_op jit(solution)/shard_map/pallas_call | solution.py:302
  30.8 0.6 %collective-permute-done.6.got = bf16[272,512]{1,0:T(8,128)(2,1)S(1)} collective-permute-done((bf16[272,512]{1,0:T(8,128)(2,1)S(1)}, bf16[272,512]{1,0:T(8,128)(2,1)S(1)}, u32[]{:S(2)}, u32[]{:S(2)}) %collective-permute-start.6) | collective-permute-done | bytes 278560 | tf_op jit(solution)/shard_map/ppermute | solution.py:33
  31.4 1.7 %shard_map.134.coarse = bf16[128,512]{1,0:T(8,128)(2,1)S(1)} custom-call(bf16[272,512]{1,0:T(8,128)(2,1)S(1)} %add_convert_fusion.mine, bf16[272,512]{1,0:T(8,128)(2,1)S(1)} %shard_map.132.passed, bf16[272,512]{1,0:T(8,128)(2,1)S(1)} %collective-permute-done.6.got, f32[1024,512]{1,0:T(8,128)S(1)} %shard_map.133.early, ...), custom_call_target="tpu_custom_call" | custom-call | flops 1000000000 | bytes 4194304 | tf_op jit(solution)/shard_map/pallas_call | solution.py:302
  33.1 0.6 %collective-permute-start.7 = (bf16[128,512]{1,0:T(8,128)(2,1)S(1)}, bf16[128,512]{1,0:T(8,128)(2,1)S(1)}, u32[]{:S(2)}, u32[]{:S(2)}) collective-permute-start(bf16[128,512]{1,0:T(8,128)(2,1)S(1)} %shard_map.134.coarse), channel_id=1, source_target_pairs={{0,32},{1,2},{2,1},{3,4},{4,3},{5,6},{6,5},{7,8},{8,7},{9,10},{10,... | collective-permute-start | bytes 393224 | tf_op jit(solution)/shard_map/ppermute | solution.py:37
  33.7 0.5 %shard_map.135 = (f32[1024,512]{1,0:T(8,128)S(1)}, bf16[1024,128]{1,0:T(8,128)(2,1)S(1)}, bf16[1024,128]{1,0:T(8,128)(2,1)S(1)}) custom-call(bf16[1024,512]{1,0:T(8,128)(2,1)S(1)} %get-tuple-element.55.updated.fine, bf16[128,512]{1,0:T(8,128)(2,1)S(1)} %shard_map.134.coarse, s32[8,128]{1,0:T(8,128)S(1)} %bitcast.5), custom_call_target="tpu_custom_call" | custom-call | flops 400000000 | bytes 4194304 | tf_op jit(solution)/shard_map/pallas_call | solution.py:302
  34.2 3.4 %collective-permute-done.7.far = bf16[128,512]{1,0:T(8,128)(2,1)S(1)} collective-permute-done((bf16[128,512]{1,0:T(8,128)(2,1)S(1)}, bf16[128,512]{1,0:T(8,128)(2,1)S(1)}, u32[]{:S(2)}, u32[]{:S(2)}) %collective-permute-start.7) | collective-permute-done | bytes 131104 | tf_op jit(solution)/shard_map/ppermute | solution.py:37
  37.5 2.5 %collective-permute-start.8 = (bf16[128,512]{1,0:T(8,128)(2,1)S(1)}, bf16[128,512]{1,0:T(8,128)(2,1)S(1)}, u32[]{:S(2)}, u32[]{:S(2)}) collective-permute-start(bf16[128,512]{1,0:T(8,128)(2,1)S(1)} %collective-permute-done.7.far), channel_id=1, source_target_pairs={{0,1},{1,0},{2,3},{3,2},{4,5},{5,4},{6,7},{7,6},{8,9},{9,8},{10,11... | collective-permute-start | bytes 393224 | tf_op jit(solution)/shard_map/ppermute | solution.py:33
  40.0 1.0 %collective-permute-done.8.near = bf16[128,512]{1,0:T(8,128)(2,1)S(1)} collective-permute-done((bf16[128,512]{1,0:T(8,128)(2,1)S(1)}, bf16[128,512]{1,0:T(8,128)(2,1)S(1)}, u32[]{:S(2)}, u32[]{:S(2)}) %collective-permute-start.8) | collective-permute-done | bytes 131104 | tf_op jit(solution)/shard_map/ppermute | solution.py:33
  41.0 1.2 %shard_map.136 = bf16[1024,512]{1,0:T(8,128)(2,1)} custom-call(f32[1024,512]{1,0:T(8,128)S(1)} %get-tuple-element.75.partial, bf16[1024,128]{1,0:T(8,128)(2,1)S(1)} %get-tuple-element.76.far_rows, bf16[1024,128]{1,0:T(8,128)(2,1)S(1)} %get-tuple-element.77.near_rows, bf16[128,512]{1,0:T(8,128)(2,1)S(1)} %collective-permute-done.7.far, ...), custom_call_target="tpu_custom_call" | custom-call | flops 400000000 | bytes 4194304 | tf_op jit(solution)/shard_map/pallas_call | solution.py:302
  (3 shorter events, 0.0 us)
Async XLA Ops:
  0.0 3.9 %copy-start.1 = (s32[64,8]{0,1:T(8,128)S(1)}, s32[64,8]{0,1:T(8,128)}, u32[]{:S(2)}) copy-start(s32[64,8]{0,1:T(8,128)} %param.17) | copy-start | bytes 6148
  1.8 8.3 %collective-permute-start = (bf16[128,512]{1,0:T(8,128)(2,1)S(1)}, bf16[128,512]{1,0:T(8,128)(2,1)S(1)}, u32[]{:S(2)}, u32[]{:S(2)}) collective-permute-start(bf16[128,512]{1,0:T(8,128)(2,1)S(1)} %get-tuple-element.48), channel_id=1, source_target_pairs={{0,1},{1,0},{2,3},{3,2},{4,5},{5,4},{6,7},{7,6},{8,9},{9,8},{10,11... | collective-permute-start | bytes 393224 | tf_op jit(solution)/shard_map/ppermute | solution.py:33
  2.6 7.5 %collective-permute-start.1 = (bf16[128,512]{1,0:T(8,128)(2,1)S(1)}, bf16[128,512]{1,0:T(8,128)(2,1)S(1)}, u32[]{:S(2)}, u32[]{:S(2)}) collective-permute-start(bf16[128,512]{1,0:T(8,128)(2,1)S(1)} %get-tuple-element.49), channel_id=1, source_target_pairs={{0,32},{1,2},{2,1},{3,4},{4,3},{5,6},{6,5},{7,8},{8,7},{9,10},{10,... | collective-permute-start | bytes 393224 | tf_op jit(solution)/shard_map/ppermute | solution.py:37
  3.9 6.2 %collective-permute-start.2 = (s32[8,64]{1,0:T(8,128)S(1)}, s32[8,64]{1,0:T(8,128)S(1)}, u32[]{:S(2)}, u32[]{:S(2)}) collective-permute-start(s32[8,64]{1,0:T(8,128)S(1)} %bitcast.6), channel_id=1, source_target_pairs={{0,1},{1,0},{2,3},{3,2},{4,5},{5,4},{6,7},{7,6},{8,9},{9,8},{10,11... | collective-permute-start | bytes 6152 | tf_op jit(solution)/shard_map/ppermute | solution.py:33
  6.0 4.1 %copy-start = (s32[1024]{0:T(1024)S(1)}, s32[1024]{0:T(1024)}, u32[]{:S(2)}) copy-start(s32[1024]{0:T(1024)} %param.16) | copy-start | bytes 12292
  16.8 1.6 %collective-permute-start.3 = (bf16[272,512]{1,0:T(8,128)(2,1)S(1)}, bf16[272,512]{1,0:T(8,128)(2,1)S(1)}, u32[]{:S(2)}, u32[]{:S(2)}) collective-permute-start(bf16[272,512]{1,0:T(8,128)(2,1)S(1)} %get-tuple-element.56.first), channel_id=1, source_target_pairs={{0,1},{1,0},{2,3},{3,2},{4,5},{5,4},{6,7},{7,6},{8,9},{9,8},{10,11... | collective-permute-start | bytes 835592 | tf_op jit(solution)/shard_map/ppermute | solution.py:33
  18.5 8.6 %collective-permute-start.4 = (bf16[272,512]{1,0:T(8,128)(2,1)S(1)}, bf16[272,512]{1,0:T(8,128)(2,1)S(1)}, u32[]{:S(2)}, u32[]{:S(2)}) collective-permute-start(bf16[272,512]{1,0:T(8,128)(2,1)S(1)} %add_convert_fusion.mine), channel_id=1, source_target_pairs={{0,32},{1,2},{2,1},{3,4},{4,3},{5,6},{6,5},{7,8},{8,7},{9,10},{10,... | collective-permute-start | bytes 835592 | tf_op jit(solution)/shard_map/ppermute | solution.py:37
  18.7 8.4 %collective-permute-start.5 = (bf16[144,512]{1,0:T(8,128)(2,1)S(1)}, bf16[144,512]{1,0:T(8,128)(2,1)S(1)}, u32[]{:S(2)}, u32[]{:S(2)}) collective-permute-start(bf16[144,512]{1,0:T(8,128)(2,1)S(1)} %pad_maximum_fusion), channel_id=1, source_target_pairs={{0,32},{1,4},{2,34},{3,6},{4,1},{5,8},{6,3},{7,10},{8,5},{9,12},{1... | collective-permute-start | bytes 442376 | tf_op jit(solution)/shard_map/ppermute | solution.py:37
  27.2 4.2 %collective-permute-start.6 = (bf16[272,512]{1,0:T(8,128)(2,1)S(1)}, bf16[272,512]{1,0:T(8,128)(2,1)S(1)}, u32[]{:S(2)}, u32[]{:S(2)}) collective-permute-start(bf16[272,512]{1,0:T(8,128)(2,1)S(1)} %shard_map.132.passed), channel_id=1, source_target_pairs={{0,1},{1,0},{2,3},{3,2},{4,5},{5,4},{6,7},{7,6},{8,9},{9,8},{10,11... | collective-permute-start | bytes 835592 | tf_op jit(solution)/shard_map/ppermute | solution.py:33
  33.1 4.5 %collective-permute-start.7 = (bf16[128,512]{1,0:T(8,128)(2,1)S(1)}, bf16[128,512]{1,0:T(8,128)(2,1)S(1)}, u32[]{:S(2)}, u32[]{:S(2)}) collective-permute-start(bf16[128,512]{1,0:T(8,128)(2,1)S(1)} %shard_map.134.coarse), channel_id=1, source_target_pairs={{0,32},{1,2},{2,1},{3,4},{4,3},{5,6},{6,5},{7,8},{8,7},{9,10},{10,... | collective-permute-start | bytes 393224 | tf_op jit(solution)/shard_map/ppermute | solution.py:37
  37.5 3.5 %collective-permute-start.8 = (bf16[128,512]{1,0:T(8,128)(2,1)S(1)}, bf16[128,512]{1,0:T(8,128)(2,1)S(1)}, u32[]{:S(2)}, u32[]{:S(2)}) collective-permute-start(bf16[128,512]{1,0:T(8,128)(2,1)S(1)} %collective-permute-done.7.far), channel_id=1, source_target_pairs={{0,1},{1,0},{2,3},{3,2},{4,5},{5,4},{6,7},{7,6},{8,9},{9,8},{10,11... | collective-permute-start | bytes 393224 | tf_op jit(solution)/shard_map/ppermute | solution.py:33

commit v5 on v4

--- a/solution.py
+++ b/solution.py
@@ -85,12 +85,16 @@
     ]
 
 
-def halo_body(features, send_rows, edge_first, held, edge_other, near, far, ids, ids_arrived, arrived, edge_arrived):
+def halo_body(
+    features, send_rows, edge_first, neighbors, held, edge_other, sources, near, far,
+    ids, ids_arrived, arrived, edge_arrived, sources_arrived,
+):
     core = lax.rem(lax.axis_index("dom"), 2)
     ids_copy = pltpu.make_async_copy(send_rows, ids, ids_arrived)
     ids_copy.start()
     copies = pieces(features, held, arrived, 4)
     edge_copies = pieces(edge_first.at[pl.ds(H, H), :], edge_other, edge_arrived, 2)
+    edge_copies.append(pltpu.make_async_copy(neighbors, sources, sources_arrived))
     for copy in copies + edge_copies:
         copy.start()
     ids_copy.wait()
@@ -108,21 +112,18 @@
 
 
 def local_body(
-    features, neighbors, edge_other, edge_first, node_first, edge_second, node_second,
-    projected, self_part, early, node_part, through, last, ids, edge_self, node_held, second, arrived, first_arrived,
-):
-    ids_copy = pltpu.make_async_copy(neighbors, ids, first_arrived.at[0])
-    edge_copy = pltpu.make_async_copy(edge_first.at[pl.ds(0, H), :], edge_self, first_arrived.at[1])
+    features, neighbors, edge_other, edge_first, node_first, edge_second,
+    projected, self_part, early, node_part, through, edge_self, node_held, second, arrived, first_arrived,
+):
+    edge_copy = pltpu.make_async_copy(edge_first.at[pl.ds(0, H), :], edge_self, first_arrived)
     copies = [
         pltpu.make_async_copy(node_first, node_held, arrived.at[0]),
         pltpu.make_async_copy(edge_second, second, arrived.at[1]),
-        pltpu.make_async_copy(node_second, last, arrived.at[2]),
     ]
-    for copy in [ids_copy, edge_copy] + copies:
+    for copy in [edge_copy] + copies:
         copy.start()
     projected[...] = (0.5 * dot(features[...], edge_other[...])).astype(BF16)
-    ids_copy.wait()
-    chosen = jnp.concatenate([columns(ids[0:1, s : s + 128], ROWS) for s in range(0, ROWS, 128)], axis=0)
+    chosen = jnp.concatenate([columns(neighbors[0:1, s : s + 128], ROWS) for s in range(0, ROWS, 128)], axis=0)
     early[...] = dot(chosen, projected[...])
     edge_copy.wait()
     self_part[...] = 0.5 * dot(features[...], edge_self[...])
@@ -157,7 +158,7 @@
 
 
 def fine_body(
-    features, local, self_part, early, node_part, near, far, neighbors, membership, edge_other, through, last,
+    features, local, self_part, early, node_part, near, far, neighbors, membership, edge_other, through, node_second,
     updated, first, projected,
 ):
     device = lax.axis_index("dom")
@@ -180,7 +181,7 @@
                 [columns(neighbors[k : k + 1, s : s + 128], ROWS + 2 * HALO) for s in spans], axis=0
             )
             total = total + gated(self_part[here, :] + dot(chosen, projected[...]))
-        updated[here, :] = node_update(features[here, :], node_part[here, :], total, through[...], last[...])
+        updated[here, :] = node_update(features[here, :], node_part[here, :], total, through[...], node_second[...])
 
     _, chip, _, near_chip = place()
     first[: 2 * CHIP, :], counts = pool((near_chip, chip), membership, updated[...])
@@ -277,13 +278,17 @@
         near_rows[here, :] = rows_of(chip + 1 - 2 * core)
 
 
-def unpool_body(partial, far_rows, near_rows, far, near, result, made, sent):
-    lookup = jnp.concatenate([far[...], near[...]], axis=0)
+def reach_body(partial, far_rows, far, grown):
+    for j in range(ROWS // 256):
+        here = slice(j * 256, (j + 1) * 256)
+        grown[here, :] = partial[here, :] + dot(far_rows[here, :], far[...])
+
+
+def unpool_body(partial, near_rows, near, result, made, sent):
     copies = []
     for j in range(ROWS // 256):
         here = slice(j * 256, (j + 1) * 256)
-        chosen = jnp.concatenate([far_rows[here, :], near_rows[here, :]], axis=1)
-        made[here, :] = (partial[here, :] + dot(chosen, lookup)).astype(BF16)
+        made[here, :] = (partial[here, :] + dot(near_rows[here, :], near[...])).astype(BF16)
         copy = pltpu.make_async_copy(
             made.at[pl.ds(j * 256, 256), :], result.at[pl.ds(j * 256, 256), :], sent.at[j]
         )
@@ -313,33 +318,34 @@
 def halo_rows(*args):
     return call(
         halo_body,
-        [((ROWS, H), BF16), ((H, H), BF16), ((HALO, H), BF16), ((HALO, H), BF16)],
+        [((ROWS, H), BF16), ((H, H), BF16), ((4, ROWS), jnp.int32), ((HALO, H), BF16), ((HALO, H), BF16)],
         [
             pltpu.VMEM((2, HALO), jnp.int32),
             pltpu.SemaphoreType.DMA(()),
             pltpu.SemaphoreType.DMA((4,)),
             pltpu.SemaphoreType.DMA((2,)),
+            pltpu.SemaphoreType.DMA(()),
         ],
         300000000,
         args,
-        (0, 1, 2),
+        (0, 1, 2, 3),
     )
 
 
 def local_parts(*args):
     return call(
         local_body,
-        [((ROWS, H), BF16)] + [((ROWS, H), F32)] * 3 + [((H, H), BF16)] * 2 + [((4, ROWS), jnp.int32)],
+        [((ROWS, H), BF16)] + [((ROWS, H), F32)] * 3 + [((H, H), BF16)],
         [
             pltpu.VMEM((H, H), BF16),
             pltpu.VMEM((2 * H, H), BF16),
             pltpu.VMEM((H, H), BF16),
-            pltpu.SemaphoreType.DMA((3,)),
             pltpu.SemaphoreType.DMA((2,)),
+            pltpu.SemaphoreType.DMA(()),
         ],
         2600000000,
         args,
-        (1, 3, 4, 5, 6),
+        (3, 4, 5),
     )
 
 
@@ -382,6 +388,10 @@
 
 def spread(*args):
     return call(spread_body, [((ROWS, H), F32), ((ROWS, CHIP), BF16), ((ROWS, CHIP), BF16)], [], 400000000, args)
+
+
+def reached(*args):
+    return call(reach_body, [((ROWS, H), F32)], [], 200000000, args)[0]
 
 
 def unpooled(*args):
@@ -415,14 +425,14 @@
     members = membership.reshape(ROWS // 128, 128)
     my_links = coarse_links.T
     their_links = sibling(my_links)
-    held, edge_other, near, far = halo_rows(features, send_rows, edge_first)
+    held, edge_other, sources, near, far = halo_rows(features, send_rows, edge_first, neighbors.T)
     near, far = sibling(near), across(far)
-    projected, self_part, early, node_part, through, last, ids = local_parts(
-        held, neighbors.T, edge_other, edge_first, node_first, edge_second, node_second
+    projected, self_part, early, node_part, through = local_parts(
+        held, sources, edge_other, edge_first, node_first, edge_second
     )
     near, far, their_links = lax.optimization_barrier((near, far, their_links))
     updated, first = fine_stage(
-        held, projected, self_part, early, node_part, near, far, ids, members, edge_other, through, last
+        held, projected, self_part, early, node_part, near, far, sources, members, edge_other, through, node_second
     )
     links = jnp.where(
         core == 0,
@@ -444,7 +454,7 @@
     partial, far_rows, near_rows = spread(updated, coarse_new, members)
     far, partial = lax.optimization_barrier((far, partial))
     near = sibling(far)
-    return unpooled(partial, far_rows, near_rows, far, near)
+    return unpooled(reached(partial, far_rows, far), near_rows, near)
 
 
 def solution(mesh):

time: 42.5 us -> 41.9 us (0.986)
  waiting for transfers between devices: 10.5 us -> 10 us
    ppermute x5, waiting for transfers between devices: 2.69 us -> 2.25 us  [sibling(): return lax.ppermute(value, 'dom', SIBLING)]
    pallas_call x10 -> x11, Pallas kernels: 19.4 us -> 19.2 us  [call(): pl.pallas_call(body, out_shape=[jax.ShapeDtypeStruct(shape, kind) for sha...]
where the time goes in v5:
time: 41.9 us; the launch traced here: 41.8 us
  Pallas kernels  19.2 us (46%)
  starting transfers between devices  12.1 us (29%)
  waiting for transfers between devices  10 us (24%)
    pallas_call x11, Pallas kernels, call(): pl.pallas_call(body, out_shape=[jax.ShapeDtypeStruct(shape, kind) for sha...  19.2 us
    ppermute x5, starting transfers between devices, sibling(): return lax.ppermute(value, 'dom', SIBLING)  8.43 us
    ppermute x4, waiting for transfers between devices, across(): lax.ppermute(value, ('grp', 'dom'), facing(lax.axis_size('grp'), step))  7.75 us
    ppermute x4, starting transfers between devices, across(): lax.ppermute(value, ('grp', 'dom'), facing(lax.axis_size('grp'), step))  3.62 us
    ppermute x5, waiting for transfers between devices, sibling(): return lax.ppermute(value, 'dom', SIBLING)  2.25 us
  transfers between devices with their start and end apart: 9, of which 5 were waited for; matrix products, arithmetic and copies ran while one was open for 0% of the time, Pallas kernels for 19%

profile of v5, /device:TPU:39, one launch (start us, length us, event | category | flops | bytes accessed | tf_op | source)
XLA Modules:
  0.0 41.8 jit_solution(7246908606683031921)
XLA Ops:
  0.0 0.0 copy-start.2
  0.0 1.8 %shard_map.127 = (bf16[1024,512]{1,0:T(8,128)(2,1)S(1)}, bf16[512,512]{1,0:T(8,128)(2,1)S(1)}, s32[4,1024]{1,0:T(4,128)S(1)}, bf16[128,512]{1,0:T(8,128)(2,1)S(1)}, bf16[128,512]{1,0:T(8,128)(2,1)S(1)}) custom-call(bf16[1024,512]{1,0:T(8,128)(2,1)} %features.1, s32[2,128]{1,0:T(2,128)} %send_rows.1, bf16[1024,512]{1,0:T(8,128)(2,1)} %edge_first.4, ...), custom_call_target="tpu_custom_call" | custom-call | flops 300000000 | bytes 4194304 | tf_op jit(solution)/shard_map/pallas_call | solution.py:307
  1.8 0.8 %collective-permute-start = (bf16[128,512]{1,0:T(8,128)(2,1)S(1)}, bf16[128,512]{1,0:T(8,128)(2,1)S(1)}, u32[]{:S(2)}, u32[]{:S(2)}) collective-permute-start(bf16[128,512]{1,0:T(8,128)(2,1)S(1)} %get-tuple-element.48), channel_id=1, source_target_pairs={{0,1},{1,0},{2,3},{3,2},{4,5},{5,4},{6,7},{7,6},{8,9},{9,8},{10,11... | collective-permute-start | bytes 393224 | tf_op jit(solution)/shard_map/ppermute | solution.py:33
  2.6 1.3 %collective-permute-start.1 = (bf16[128,512]{1,0:T(8,128)(2,1)S(1)}, bf16[128,512]{1,0:T(8,128)(2,1)S(1)}, u32[]{:S(2)}, u32[]{:S(2)}) collective-permute-start(bf16[128,512]{1,0:T(8,128)(2,1)S(1)} %get-tuple-element.49), channel_id=1, source_target_pairs={{0,32},{1,2},{2,1},{3,4},{4,3},{5,6},{6,5},{7,8},{8,7},{9,10},{10,... | collective-permute-start | bytes 393224 | tf_op jit(solution)/shard_map/ppermute | solution.py:37
  3.9 0.0 copy-done.2
  3.9 2.1 %collective-permute-start.2 = (s32[8,64]{1,0:T(8,128)S(1)}, s32[8,64]{1,0:T(8,128)S(1)}, u32[]{:S(2)}, u32[]{:S(2)}) collective-permute-start(s32[8,64]{1,0:T(8,128)S(1)} %bitcast.7), channel_id=1, source_target_pairs={{0,1},{1,0},{2,3},{3,2},{4,5},{5,4},{6,7},{7,6},{8,9},{9,8},{10,11... | collective-permute-start | bytes 6152 | tf_op jit(solution)/shard_map/ppermute | solution.py:33
  6.0 0.0 copy-start
  6.0 0.0 copy-start.1
  6.0 3.5 %shard_map.128 = (bf16[1024,512]{1,0:T(8,128)(2,1)S(1)}, f32[1024,512]{1,0:T(8,128)S(1)}, f32[1024,512]{1,0:T(8,128)S(1)}, f32[1024,512]{1,0:T(8,128)S(1)}, bf16[512,512]{1,0:T(8,128)(2,1)S(1)}) custom-call(bf16[1024,512]{1,0:T(8,128)(2,1)S(1)} %get-tuple-element.41.features, s32[4,1024]{1,0:T(4,128)S(1)} %get-tuple-element.42.neighbors, ...), custom_call_target="tpu_custom_call" | custom-call | flops 2600000000 | bytes 4194304 | tf_op jit(solution)/shard_map/pallas_call | solution.py:307
  9.5 0.0 collective-permute-done.2
  9.5 0.0 collective-permute-done.near
  9.5 0.0 collective-permute-done.1.far
  9.5 0.0 copy-done
  9.5 0.0 copy-done.1
  9.5 6.7 %shard_map.129 = (bf16[1024,512]{1,0:T(8,128)(2,1)S(1)}, bf16[272,512]{1,0:T(8,128)(2,1)S(1)}) custom-call(bf16[1024,512]{1,0:T(8,128)(2,1)S(1)} %get-tuple-element.41.features, bf16[1024,512]{1,0:T(8,128)(2,1)S(1)} %get-tuple-element.44.local, f32[1024,512]{1,0:T(8,128)S(1)} %get-tuple-element.45.self_part, f32[1024,512]{1,0:T(8,128)S(1)} %get-tuple-element.46.early, ...), custom_call_target="tpu_custom_call" | custom-call | flops 7000000000 | bytes 4194304 | tf_op jit(solution)/shard_map/pallas_call | solution.py:307
  16.2 0.1 collective-permute-start.3
  16.3 0.4 shard_map.130
  16.7 1.1 %collective-permute-done.3 = bf16[272,512]{1,0:T(8,128)(2,1)S(1)} collective-permute-done((bf16[272,512]{1,0:T(8,128)(2,1)S(1)}, bf16[272,512]{1,0:T(8,128)(2,1)S(1)}, u32[]{:S(2)}, u32[]{:S(2)}) %collective-permute-start.3) | collective-permute-done | bytes 278560 | tf_op jit(solution)/shard_map/ppermute | solution.py:33
  17.9 0.1 add_convert_fusion.mine
  17.9 0.1 collective-permute-start.4
  18.1 1.6 %collective-permute-start.5 = (bf16[144,512]{1,0:T(8,128)(2,1)S(1)}, bf16[144,512]{1,0:T(8,128)(2,1)S(1)}, u32[]{:S(2)}, u32[]{:S(2)}) collective-permute-start(bf16[144,512]{1,0:T(8,128)(2,1)S(1)} %pad_maximum_fusion), channel_id=1, source_target_pairs={{0,32},{1,4},{2,34},{3,6},{4,1},{5,8},{6,3},{7,10},{8,5},{9,12},{1... | collective-permute-start | bytes 442376 | tf_op jit(solution)/shard_map/ppermute | solution.py:37
  19.7 0.1 add_select_fusion.links
  19.8 2.3 %shard_map.131 = (bf16[1024,128]{1,0:T(8,128)(2,1)S(1)}, bf16[1024,128]{1,0:T(8,128)(2,1)S(1)}, bf16[1024,128]{1,0:T(8,128)(2,1)S(1)}, bf16[1024,512]{1,0:T(8,12...) custom-call(s32[8,128]{1,0:T(8,128)S(1)} %add_select_fusion.links, ...), custom_call_target="tpu_custom_call" | custom-call | flops 400000000 | bytes 4194304 | tf_op jit(solution)/shard_map/pallas_call | solution.py:307
  22.1 4.4 %collective-permute-done.5.two = bf16[144,512]{1,0:T(8,128)(2,1)S(1)} collective-permute-done((bf16[144,512]{1,0:T(8,128)(2,1)S(1)}, bf16[144,512]{1,0:T(8,128)(2,1)S(1)}, u32[]{:S(2)}, u32[]{:S(2)}) %collective-permute-start.5) | collective-permute-done | bytes 147488 | tf_op jit(solution)/shard_map/ppermute | solution.py:37
  26.5 0.0 collective-permute-done.4.one
  26.5 0.1 shard_map.132.passed
  26.7 3.0 %collective-permute-start.6 = (bf16[272,512]{1,0:T(8,128)(2,1)S(1)}, bf16[272,512]{1,0:T(8,128)(2,1)S(1)}, u32[]{:S(2)}, u32[]{:S(2)}) collective-permute-start(bf16[272,512]{1,0:T(8,128)(2,1)S(1)} %shard_map.132.passed), channel_id=1, source_target_pairs={{0,1},{1,0},{2,3},{3,2},{4,5},{5,4},{6,7},{7,6},{8,9},{9,8},{10,11... | collective-permute-start | bytes 835592 | tf_op jit(solution)/shard_map/ppermute | solution.py:33
  29.6 0.6 %shard_map.133.early = f32[1024,512]{1,0:T(8,128)S(1)} custom-call(bf16[272,512]{1,0:T(8,128)(2,1)S(1)} %shard_map.132.passed, bf16[1024,128]{1,0:T(8,128)(2,1)S(1)} %get-tuple-element.65.far_rows, bf16[1024,512]{1,0:T(8,128)(2,1)S(1)} %get-tuple-element.66.edge_first), custom_call_target="tpu_custom_call" | custom-call | flops 200000000 | bytes 4194304 | tf_op jit(solution)/shard_map/pallas_call | solution.py:307
  30.3 0.5 %collective-permute-done.6.got = bf16[272,512]{1,0:T(8,128)(2,1)S(1)} collective-permute-done((bf16[272,512]{1,0:T(8,128)(2,1)S(1)}, bf16[272,512]{1,0:T(8,128)(2,1)S(1)}, u32[]{:S(2)}, u32[]{:S(2)}) %collective-permute-start.6) | collective-permute-done | bytes 278560 | tf_op jit(solution)/shard_map/ppermute | solution.py:33
  30.8 1.7 %shard_map.134.coarse = bf16[128,512]{1,0:T(8,128)(2,1)S(1)} custom-call(bf16[272,512]{1,0:T(8,128)(2,1)S(1)} %add_convert_fusion.mine, bf16[272,512]{1,0:T(8,128)(2,1)S(1)} %shard_map.132.passed, bf16[272,512]{1,0:T(8,128)(2,1)S(1)} %collective-permute-done.6.got, f32[1024,512]{1,0:T(8,128)S(1)} %shard_map.133.early, ...), custom_call_target="tpu_custom_call" | custom-call | flops 1000000000 | bytes 4194304 | tf_op jit(solution)/shard_map/pallas_call | solution.py:307
  32.5 0.6 %collective-permute-start.7 = (bf16[128,512]{1,0:T(8,128)(2,1)S(1)}, bf16[128,512]{1,0:T(8,128)(2,1)S(1)}, u32[]{:S(2)}, u32[]{:S(2)}) collective-permute-start(bf16[128,512]{1,0:T(8,128)(2,1)S(1)} %shard_map.134.coarse), channel_id=1, source_target_pairs={{0,32},{1,2},{2,1},{3,4},{4,3},{5,6},{6,5},{7,8},{8,7},{9,10},{10,... | collective-permute-start | bytes 393224 | tf_op jit(solution)/shard_map/ppermute | solution.py:37
  33.1 0.5 %shard_map.135 = (f32[1024,512]{1,0:T(8,128)S(1)}, bf16[1024,128]{1,0:T(8,128)(2,1)S(1)}, bf16[1024,128]{1,0:T(8,128)(2,1)S(1)}) custom-call(bf16[1024,512]{1,0:T(8,128)(2,1)S(1)} %get-tuple-element.53.updated.fine, bf16[128,512]{1,0:T(8,128)(2,1)S(1)} %shard_map.134.coarse, s32[8,128]{1,0:T(8,128)S(1)} %bitcast.5), custom_call_target="tpu_custom_call" | custom-call | flops 400000000 | bytes 4194304 | tf_op jit(solution)/shard_map/pallas_call | solution.py:307
  33.6 3.4 %collective-permute-done.7.far = bf16[128,512]{1,0:T(8,128)(2,1)S(1)} collective-permute-done((bf16[128,512]{1,0:T(8,128)(2,1)S(1)}, bf16[128,512]{1,0:T(8,128)(2,1)S(1)}, u32[]{:S(2)}, u32[]{:S(2)}) %collective-permute-start.7) | collective-permute-done | bytes 131104 | tf_op jit(solution)/shard_map/ppermute | solution.py:37
  37.0 2.5 %collective-permute-start.8 = (bf16[128,512]{1,0:T(8,128)(2,1)S(1)}, bf16[128,512]{1,0:T(8,128)(2,1)S(1)}, u32[]{:S(2)}, u32[]{:S(2)}) collective-permute-start(bf16[128,512]{1,0:T(8,128)(2,1)S(1)} %collective-permute-done.7.far), channel_id=1, source_target_pairs={{0,1},{1,0},{2,3},{3,2},{4,5},{5,4},{6,7},{7,6},{8,9},{9,8},{10,11... | collective-permute-start | bytes 393224 | tf_op jit(solution)/shard_map/ppermute | solution.py:33
  39.4 0.4 %shard_map.136.partial = f32[1024,512]{1,0:T(8,128)S(1)} custom-call(f32[1024,512]{1,0:T(8,128)S(1)} %get-tuple-element.73.partial, bf16[1024,128]{1,0:T(8,128)(2,1)S(1)} %get-tuple-element.74.far_rows, bf16[128,512]{1,0:T(8,128)(2,1)S(1)} %collective-permute-done.7.far), custom_call_target="tpu_custom_call" | custom-call | flops 200000000 | bytes 4194304 | tf_op jit(solution)/shard_map/pallas_call | solution.py:307
  39.9 0.6 %collective-permute-done.8.near = bf16[128,512]{1,0:T(8,128)(2,1)S(1)} collective-permute-done((bf16[128,512]{1,0:T(8,128)(2,1)S(1)}, bf16[128,512]{1,0:T(8,128)(2,1)S(1)}, u32[]{:S(2)}, u32[]{:S(2)}) %collective-permute-start.8) | collective-permute-done | bytes 131104 | tf_op jit(solution)/shard_map/ppermute | solution.py:33
  40.4 1.2 %shard_map.137 = bf16[1024,512]{1,0:T(8,128)(2,1)} custom-call(f32[1024,512]{1,0:T(8,128)S(1)} %shard_map.136.partial, bf16[1024,128]{1,0:T(8,128)(2,1)S(1)} %get-tuple-element.76.near_rows, bf16[128,512]{1,0:T(8,128)(2,1)S(1)} %collective-permute-done.8.near), custom_call_target="tpu_custom_call" | custom-call | flops 400000000 | bytes 4194304 | tf_op jit(solution)/shard_map/pallas_call | solution.py:307
  (3 shorter events, 0.0 us)
Async XLA Ops:
  0.0 3.9 %copy-start.2 = (s32[64,8]{0,1:T(8,128)S(1)}, s32[64,8]{0,1:T(8,128)}, u32[]{:S(2)}) copy-start(s32[64,8]{0,1:T(8,128)} %param.17) | copy-start | bytes 6148
  1.8 7.7 %collective-permute-start = (bf16[128,512]{1,0:T(8,128)(2,1)S(1)}, bf16[128,512]{1,0:T(8,128)(2,1)S(1)}, u32[]{:S(2)}, u32[]{:S(2)}) collective-permute-start(bf16[128,512]{1,0:T(8,128)(2,1)S(1)} %get-tuple-element.48), channel_id=1, source_target_pairs={{0,1},{1,0},{2,3},{3,2},{4,5},{5,4},{6,7},{7,6},{8,9},{9,8},{10,11... | collective-permute-start | bytes 393224 | tf_op jit(solution)/shard_map/ppermute | solution.py:33
  2.6 6.9 %collective-permute-start.1 = (bf16[128,512]{1,0:T(8,128)(2,1)S(1)}, bf16[128,512]{1,0:T(8,128)(2,1)S(1)}, u32[]{:S(2)}, u32[]{:S(2)}) collective-permute-start(bf16[128,512]{1,0:T(8,128)(2,1)S(1)} %get-tuple-element.49), channel_id=1, source_target_pairs={{0,32},{1,2},{2,1},{3,4},{4,3},{5,6},{6,5},{7,8},{8,7},{9,10},{10,... | collective-permute-start | bytes 393224 | tf_op jit(solution)/shard_map/ppermute | solution.py:37
  3.9 5.6 %collective-permute-start.2 = (s32[8,64]{1,0:T(8,128)S(1)}, s32[8,64]{1,0:T(8,128)S(1)}, u32[]{:S(2)}, u32[]{:S(2)}) collective-permute-start(s32[8,64]{1,0:T(8,128)S(1)} %bitcast.7), channel_id=1, source_target_pairs={{0,1},{1,0},{2,3},{3,2},{4,5},{5,4},{6,7},{7,6},{8,9},{9,8},{10,11... | collective-permute-start | bytes 6152 | tf_op jit(solution)/shard_map/ppermute | solution.py:33
  6.0 3.5 %copy-start = (s32[1024]{0:T(1024)S(1)}, s32[1024]{0:T(1024)}, u32[]{:S(2)}) copy-start(s32[1024]{0:T(1024)} %param.16) | copy-start | bytes 12292
  6.0 3.6 %copy-start.1 = (bf16[512,512]{1,0:T(8,128)(2,1)S(1)}, bf16[512,512]{1,0:T(8,128)(2,1)}, u32[]{:S(2)}) copy-start(bf16[512,512]{1,0:T(8,128)(2,1)} %node_second.2) | copy-start | bytes 1572868
  16.2 1.6 %collective-permute-start.3 = (bf16[272,512]{1,0:T(8,128)(2,1)S(1)}, bf16[272,512]{1,0:T(8,128)(2,1)S(1)}, u32[]{:S(2)}, u32[]{:S(2)}) collective-permute-start(bf16[272,512]{1,0:T(8,128)(2,1)S(1)} %get-tuple-element.54.first), channel_id=1, source_target_pairs={{0,1},{1,0},{2,3},{3,2},{4,5},{5,4},{6,7},{7,6},{8,9},{9,8},{10,11... | collective-permute-start | bytes 835592 | tf_op jit(solution)/shard_map/ppermute | solution.py:33
  17.9 8.6 %collective-permute-start.4 = (bf16[272,512]{1,0:T(8,128)(2,1)S(1)}, bf16[272,512]{1,0:T(8,128)(2,1)S(1)}, u32[]{:S(2)}, u32[]{:S(2)}) collective-permute-start(bf16[272,512]{1,0:T(8,128)(2,1)S(1)} %add_convert_fusion.mine), channel_id=1, source_target_pairs={{0,32},{1,2},{2,1},{3,4},{4,3},{5,6},{6,5},{7,8},{8,7},{9,10},{10,... | collective-permute-start | bytes 835592 | tf_op jit(solution)/shard_map/ppermute | solution.py:37
  18.1 8.4 %collective-permute-start.5 = (bf16[144,512]{1,0:T(8,128)(2,1)S(1)}, bf16[144,512]{1,0:T(8,128)(2,1)S(1)}, u32[]{:S(2)}, u32[]{:S(2)}) collective-permute-start(bf16[144,512]{1,0:T(8,128)(2,1)S(1)} %pad_maximum_fusion), channel_id=1, source_target_pairs={{0,32},{1,4},{2,34},{3,6},{4,1},{5,8},{6,3},{7,10},{8,5},{9,12},{1... | collective-permute-start | bytes 442376 | tf_op jit(solution)/shard_map/ppermute | solution.py:37
  26.7 4.2 %collective-permute-start.6 = (bf16[272,512]{1,0:T(8,128)(2,1)S(1)}, bf16[272,512]{1,0:T(8,128)(2,1)S(1)}, u32[]{:S(2)}, u32[]{:S(2)}) collective-permute-start(bf16[272,512]{1,0:T(8,128)(2,1)S(1)} %shard_map.132.passed), channel_id=1, source_target_pairs={{0,1},{1,0},{2,3},{3,2},{4,5},{5,4},{6,7},{7,6},{8,9},{9,8},{10,11... | collective-permute-start | bytes 835592 | tf_op jit(solution)/shard_map/ppermute | solution.py:33
  32.5 4.5 %collective-permute-start.7 = (bf16[128,512]{1,0:T(8,128)(2,1)S(1)}, bf16[128,512]{1,0:T(8,128)(2,1)S(1)}, u32[]{:S(2)}, u32[]{:S(2)}) collective-permute-start(bf16[128,512]{1,0:T(8,128)(2,1)S(1)} %shard_map.134.coarse), channel_id=1, source_target_pairs={{0,32},{1,2},{2,1},{3,4},{4,3},{5,6},{6,5},{7,8},{8,7},{9,10},{10,... | collective-permute-start | bytes 393224 | tf_op jit(solution)/shard_map/ppermute | solution.py:37
  37.0 3.5 %collective-permute-start.8 = (bf16[128,512]{1,0:T(8,128)(2,1)S(1)}, bf16[128,512]{1,0:T(8,128)(2,1)S(1)}, u32[]{:S(2)}, u32[]{:S(2)}) collective-permute-start(bf16[128,512]{1,0:T(8,128)(2,1)S(1)} %collective-permute-done.7.far), channel_id=1, source_target_pairs={{0,1},{1,0},{2,3},{3,2},{4,5},{5,4},{6,7},{7,6},{8,9},{9,8},{10,11... | collective-permute-start | bytes 393224 | tf_op jit(solution)/shard_map/ppermute | solution.py:33
